TPU v7x, 128 devices: a whole 4x4x4 slice. The times are simulated.
128 devices in a mesh: row: 16 (over z_lo, y, core), col: 8 (over z_hi, x).
Axes of the slice: x: 4, y: 4, z: 4 (z_hi: 2, z_lo: 2; z = z_hi * 2 + z_lo), core: 2. Of those that a mesh axis runs over, the one named last changes fastest.
Arguments:
- iterate: bfloat16 [6144, 9216], P('row', 'col'), may hold values from -2.1875 to 2.1875
Outputs:
- update: bfloat16 [6144, 9216], P('row', 'col')
All inputs are finite; a program needn't handle non-finite values.
Results may differ from a plain program's by a relative error of at most 0.0052.
Values may be sent and summed in bfloat16 or wider, within the bound.
No kernel may reach another device: no remote copies, remote signals or barrier semaphores. Data moves between devices by JAX's collectives and lax.ppermute only.
A program may use at most 128 MiB of HBM per device.

v0:
```python
import jax
import jax.numpy as jnp
from jax import lax
from jax.sharding import PartitionSpec as P

N = 9216


lead_coef = 3.4445
square_coef = -4.775
quart_coef = 2.0315


def local(iterate):
    panel = lax.all_gather(iterate, "row", axis=0, tiled=True)
    terms = jnp.einsum("ik,jk->ij", panel, iterate, preferred_element_type=jnp.float32)
    summed = lax.psum_scatter(terms, "col", scatter_dimension=0, tiled=True)
    gram_block = (summed / N).astype(jnp.bfloat16)
    gram_cols = lax.all_gather(gram_block, "col", axis=0, tiled=True)
    rows = gram_cols
    square = jnp.dot(
        lax.all_gather(gram_block, "row", axis=1, tiled=True),
        rows,
        preferred_element_type=jnp.float32,
    )
    poly = (square_coef * gram_block.astype(jnp.float32) + quart_coef * square).astype(jnp.bfloat16)
    rows = panel
    mixed = jnp.einsum(
        "ki,kj->ij",
        lax.all_gather(poly, "col", axis=0, tiled=True),
        rows,
        preferred_element_type=jnp.float32,
    )
    return (lead_coef * iterate.astype(jnp.float32) + mixed).astype(jnp.bfloat16)


def solution(mesh):
    in_specs = (P("row", "col"),)
    out_specs = P("row", "col")
    return jax.shard_map(local, mesh=mesh, in_specs=in_specs, out_specs=out_specs, check_vma=False)
```

profile of v0, /device:TPU:1, one launch (start us, length us, event | category | flops | bytes accessed | tf_op | source)
XLA Modules:
  0.0 469.3 jit_solution(9990958525066368659)
XLA Ops:
  6.5 0.0 all-gather.5.cloned.1.call-start
  6.5 0.7 all-gather.5.cloned.1.call-update
  7.3 0.0 reduce-scatter.2.cloned.1.call-start
  7.3 84.7 %all-gather.5.cloned.1.call-done = bf16[6144,1152]{1,0:T(8,128)(2,1)} async-done(((bf16[384,1152]{1,0:T(8,128)(2,1)}), bf16[6144,1152]{1,0:T(8,128)(2,1)}) %all-gather.5.cloned.1.call-update) | async-done | bytes 14155792 | tf_op jit(solution)/shard_map/all_gather | solution.py:15
  92.0 13.5 %fusion.3 = f32[6144,384]{1,0:T(8,128)} fusion(bf16[6144,1152]{1,0:T(8,128)(2,1)} %all-gather.5.cloned.1.call-done, bf16[384,1152]{1,0:T(8,128)(2,1)} %param.1), kind=kOutput, calls=%fused_computation.6 | convolution fusion | flops 5435817984 | bytes 24477696 | tf_op jit(solution)/shard_map/ik,jk->ij/dot_general | solution.py:16
  105.6 0.0 reduce-scatter.2.cloned.1.call-update
  105.6 0.0 all-gather.9.cloned.1.call-start
  105.6 126.3 %reduce-scatter.2.cloned.1.call-done = f32[768,384]{1,0:T(8,128)} async-done(((f32[6144,384]{1,0:T(8,128)}), f32[768,384]{1,0:T(8,128)}) %reduce-scatter.2.cloned.1.call-update) | async-done | bytes 1179664 | tf_op jit(solution)/shard_map/reduce_scatter | solution.py:17
  232.0 2.2 multiply_convert_fusion
  234.2 0.0 all-gather.9.cloned.1.call-update
  234.2 0.0 all-gather.7.cloned.1.call-start
  234.2 0.5 all-gather.7.cloned.1.call-update
  234.8 0.0 copy-start
  234.8 0.0 all-gather.11.cloned.1.call-start
  234.8 73.4 %all-gather.9.cloned.1.call-done = bf16[6144,384]{1,0:T(8,128)(2,1)} async-done(((bf16[768,384]{1,0:T(8,128)(2,1)}), bf16[6144,384]{1,0:T(8,128)(2,1)}) %all-gather.9.cloned.1.call-update) | async-done | bytes 4718608 | tf_op jit(solution)/shard_map/all_gather | solution.py:19
  308.2 57.2 %all-gather.7.cloned.1.call-done = bf16[768,6144]{1,0:T(8,128)(2,1)} async-done(((bf16[768,384]{1,0:T(8,128)(2,1)}), bf16[768,6144]{1,0:T(8,128)(2,1)}) %all-gather.7.cloned.1.call-update) | async-done | bytes 9437200 | tf_op jit(solution)/shard_map/all_gather | solution.py:22
  365.5 9.8 %fusion.2 = bf16[768,384]{1,0:T(8,128)(2,1)} fusion(bf16[768,6144]{1,0:T(8,128)(2,1)} %all-gather.7.cloned.1.call-done, bf16[6144,384]{1,0:T(8,128)(2,1)} %all-gather.9.cloned.1.call-done, bf16[768,384]{1,0:T(8,128)(2,1)} %multiply_convert_fusion), kind=kOutput, calls=%fused_computation.4 | convolution fusion | flops 3625353216 | bytes 15335424 | tf_op jit(solution)/shard_map/dot_general | solution.py:21
  375.3 0.0 all-gather.11.cloned.1.call-update
  375.3 76.1 %all-gather.11.cloned.1.call-done = bf16[6144,384]{1,0:T(8,128)(2,1)} async-done(((bf16[768,384]{1,0:T(8,128)(2,1)}), bf16[6144,384]{1,0:T(8,128)(2,1)}) %all-gather.11.cloned.1.call-update) | async-done | bytes 4718608 | tf_op jit(solution)/shard_map/all_gather | solution.py:30
  451.4 0.0 copy-done
  451.4 11.4 %fusion = bf16[384,1152]{1,0:T(8,128)(2,1)} fusion(bf16[6144,384]{1,0:T(8,128)(2,1)} %all-gather.11.cloned.1.call-done, bf16[6144,1152]{1,0:T(8,128)(2,1)} %all-gather.5.cloned.1.call-done, bf16[384,1152]{1,0:T(8,128)(2,1)S(1)} %copy-done), kind=kOutput, calls=%fused_computation.1 | convolution fusion | flops 5437587456 | bytes 20643840 | tf_op jit(solution)/shard_map/ki,kj->ij/dot_general | solution.py:28
Async XLA Ops:
  6.5 85.5 %all-gather.5.cloned.1.call-start = ((), (), s32[]{:S(2)}) async-start(), calls=%async_computation.1 | async-start | bytes 15040512 | tf_op jit(solution)/shard_map/all_gather | solution.py:15
  7.3 224.7 %reduce-scatter.2.cloned.1.call-start = ((), (), s32[]{:S(2)}) async-start(), calls=%async_computation.2 | async-start | bytes 10616832 | tf_op jit(solution)/shard_map/reduce_scatter | solution.py:17
  105.6 202.6 %all-gather.9.cloned.1.call-start = ((), (), s32[]{:S(2)}) async-start(), calls=%async_computation.4 | async-start | bytes 5308416 | tf_op jit(solution)/shard_map/all_gather | solution.py:19
  234.2 131.3 %all-gather.7.cloned.1.call-start = ((), (), s32[]{:S(2)}) async-start(), calls=%async_computation.3 | async-start | bytes 10027008 | tf_op jit(solution)/shard_map/all_gather | solution.py:22
  234.8 216.6 %copy-start = (bf16[384,1152]{1,0:T(8,128)(2,1)S(1)}, bf16[384,1152]{1,0:T(8,128)(2,1)}, u32[]{:S(2)}) copy-start(bf16[384,1152]{1,0:T(8,128)(2,1)} %param.1) | copy-start | bytes 2654212
  234.8 216.6 %all-gather.11.cloned.1.call-start = ((), (), s32[]{:S(2)}) async-start(), calls=%async_computation.5 | async-start | bytes 5308416 | tf_op jit(solution)/shard_map/all_gather | solution.py:30
Sparse Core Ops, SparseCore 0:
  9.1 82.9 all-gather.4
  105.7 126.2 reduce-scatter.1
  234.6 73.6 all-gather.8
  309.8 55.5 all-gather.6
  375.4 75.9 all-gather.10
where the time goes:
time: 469 us
  waiting for transfers between devices  419 us (89%)
  matrix products  34.7 us (7%)
  between operations  13.1 us (3%)
    reduce_scatter x1, waiting for transfers between devices, local(): summed = lax.psum_scatter(terms, 'col', scatter_dimension=0, tiled=True)  126 us
    all_gather x1, waiting for transfers between devices, local(): panel = lax.all_gather(iterate, 'row', axis=0, tiled=True)  84.7 us
    all_gather x1, waiting for transfers between devices, local(): lax.all_gather(poly, 'col', axis=0, tiled=True)  76.1 us
    all_gather x1, waiting for transfers between devices, local(): gram_cols = lax.all_gather(gram_block, 'col', axis=0, tiled=True)  73.4 us
    all_gather x1, waiting for transfers between devices, local(): lax.all_gather(gram_block, 'row', axis=1, tiled=True)  57.2 us
    dot_general x1, matrix products, local(): jnp.einsum('ik,jk->ij', panel, iterate, preferred_element_type=jnp.float32)  13.5 us
    dot_general x1, matrix products, local(): jnp.einsum('ki,kj->ij', lax.all_gather(poly, 'col', axis=0, tiled=True),...  11.4 us
    dot_general x1, matrix products, local(): jnp.dot(lax.all_gather(gram_block, 'row', axis=1, tiled=True), rows, pref...  9.79 us
  transfers between devices with their start and end apart: 5, of which 5 were waited for; matrix products, arithmetic and copies ran while one was open for 0% of the time, Pallas kernels for 0%

commit v1 on v0

v1 whole, which is shorter than its diff:
```python
import jax
import jax.numpy as jnp
from jax import lax
from jax.experimental import pallas as pl
from jax.experimental.pallas import tpu as pltpu
from jax.sharding import Mesh, PartitionSpec as P

N = 9216

lead_coef = 3.4445
square_coef = -4.775
quart_coef = 2.0315

AXES = ("zl", "y", "c", "zh", "x")
SIZES = (2, 4, 2, 2, 4)
ROW = ("zl", "y", "c")
COL = ("zh", "x")
f32 = jnp.float32
bf16 = jnp.bfloat16
VMEM_LIMIT = 36 * 2**20

def swap_zl(v):
    return lax.ppermute(v, "zl", [(0, 1), (1, 0)])


def swap_zh(v):
    return lax.ppermute(v, "zh", [(0, 1), (1, 0)])


def swap_core(v):
    return lax.ppermute(v, "c", [(0, 1), (1, 0)])


def swap_x1(v):
    return lax.ppermute(v, "x", [(i, i ^ 1) for i in range(4)])


def swap_x3(v):
    return lax.ppermute(v, "x", [(i, i ^ 3) for i in range(4)])


def partner(v, first):
    pairs = []
    for c in range(2):
        by = 1 if (c == 0) == first else 3
        pairs += [(c * 4 + x, c * 4 + (x ^ by)) for x in range(4)]
    return lax.ppermute(v, ("c", "x"), pairs)


def along_y(v, first=True):
    pairs = []
    for y in range(4):
        for c in range(2):
            by = 1 if (c == 0) == first else -1
            pairs.append((y * 2 + c, (y + by) % 4 * 2 + c))
    return lax.ppermute(v, ("y", "c"), pairs)


def together(*values):
    return lax.optimization_barrier(values)


ARRIVAL = ((0, "v"), (0, "r0"), (1, "v"), (0, "r1"), (0, "f"), (1, "r0"), (1, "r1"), (1, "f"))
BATCHES = 3


VM = pl.BlockSpec(memory_space=pltpu.VMEM)
SM = pl.BlockSpec(memory_space=pltpu.SMEM)
HBM = pl.BlockSpec(memory_space=pltpu.HBM)


def call(kernel, out_shape, in_specs, scratch, *args):
    outs = jax.tree.map(lambda _: VM, out_shape)
    return pl.pallas_call(
        kernel,
        out_shape=out_shape,
        in_specs=in_specs,
        out_specs=outs,
        scratch_shapes=scratch,
        cost_estimate=pl.CostEstimate(flops=0, bytes_accessed=0, transcendentals=0),
        compiler_params=pltpu.CompilerParams(vmem_limit_bytes=VMEM_LIMIT),
    )(*args)


def place_of(where_ref, d, h):
    return jnp.bitwise_xor(where_ref[0], d) * 2 + jnp.bitwise_xor(where_ref[1], h)


def start_copies(copies, refs, panel, sems):
    started = []
    for i, (ref, src, dst, rows) in enumerate(copies):
        copy = pltpu.make_async_copy(refs[ref].at[pl.ds(src, rows)], panel.at[pl.ds(dst, rows)], sems.at[i])
        copy.start()
        started.append(copy)
    return started


def terms_of(where, own, sibling, arrays, copies, send):
    rows, depth = own.shape
    t = rows // 3

    def kernel(where_ref, own_ref, sib_ref, *refs):
        refs, out, panel, sems = refs[:-3], refs[-3], refs[-2], refs[-1]
        for copy in start_copies(copies, refs, panel, sems):
            copy.wait()
        for slot, d in enumerate((where_ref[2], 2) if send else (0, where_ref[3])):
            x = jnp.bitwise_xor(where_ref[0], d)
            pair = panel[pl.ds(pl.multiple_of(x * 2 * t, 2 * t), 2 * t)]
            for i, left in enumerate((own_ref, sib_ref)):
                value = lax.dot_general(
                    left[...], pair, (((1,), (1,)), ((), ())), preferred_element_type=f32
                ).astype(out.dtype)
                for z in range(2):
                    h = jnp.bitwise_xor(where_ref[1], z)
                    out[slot, h, i * rows : (i + 1) * rows] = value[:, z * t : (z + 1) * t]

    return call(
        kernel, jax.ShapeDtypeStruct((2, 2, 2 * rows, t), bf16 if send else f32),
        [SM, VM, VM] + [HBM] * len(arrays),
        [pltpu.VMEM((8 * t, depth), bf16), pltpu.SemaphoreType.DMA((len(copies),))],
        where, own, sibling, *arrays,
    )


def sum_pair(keep, got):
    shape = keep.shape[1:]

    def kernel(k, g, mine, other):
        other[...] = (k[1] + g[1].astype(f32)).astype(bf16)
        mine[...] = k[0] + g[0].astype(f32)

    return call(kernel, [jax.ShapeDtypeStruct(shape, f32), jax.ShapeDtypeStruct(shape, bf16)], [VM] * 2, [], keep, got)


def sum_other(mine, got):
    def kernel(m, g, out):
        out[...] = (m[1] + g[1].astype(f32)).astype(bf16)

    return call(kernel, jax.ShapeDtypeStruct(mine.shape[1:], bf16), [VM] * 2, [], mine, got)


def finish(sums):
    rows, t = sums[0][2].shape
    flat = [a for three in sums for a in three]

    def kernel(*refs):
        out = refs[-1]
        for b in range(len(sums)):
            mine, x_part, z_part = refs[3 * b : 3 * b + 3]
            value = (mine[0] + x_part[0].astype(f32) + z_part[...].astype(f32)) / N
            out[:, b * t : (b + 1) * t] = value.astype(bf16)

    return call(kernel, jax.ShapeDtypeStruct((rows, len(sums) * t), bf16), [VM] * len(flat), [], *flat)


def times_x(where, full, arrays, copies, total, half, dtype):
    spots = list(full)
    both, depth = full[spots[0]].shape
    cols = arrays[0].shape[1]
    count = len(spots)
    extra = [] if total is None else [total]
    part = slice(0, both) if half is None else slice(half * both // 2, (half + 1) * both // 2)
    rows = part.stop - part.start
    lists = [[spec for spec in copies if spec[2] // depth == e] for e in range(8)]

    def kernel(where_ref, *refs):
        slices, pieces, refs = refs[:count], refs[count : count + len(arrays)], refs[count + len(arrays) :]
        out, held, sems = refs[-3:]

        def copy_of(i, j, spec):
            ref, src, dst, size = spec
            target = held.at[pl.ds(i * depth + dst % depth, size)]
            return pltpu.make_async_copy(pieces[ref].at[pl.ds(src, size)], target, sems.at[i, j])

        for i, spot in enumerate(spots):
            place = place_of(where_ref, *spot)
            for e in range(8):
                @pl.when(place == e)
                def _(i=i, e=e):
                    for j, spec in enumerate(lists[e]):
                        copy_of(i, j, spec).start()

        for i in range(0, count, 2):
            for k in (i, i + 1):
                for j, spec in enumerate(lists[0]):
                    copy_of(k, j, spec).wait()
            left = jnp.concatenate([slices[i][part], slices[i + 1][part]], axis=1)
            value = jnp.dot(left, held[i * depth : (i + 2) * depth], preferred_element_type=f32)
            if i > 0:
                value = out[...] + value
            elif extra:
                value = refs[0][part] + value
            out[...] = value.astype(dtype)

    return call(
        kernel, jax.ShapeDtypeStruct((rows, cols), dtype), [SM] + [VM] * count + [HBM] * len(arrays) + [VM] * len(extra),
        [pltpu.VMEM((count * depth, cols), bf16), pltpu.SemaphoreType.DMA((count, len(lists[0])))],
        where, *[full[spot] for spot in spots], *arrays, *extra,
    )


def add_rounded(mine, got):
    def kernel(m, g, y, v):
        value = m[...] + g[...].astype(f32)
        y[...] = value
        v[...] = value.astype(bf16)

    out = [jax.ShapeDtypeStruct(mine.shape, f32), jax.ShapeDtypeStruct(mine.shape, bf16)]
    return call(kernel, out, [VM] * 2, [], mine, got)


def arrange(where, full):
    spots = list(full)

    def kernel(where_ref, *refs):
        for spot, part in zip(spots, refs[:8]):
            refs[8][place_of(where_ref, *spot)] = part[...]

    out = jax.ShapeDtypeStruct((8,) + full[spots[0]].shape, bf16)
    return call(kernel, out, [SM] + [VM] * 8, [], where, *[full[spot] for spot in spots])


def times_y(gram, arrays, spots, total, half, dtype):
    _, both, depth = gram.shape
    t = depth // BATCHES
    cols = arrays[0].shape[1]
    copies = [(i, 0, i * a.shape[0], a.shape[0]) for i, a in enumerate(arrays)]
    extra = [] if total is None else [total]
    halves = (0, 1) if half is None else (half,)
    rows = both // 2

    def kernel(gram_ref, *refs):
        ys = refs[len(extra) : len(extra) + len(arrays)]
        out, panel, sems = refs[-3:]
        for copy in start_copies(copies, ys, panel, sems):
            copy.wait()
        for i, one in enumerate(halves):
            part = slice(one * rows, (one + 1) * rows)
            left = jnp.concatenate([gram_ref[e, part, j * t : (j + 1) * t] for e, j in spots], axis=1)
            value = jnp.dot(left, panel[...], preferred_element_type=f32)
            if extra:
                value = refs[0][part] + value
            out[i * rows : (i + 1) * rows] = value.astype(dtype)

    return call(
        kernel, jax.ShapeDtypeStruct((rows * len(halves), cols), dtype), [VM] * (1 + len(extra)) + [HBM] * len(arrays),
        [pltpu.VMEM((len(spots) * t, cols), bf16), pltpu.SemaphoreType.DMA((len(copies),))],
        gram, *extra, *arrays,
    )


def result(own, y, mine, got):
    def kernel(own_ref, y_ref, m, g, out):
        square = m[...] + g[...].astype(f32)
        out[...] = (lead_coef * own_ref[...].astype(f32) + square_coef * y_ref[...] + quart_coef * square).astype(bf16)

    return call(kernel, jax.ShapeDtypeStruct(own.shape, bf16), [VM] * 4, [], own, y, mine, got)


def local(own):
    rows = own.shape[0]
    t = rows // 3
    core = lax.axis_index("c")
    where = jnp.stack([lax.axis_index("x"), lax.axis_index("zh"), 1 + 2 * core, 3 - 2 * core]).astype(jnp.int32)

    place = {}
    panel_copies = []
    batches = []
    queue = [(p, i, (plane, slot, i)) for p, (plane, slot) in enumerate(ARRIVAL) for i in range(3)]
    for b in range(BATCHES):
        mine = queue[8 * b : 8 * b + 8]
        used = sorted({p for p, _, _ in mine})
        copies = []
        for e, (p, i, key) in enumerate(mine):
            place[key] = (e, b)
            panel_copies.append((p, i * t, (e * BATCHES + b) * t, t))
            copies.append((used.index(p), i * t, e * t, t))
        batches.append((used, copies))
    panel_copies.sort(key=lambda c: c[2])
    x = {}

    def terms(b, send):
        used, copies = batches[b]
        return terms_of(where, own, w, [x[ARRIVAL[p]] for p in used], copies, send)

    r0 = along_y(own)
    w = swap_core(own)
    z = swap_zl(own)
    r1 = along_y(own, False)
    r0, w, z, r1 = together(r0, w, z, r1)
    x[0, "v"], x[0, "r0"], x[1, "v"], x[0, "r1"] = own, r0, z, r1
    rz0 = along_y(z)
    f = along_y(r0)
    rz1 = swap_zl(r1)
    got1 = partner(terms(0, True), True)
    keep1 = terms(0, False)
    rz0, f, rz1, got1, keep1 = together(rz0, f, rz1, got1, keep1)
    x[0, "f"], x[1, "r0"], x[1, "r1"] = f, rz0, rz1
    fz = along_y(rz0)
    mine1, other1 = sum_pair(keep1, got1)
    last1 = partner(other1, False)
    send2 = terms(1, True)
    got2 = partner(send2, True)
    keep2 = terms(1, False)
    fz, keep2 = together(fz, keep2)
    x[1, "f"] = fz
    send3 = terms(2, True)
    got2, send3, last1 = together(got2, send3, last1)
    got3 = partner(send3, True)
    keep3 = terms(2, False)
    z1 = swap_zh(sum_other(mine1, last1))
    mine2, other2 = sum_pair(keep2, got2)
    last2 = partner(other2, False)
    got3, keep3, last2, z1 = together(got3, keep3, last2, z1)
    z2 = swap_zh(sum_other(mine2, last2))
    mine3, other3 = sum_pair(keep3, got3)
    last3 = partner(other3, False)
    last3, z2 = together(last3, z2)
    z3 = swap_zh(sum_other(mine3, last3))
    mine = finish([(mine1, last1, z1), (mine2, last2, z2), (mine3, last3, z3)])
    arrays = [x[key] for key in ARRIVAL]

    a1 = swap_x1(mine)
    a3 = swap_x3(mine)
    b0 = swap_zh(mine)
    a1, a3, b0 = together(a1, a3, b0)
    b3 = swap_x3(b0)
    b1 = swap_x1(b0)
    a2 = swap_x3(a1)
    near = {(0, 0): mine, (1, 0): a1, (3, 0): a3, (0, 1): b0}
    part = times_x(where, near, arrays, panel_copies, None, None, f32)
    b1, b3, part = together(b1, b3, part)
    b2 = swap_x1(b3)
    next_ones = {(1, 1): b1, (3, 1): b3}
    part = times_x(where, next_ones, arrays, panel_copies, part, None, f32)
    a2, b2, part = together(a2, b2, part)
    late = {(2, 0): a2, (2, 1): b2}
    give = times_x(where, late, arrays, panel_copies, part, 1, bf16)
    got = swap_core(give)
    y = times_x(where, late, arrays, panel_copies, part, 0, f32)
    got, y = together(got, y)
    y, v = add_rounded(y, got)

    def add(total, keys, half=None, dtype=f32):
        spots = [place[plane, slot, i] for plane, slot in keys for i in range(3)]
        return times_y(gram, [u[key] for key in keys], spots, total, half, dtype)

    u = {}
    r0 = along_y(v)
    r1 = along_y(v, False)
    z = swap_zl(v)
    gram = arrange(where, near | next_ones | late)
    r0, z, r1, gram = together(r0, z, r1, gram)
    u[0, "v"], u[0, "r0"], u[1, "v"], u[0, "r1"] = v, r0, z, r1
    rz0 = along_y(z)
    f = along_y(r0)
    rz1 = swap_zl(r1)
    total = add(None, ARRIVAL[:4])
    rz0, f, rz1, total = together(rz0, f, rz1, total)
    u[0, "f"], u[1, "r0"], u[1, "r1"] = f, rz0, rz1
    fz = along_y(rz0)
    total = add(total, ARRIVAL[4:7])
    fz, total = together(fz, total)
    u[1, "f"] = fz
    got = swap_core(add(total, ARRIVAL[7:], 1, bf16))
    mine = add(total, ARRIVAL[7:], 0)
    got, mine = together(got, mine)
    return result(own, y, mine, got)


def solution(mesh):
    fine = Mesh(mesh.devices.reshape(SIZES), AXES)
    spec = P(ROW, COL)
    return jax.shard_map(local, mesh=fine, in_specs=(spec,), out_specs=spec, check_vma=False)
```

time: 469 us -> 221 us (0.47)
  waiting for transfers between devices: 419 us -> 124 us
  starting transfers between devices: 0.16 us -> 56.7 us
  Pallas kernels: 0 us -> 39.5 us
  matrix products: 34.7 us -> 0 us
  between operations: 13.1 us -> 0.23 us
    all_gather x4 -> x0, waiting for transfers between devices: 291 us -> none  [the longest x1 84.7 us: local(): panel = lax.all_gather(iterate, 'row', axis=0, tiled=True)]
    reduce_scatter x1 -> x0, waiting for transfers between devices: 126 us -> none  [local(): summed = lax.psum_scatter(terms, 'col', scatter_dimension=0, tiled=True)]
    ppermute x0 -> x33, waiting for transfers between devices: none -> 124 us  [the longest x10 58.6 us: along_y(): return lax.ppermute(v, ('y', 'c'), pairs)]
    ppermute x0 -> x33, starting transfers between devices: none -> 56.7 us  [the longest x4 13 us: swap_zh(): return lax.ppermute(v, 'zh', [(0, 1), (1, 0)])]
    pallas_call x0 -> x24, Pallas kernels: none -> 39.5 us  [call(): pl.pallas_call(kernel, out_shape=out_shape, in_specs=in_specs, out_specs=...]
    dot_general x3 -> x0, matrix products: 34.7 us -> none  [the longest x1 13.5 us: local(): jnp.einsum('ik,jk->ij', panel, iterate, preferred_element_type=jnp.float32)]
  transfers between devices with their start and end apart: 5 -> 33, of which waited for: 5 -> 26; matrix products, arithmetic and copies ran while one was open for 0% -> 0% of each run, Pallas kernels for 0% -> 16%
where the time goes in v1:
time: 221 us
  waiting for transfers between devices  124 us (56%)
  starting transfers between devices  56.7 us (26%)
  Pallas kernels  39.5 us (18%)
    ppermute x10, waiting for transfers between devices, along_y(): return lax.ppermute(v, ('y', 'c'), pairs)  58.6 us
    pallas_call x24, Pallas kernels, call(): pl.pallas_call(kernel, out_shape=out_shape, in_specs=in_specs, out_specs=...  39.5 us
    ppermute x3, waiting for transfers between devices, swap_x3(): return lax.ppermute(v, 'x', [(i, i ^ 3) for i in range(4)])  21.3 us
    ppermute x6, waiting for transfers between devices, partner(): return lax.ppermute(v, ('c', 'x'), pairs)  18.6 us
    ppermute x4, waiting for transfers between devices, swap_zh(): return lax.ppermute(v, 'zh', [(0, 1), (1, 0)])  15.9 us
    ppermute x4, starting transfers between devices, swap_zh(): return lax.ppermute(v, 'zh', [(0, 1), (1, 0)])  13 us
    ppermute x10, starting transfers between devices, along_y(): return lax.ppermute(v, ('y', 'c'), pairs)  12.5 us
    ppermute x3, starting transfers between devices, swap_core(): return lax.ppermute(v, 'c', [(0, 1), (1, 0)])  10.8 us
  transfers between devices with their start and end apart: 33, of which 26 were waited for; matrix products, arithmetic and copies ran while one was open for 0% of the time, Pallas kernels for 16%

profile of v1, /device:TPU:1, one launch (start us, length us, event | category | flops | bytes accessed | tf_op | source)
XLA Modules:
  0.0 221.3 jit_solution(11472961710478745420)
XLA Ops:
  0.0 2.1 collective-permute-start.3
  3.8 2.7 %collective-permute-start.1 = (bf16[384,1152]{1,0:T(8,128)(2,1)}, bf16[384,1152]{1,0:T(8,128)(2,1)S(1)}, u32[]{:S(2)}, u32[]{:S(2)}) collective-permute-start(bf16[384,1152]{1,0:T(8,128)(2,1)} %own_ref.13), channel_id=1, source_target_pairs={{0,8},{8,0},{1,9},{9,1},{2,10},{10,2},{3,11},{11,3},{4,12},{12,4},... | collective-permute-start | bytes 2654216 | tf_op jit(solution)/shard_map/ppermute | solution.py:31
  6.9 11.0 %collective-permute-done.3.refs_1_.refs_7_.refs_5_ = bf16[384,1152]{1,0:T(8,128)(2,1)S(1)} collective-permute-done((bf16[384,1152]{1,0:T(8,128)(2,1)}, bf16[384,1152]{1,0:T(8,128)(2,1)S(1)}, u32[]{:S(2)}, u32[]{:S(2)}) %collective-permute-start.3) | collective-permute-done | bytes 884768 | tf_op jit(solution)/shard_map/ppermute | solution.py:56
  17.9 3.6 %collective-permute-done.2.refs_2_.refs_0_.refs_6_.refs_4_ = bf16[384,1152]{1,0:T(8,128)(2,1)S(1)} collective-permute-done((bf16[384,1152]{1,0:T(8,128)(2,1)}, bf16[384,1152]{1,0:T(8,128)(2,1)S(1)}, u32[]{:S(2)}, u32[]{:S(2)}) %collective-permute-start.2) | collective-permute-done | bytes 884768 | tf_op jit(solution)/shard_map/ppermute | solution.py:23
  21.5 3.0 %collective-permute-done.refs_1_.refs_5_.refs_3_ = bf16[384,1152]{1,0:T(8,128)(2,1)S(1)} collective-permute-done((bf16[384,1152]{1,0:T(8,128)(2,1)}, bf16[384,1152]{1,0:T(8,128)(2,1)S(1)}, u32[]{:S(2)}, u32[]{:S(2)}) %collective-permute-start) | collective-permute-done | bytes 884768 | tf_op jit(solution)/shard_map/ppermute | solution.py:56
  24.5 3.0 %collective-permute-start.5 = (bf16[384,1152]{1,0:T(8,128)(2,1)S(1)}, bf16[384,1152]{1,0:T(8,128)(2,1)S(1)}, u32[]{:S(2)}, u32[]{:S(2)}) collective-permute-start(bf16[384,1152]{1,0:T(8,128)(2,1)S(1)} %collective-permute-done.refs_1_.refs_5_.refs_3_), channel_id=1, source_target_pairs={{0,16},{8,56},{16,32},{24,8},{32,48},{40,24},{48,0},{56,40},{1,17}... | collective-permute-start | bytes 2654216 | tf_op jit(solution)/shard_map/ppermute | solution.py:56
  30.4 2.4 %shard_map.17 = bf16[2,2,768,128]{3,2,1,0:T(8,128)(2,1)S(1)} custom-call(s32[4]{0:T(128)S(1)} %pad_add_fusion.where_ref, bf16[384,1152]{1,0:T(8,128)(2,1)S(1)} %copy-done, bf16[384,1152]{1,0:T(8,128)(2,1)S(1)} %collective-permute-done.1.sib_ref, bf16[384,1152]{1,0:T(8,128)(2,1)S(1)} %copy-done, ...), custom_call_target="tpu_custom_call" | custom-call | tf_op jit(solution)/shard_map/pallas_call | solution.py:74
  32.8 2.6 %collective-permute-start.7 = (bf16[2,2,768,128]{3,2,1,0:T(8,128)(2,1)S(1)}, bf16[2,2,768,128]{3,2,1,0:T(8,128)(2,1)S(1)}, u32[]{:S(2)}, u32[]{:S(2)}) collective-permute-start(bf16[2,2,768,128]{3,2,1,0:T(8,128)(2,1)S(1)} %shard_map.17), channel_id=1, source_target_pairs={{0,1},{1,0},{2,3},{3,2},{8,11},{9,10},{10,9},{11,8},{4,5},{5,4},{6... | collective-permute-start | bytes 2359304 | tf_op jit(solution)/shard_map/ppermute | solution.py:47
  35.3 2.4 %shard_map.18.k = f32[2,2,768,128]{3,2,1,0:T(8,128)S(1)} custom-call(s32[4]{0:T(128)S(1)} %pad_add_fusion.where_ref, bf16[384,1152]{1,0:T(8,128)(2,1)S(1)} %copy-done.1, bf16[384,1152]{1,0:T(8,128)(2,1)S(1)} %collective-permute-done.1.sib_ref, bf16[384,1152]{1,0:T(8,128)(2,1)S(1)} %copy-done.1, ...), custom_call_target="tpu_custom_call" | custom-call | tf_op jit(solution)/shard_map/pallas_call | solution.py:74
  37.7 7.5 %collective-permute-done.7.g = bf16[2,2,768,128]{3,2,1,0:T(8,128)(2,1)S(1)} collective-permute-done((bf16[2,2,768,128]{3,2,1,0:T(8,128)(2,1)S(1)}, bf16[2,2,768,128]{3,2,1,0:T(8,128)(2,1)S(1)}, u32[]{:S(2)}, u32[]{:S(2)}) %collective-permute-start.7) | collective-permute-done | bytes 786464 | tf_op jit(solution)/shard_map/ppermute | solution.py:47
  45.2 2.8 %collective-permute-done.6.refs_1_.refs_10_.refs_8_ = bf16[384,1152]{1,0:T(8,128)(2,1)S(1)} collective-permute-done((bf16[384,1152]{1,0:T(8,128)(2,1)S(1)}, bf16[384,1152]{1,0:T(8,128)(2,1)S(1)}, u32[]{:S(2)}, u32[]{:S(2)}) %collective-permute-start.6) | collective-permute-done | bytes 884768 | tf_op jit(solution)/shard_map/ppermute | solution.py:23
  48.0 2.0 collective-permute-start.9
  50.1 2.4 %shard_map.20 = bf16[2,2,768,128]{3,2,1,0:T(8,128)(2,1)S(1)} custom-call(s32[4]{0:T(128)S(1)} %pad_add_fusion.where_ref, bf16[384,1152]{1,0:T(8,128)(2,1)S(1)} %copy-done.1, bf16[384,1152]{1,0:T(8,128)(2,1)S(1)} %collective-permute-done.1.sib_ref, bf16[384,1152]{1,0:T(8,128)(2,1)S(1)} %collective-permute-done.2.refs_2_.refs_0_.refs_6_.refs_4_, ...), custom_call_target="tpu_custom_call" | custom-call | tf_op jit(solution)/shard_map/pallas_call | solution.py:74
  52.5 2.6 %collective-permute-start.8 = (bf16[2,2,768,128]{3,2,1,0:T(8,128)(2,1)S(1)}, bf16[2,2,768,128]{3,2,1,0:T(8,128)(2,1)S(1)}, u32[]{:S(2)}, u32[]{:S(2)}) collective-permute-start(bf16[2,2,768,128]{3,2,1,0:T(8,128)(2,1)S(1)} %shard_map.20), channel_id=1, source_target_pairs={{0,1},{1,0},{2,3},{3,2},{8,11},{9,10},{10,9},{11,8},{4,5},{5,4},{6... | collective-permute-start | bytes 2359304 | tf_op jit(solution)/shard_map/ppermute | solution.py:47
  55.3 2.4 %shard_map.21.k = f32[2,2,768,128]{3,2,1,0:T(8,128)S(1)} custom-call(s32[4]{0:T(128)S(1)} %pad_add_fusion.where_ref, bf16[384,1152]{1,0:T(8,128)(2,1)S(1)} %copy-done.1, bf16[384,1152]{1,0:T(8,128)(2,1)S(1)} %collective-permute-done.1.sib_ref, bf16[384,1152]{1,0:T(8,128)(2,1)S(1)} %collective-permute-done.2.refs_2_.refs_0_.refs_6_.refs_4_, ...), custom_call_target="tpu_custom_call" | custom-call | tf_op jit(solution)/shard_map/pallas_call | solution.py:74
  57.7 2.5 %collective-permute-done.9.refs_2_.refs_11_.refs_9_ = bf16[384,1152]{1,0:T(8,128)(2,1)S(1)} collective-permute-done((bf16[384,1152]{1,0:T(8,128)(2,1)S(1)}, bf16[384,1152]{1,0:T(8,128)(2,1)S(1)}, u32[]{:S(2)}, u32[]{:S(2)}) %collective-permute-start.9) | collective-permute-done | bytes 884768 | tf_op jit(solution)/shard_map/ppermute | solution.py:56
  60.2 2.4 %shard_map.22 = bf16[2,2,768,128]{3,2,1,0:T(8,128)(2,1)S(1)} custom-call(s32[4]{0:T(128)S(1)} %pad_add_fusion.where_ref, bf16[384,1152]{1,0:T(8,128)(2,1)S(1)} %copy-done.1, bf16[384,1152]{1,0:T(8,128)(2,1)S(1)} %collective-permute-done.1.sib_ref, bf16[384,1152]{1,0:T(8,128)(2,1)S(1)} %collective-permute-done.4.refs_3_.refs_0_.refs_9_.refs_7_, ...), custom_call_target="tpu_custom_call" | custom-call | tf_op jit(solution)/shard_map/pallas_call | solution.py:74
  62.6 3.9 %collective-permute-done.10.g.refs_1_ = bf16[2,768,128]{2,1,0:T(8,128)(2,1)S(1)} collective-permute-done((bf16[2,768,128]{2,1,0:T(8,128)(2,1)S(1)}, bf16[2,768,128]{2,1,0:T(8,128)(2,1)S(1)}, u32[]{:S(2)}, u32[]{:S(2)}) %collective-permute-start.10) | collective-permute-done | bytes 393248 | tf_op jit(solution)/shard_map/ppermute | solution.py:47
  66.5 2.3 %collective-permute-done.8.g = bf16[2,2,768,128]{3,2,1,0:T(8,128)(2,1)S(1)} collective-permute-done((bf16[2,2,768,128]{3,2,1,0:T(8,128)(2,1)S(1)}, bf16[2,2,768,128]{3,2,1,0:T(8,128)(2,1)S(1)}, u32[]{:S(2)}, u32[]{:S(2)}) %collective-permute-start.8) | collective-permute-done | bytes 786464 | tf_op jit(solution)/shard_map/ppermute | solution.py:47
  68.8 2.5 %collective-permute-start.11 = (bf16[2,2,768,128]{3,2,1,0:T(8,128)(2,1)S(1)}, bf16[2,2,768,128]{3,2,1,0:T(8,128)(2,1)S(1)}, u32[]{:S(2)}, u32[]{:S(2)}) collective-permute-start(bf16[2,2,768,128]{3,2,1,0:T(8,128)(2,1)S(1)} %shard_map.22), channel_id=1, source_target_pairs={{0,1},{1,0},{2,3},{3,2},{8,11},{9,10},{10,9},{11,8},{4,5},{5,4},{6... | collective-permute-start | bytes 2359304 | tf_op jit(solution)/shard_map/ppermute | solution.py:47
  71.6 3.7 %collective-permute-start.13 = (bf16[768,128]{1,0:T(8,128)(2,1)S(1)}, bf16[768,128]{1,0:T(8,128)(2,1)S(1)}, u32[]{:S(2)}, u32[]{:S(2)}) collective-permute-start(bf16[768,128]{1,0:T(8,128)(2,1)S(1)} %shard_map.25), channel_id=1, source_target_pairs={{0,4},{4,0},{1,5},{5,1},{2,6},{6,2},{3,7},{7,3},{8,12},{12,8},{9,1... | collective-permute-start | bytes 589832 | tf_op jit(solution)/shard_map/ppermute | solution.py:27
  75.3 2.4 %shard_map.23.k = f32[2,2,768,128]{3,2,1,0:T(8,128)S(1)} custom-call(s32[4]{0:T(128)S(1)} %pad_add_fusion.where_ref, bf16[384,1152]{1,0:T(8,128)(2,1)S(1)} %copy-done.1, bf16[384,1152]{1,0:T(8,128)(2,1)S(1)} %collective-permute-done.1.sib_ref, bf16[384,1152]{1,0:T(8,128)(2,1)S(1)} %collective-permute-done.4.refs_3_.refs_0_.refs_9_.refs_7_, ...), custom_call_target="tpu_custom_call" | custom-call | tf_op jit(solution)/shard_map/pallas_call | solution.py:74
  77.7 2.4 %collective-permute-done.13.refs_2_ = bf16[768,128]{1,0:T(8,128)(2,1)S(1)} collective-permute-done((bf16[768,128]{1,0:T(8,128)(2,1)S(1)}, bf16[768,128]{1,0:T(8,128)(2,1)S(1)}, u32[]{:S(2)}, u32[]{:S(2)}) %collective-permute-start.13) | collective-permute-done | bytes 196640 | tf_op jit(solution)/shard_map/ppermute | solution.py:27
  80.1 2.6 %collective-permute-done.12.g.refs_4_ = bf16[2,768,128]{2,1,0:T(8,128)(2,1)S(1)} collective-permute-done((bf16[2,768,128]{2,1,0:T(8,128)(2,1)S(1)}, bf16[2,768,128]{2,1,0:T(8,128)(2,1)S(1)}, u32[]{:S(2)}, u32[]{:S(2)}) %collective-permute-start.12) | collective-permute-done | bytes 393248 | tf_op jit(solution)/shard_map/ppermute | solution.py:47
  82.8 2.3 %collective-permute-done.11.g = bf16[2,2,768,128]{3,2,1,0:T(8,128)(2,1)S(1)} collective-permute-done((bf16[2,2,768,128]{3,2,1,0:T(8,128)(2,1)S(1)}, bf16[2,2,768,128]{3,2,1,0:T(8,128)(2,1)S(1)}, u32[]{:S(2)}, u32[]{:S(2)}) %collective-permute-start.11) | collective-permute-done | bytes 786464 | tf_op jit(solution)/shard_map/ppermute | solution.py:47
  85.3 3.7 %collective-permute-start.15 = (bf16[768,128]{1,0:T(8,128)(2,1)S(1)}, bf16[768,128]{1,0:T(8,128)(2,1)S(1)}, u32[]{:S(2)}, u32[]{:S(2)}) collective-permute-start(bf16[768,128]{1,0:T(8,128)(2,1)S(1)} %shard_map.27), channel_id=1, source_target_pairs={{0,4},{4,0},{1,5},{5,1},{2,6},{6,2},{3,7},{7,3},{8,12},{12,8},{9,1... | collective-permute-start | bytes 589832 | tf_op jit(solution)/shard_map/ppermute | solution.py:27
  89.0 4.2 %collective-permute-done.15.refs_5_ = bf16[768,128]{1,0:T(8,128)(2,1)S(1)} collective-permute-done((bf16[768,128]{1,0:T(8,128)(2,1)S(1)}, bf16[768,128]{1,0:T(8,128)(2,1)S(1)}, u32[]{:S(2)}, u32[]{:S(2)}) %collective-permute-start.15) | collective-permute-done | bytes 196640 | tf_op jit(solution)/shard_map/ppermute | solution.py:27
  93.3 2.9 %collective-permute-start.16 = (bf16[768,128]{1,0:T(8,128)(2,1)S(1)}, bf16[768,128]{1,0:T(8,128)(2,1)S(1)}, u32[]{:S(2)}, u32[]{:S(2)}) collective-permute-start(bf16[768,128]{1,0:T(8,128)(2,1)S(1)} %shard_map.28), channel_id=1, source_target_pairs={{0,4},{4,0},{1,5},{5,1},{2,6},{6,2},{3,7},{7,3},{8,12},{12,8},{9,1... | collective-permute-start | bytes 589832 | tf_op jit(solution)/shard_map/ppermute | solution.py:27
  96.2 3.4 %collective-permute-done.16.refs_8_ = bf16[768,128]{1,0:T(8,128)(2,1)S(1)} collective-permute-done((bf16[768,128]{1,0:T(8,128)(2,1)S(1)}, bf16[768,128]{1,0:T(8,128)(2,1)S(1)}, u32[]{:S(2)}, u32[]{:S(2)}) %collective-permute-start.16) | collective-permute-done | bytes 196640 | tf_op jit(solution)/shard_map/ppermute | solution.py:27
  99.8 2.7 %collective-permute-start.19 = (bf16[768,384]{1,0:T(8,128)(2,1)S(1)}, bf16[768,384]{1,0:T(8,128)(2,1)S(1)}, u32[]{:S(2)}, u32[]{:S(2)}) collective-permute-start(bf16[768,384]{1,0:T(8,128)(2,1)S(1)} %shard_map.29.refs_0_), channel_id=1, source_target_pairs={{0,4},{4,0},{1,5},{5,1},{2,6},{6,2},{3,7},{7,3},{8,12},{12,8},{9,1... | collective-permute-start | bytes 1769480 | tf_op jit(solution)/shard_map/ppermute | solution.py:27
  102.5 5.0 %collective-permute-start.18 = (bf16[768,384]{1,0:T(8,128)(2,1)S(1)}, bf16[768,384]{1,0:T(8,128)(2,1)S(1)}, u32[]{:S(2)}, u32[]{:S(2)}) collective-permute-start(bf16[768,384]{1,0:T(8,128)(2,1)S(1)} %shard_map.29.refs_0_), channel_id=1, source_target_pairs={{0,3},{1,2},{2,1},{3,0},{4,7},{5,6},{6,5},{7,4},{8,11},{9,10},{10,... | collective-permute-start | bytes 1769480 | tf_op jit(solution)/shard_map/ppermute | solution.py:39
  107.5 5.9 %collective-permute-done.19.refs_3_ = bf16[768,384]{1,0:T(8,128)(2,1)S(1)} collective-permute-done((bf16[768,384]{1,0:T(8,128)(2,1)S(1)}, bf16[768,384]{1,0:T(8,128)(2,1)S(1)}, u32[]{:S(2)}, u32[]{:S(2)}) %collective-permute-start.19) | collective-permute-done | bytes 589856 | tf_op jit(solution)/shard_map/ppermute | solution.py:27
  113.4 6.4 %collective-permute-done.18.refs_2_ = bf16[768,384]{1,0:T(8,128)(2,1)S(1)} collective-permute-done((bf16[768,384]{1,0:T(8,128)(2,1)S(1)}, bf16[768,384]{1,0:T(8,128)(2,1)S(1)}, u32[]{:S(2)}, u32[]{:S(2)}) %collective-permute-start.18) | collective-permute-done | bytes 589856 | tf_op jit(solution)/shard_map/ppermute | solution.py:39
  123.7 5.6 %shard_map.30.refs_10_ = f32[768,1152]{1,0:T(8,128)S(1)} custom-call(s32[4]{0:T(128)S(1)} %pad_add_fusion.where_ref, bf16[768,384]{1,0:T(8,128)(2,1)S(1)} %shard_map.29.refs_0_, bf16[768,384]{1,0:T(8,128)(2,1)S(1)} %collective-permute-done.17.refs_1_, bf16[768,384]{1,0:T(8,128)(2,1)S(1)} %collective-permute-done.18.refs_2_, ...), custom_call_target="tpu_custom_call" | custom-call | tf_op jit(solution)/shard_map/pallas_call | solution.py:74
  129.3 5.5 %collective-permute-done.22.refs_1_.refs_5_ = bf16[768,384]{1,0:T(8,128)(2,1)S(1)} collective-permute-done((bf16[768,384]{1,0:T(8,128)(2,1)S(1)}, bf16[768,384]{1,0:T(8,128)(2,1)S(1)}, u32[]{:S(2)}, u32[]{:S(2)}) %collective-permute-start.22) | collective-permute-done | bytes 589856 | tf_op jit(solution)/shard_map/ppermute | solution.py:39
  135.2 2.8 %shard_map.31.refs_10_ = f32[768,1152]{1,0:T(8,128)S(1)} custom-call(s32[4]{0:T(128)S(1)} %pad_add_fusion.where_ref, bf16[768,384]{1,0:T(8,128)(2,1)S(1)} %collective-permute-done.21.refs_0_.refs_4_, bf16[768,384]{1,0:T(8,128)(2,1)S(1)} %collective-permute-done.22.refs_1_.refs_5_, bf16[384,1152]{1,0:T(8,128)(2,1)S(1)} %copy-done.1, ...), custom_call_target="tpu_custom_call" | custom-call | tf_op jit(solution)/shard_map/pallas_call | solution.py:74
  138.0 9.4 %collective-permute-done.20.refs_0_.refs_6_ = bf16[768,384]{1,0:T(8,128)(2,1)S(1)} collective-permute-done((bf16[768,384]{1,0:T(8,128)(2,1)S(1)}, bf16[768,384]{1,0:T(8,128)(2,1)S(1)}, u32[]{:S(2)}, u32[]{:S(2)}) %collective-permute-start.20) | collective-permute-done | bytes 589856 | tf_op jit(solution)/shard_map/ppermute | solution.py:39
  147.4 2.0 shard_map.32
  149.4 3.6 %collective-permute-start.24 = (bf16[384,1152]{1,0:T(8,128)(2,1)S(1)}, bf16[384,1152]{1,0:T(8,128)(2,1)S(1)}, u32[]{:S(2)}, u32[]{:S(2)}) collective-permute-start(bf16[384,1152]{1,0:T(8,128)(2,1)S(1)} %shard_map.32), channel_id=1, source_target_pairs={{0,8},{8,0},{1,9},{9,1},{2,10},{10,2},{3,11},{11,3},{4,12},{12,4},... | collective-permute-start | bytes 2654216 | tf_op jit(solution)/shard_map/ppermute | solution.py:31
  153.0 2.2 %shard_map.33.m = f32[384,1152]{1,0:T(8,128)S(1)} custom-call(s32[4]{0:T(128)S(1)} %pad_add_fusion.where_ref, bf16[768,384]{1,0:T(8,128)(2,1)S(1)} %collective-permute-done.20.refs_0_.refs_6_, bf16[768,384]{1,0:T(8,128)(2,1)S(1)} %collective-permute-done.23.refs_1_.refs_7_, bf16[384,1152]{1,0:T(8,128)(2,1)S(1)} %copy-done.1, ...), custom_call_target="tpu_custom_call" | custom-call | tf_op jit(solution)/shard_map/pallas_call | solution.py:74
  156.3 2.6 %collective-permute-start.25 = (bf16[384,1152]{1,0:T(8,128)(2,1)S(1)}, bf16[384,1152]{1,0:T(8,128)(2,1)S(1)}, u32[]{:S(2)}, u32[]{:S(2)}) collective-permute-start(bf16[384,1152]{1,0:T(8,128)(2,1)S(1)} %get-tuple-element.94.refs_0_), channel_id=1, source_target_pairs={{0,16},{8,56},{16,32},{24,8},{32,48},{40,24},{48,0},{56,40},{1,17}... | collective-permute-start | bytes 2654216 | tf_op jit(solution)/shard_map/ppermute | solution.py:56
  159.9 16.8 %collective-permute-done.27.refs_3_ = bf16[384,1152]{1,0:T(8,128)(2,1)S(1)} collective-permute-done((bf16[384,1152]{1,0:T(8,128)(2,1)S(1)}, bf16[384,1152]{1,0:T(8,128)(2,1)S(1)}, u32[]{:S(2)}, u32[]{:S(2)}) %collective-permute-start.27) | collective-permute-done | bytes 884768 | tf_op jit(solution)/shard_map/ppermute | solution.py:56
  179.2 4.0 %shard_map.36.refs_0_ = f32[768,1152]{1,0:T(8,128)S(1)} custom-call(bf16[8,768,384]{2,1,0:T(8,128)(2,1)S(1)} %shard_map.35.gram_ref, bf16[384,1152]{1,0:T(8,128)(2,1)S(1)} %get-tuple-element.94.refs_0_, bf16[384,1152]{1,0:T(8,128)(2,1)S(1)} %collective-permute-done.25.refs_1_, bf16[384,1152]{1,0:T(8,128)(2,1)S(1)} %collective-permute-done.26.refs_2_, ...), custom_call_target="tpu_custom_call" | custom-call | tf_op jit(solution)/shard_map/pallas_call | solution.py:74
  183.2 6.8 %collective-permute-done.28.refs_2_ = bf16[384,1152]{1,0:T(8,128)(2,1)S(1)} collective-permute-done((bf16[384,1152]{1,0:T(8,128)(2,1)S(1)}, bf16[384,1152]{1,0:T(8,128)(2,1)S(1)}, u32[]{:S(2)}, u32[]{:S(2)}) %collective-permute-start.28) | collective-permute-done | bytes 884768 | tf_op jit(solution)/shard_map/ppermute | solution.py:56
  190.0 9.5 %collective-permute-done.29.refs_1_ = bf16[384,1152]{1,0:T(8,128)(2,1)S(1)} collective-permute-done((bf16[384,1152]{1,0:T(8,128)(2,1)S(1)}, bf16[384,1152]{1,0:T(8,128)(2,1)S(1)}, u32[]{:S(2)}, u32[]{:S(2)}) %collective-permute-start.29) | collective-permute-done | bytes 884768 | tf_op jit(solution)/shard_map/ppermute | solution.py:56
  201.1 3.3 %shard_map.37.refs_0_ = f32[768,1152]{1,0:T(8,128)S(1)} custom-call(bf16[8,768,384]{2,1,0:T(8,128)(2,1)S(1)} %shard_map.35.gram_ref, f32[768,1152]{1,0:T(8,128)S(1)} %shard_map.36.refs_0_, bf16[384,1152]{1,0:T(8,128)(2,1)S(1)} %collective-permute-done.29.refs_1_, bf16[384,1152]{1,0:T(8,128)(2,1)S(1)} %collective-permute-done.28.refs_2_, ...), custom_call_target="tpu_custom_call" | custom-call | tf_op jit(solution)/shard_map/pallas_call | solution.py:74
  204.4 7.9 %collective-permute-done.31.refs_1_ = bf16[384,1152]{1,0:T(8,128)(2,1)S(1)} collective-permute-done((bf16[384,1152]{1,0:T(8,128)(2,1)S(1)}, bf16[384,1152]{1,0:T(8,128)(2,1)S(1)}, u32[]{:S(2)}, u32[]{:S(2)}) %collective-permute-start.31) | collective-permute-done | bytes 884768 | tf_op jit(solution)/shard_map/ppermute | solution.py:56
  213.2 4.6 %collective-permute-start.32 = (bf16[384,1152]{1,0:T(8,128)(2,1)S(1)}, bf16[384,1152]{1,0:T(8,128)(2,1)S(1)}, u32[]{:S(2)}, u32[]{:S(2)}) collective-permute-start(bf16[384,1152]{1,0:T(8,128)(2,1)S(1)} %shard_map.38), channel_id=1, source_target_pairs={{0,8},{8,0},{1,9},{9,1},{2,10},{10,2},{3,11},{11,3},{4,12},{12,4},... | collective-permute-start | bytes 2654216 | tf_op jit(solution)/shard_map/ppermute | solution.py:31
  (47 shorter events, 21.0 us)
Async XLA Ops:
  0.0 17.9 %collective-permute-start.3 = (bf16[384,1152]{1,0:T(8,128)(2,1)}, bf16[384,1152]{1,0:T(8,128)(2,1)S(1)}, u32[]{:S(2)}, u32[]{:S(2)}) collective-permute-start(bf16[384,1152]{1,0:T(8,128)(2,1)} %own_ref.13), channel_id=1, source_target_pairs={{0,48},{8,24},{16,0},{24,40},{32,16},{40,56},{48,32},{56,8},{1,49}... | collective-permute-start | bytes 2654216 | tf_op jit(solution)/shard_map/ppermute | solution.py:56
  2.1 19.4 %collective-permute-start.2 = (bf16[384,1152]{1,0:T(8,128)(2,1)}, bf16[384,1152]{1,0:T(8,128)(2,1)S(1)}, u32[]{:S(2)}, u32[]{:S(2)}) collective-permute-start(bf16[384,1152]{1,0:T(8,128)(2,1)} %own_ref.13), channel_id=1, source_target_pairs={{0,64},{64,0},{1,65},{65,1},{2,66},{66,2},{3,67},{67,3},{4,68},{68... | collective-permute-start | bytes 2654216 | tf_op jit(solution)/shard_map/ppermute | solution.py:23
  3.8 17.7 %collective-permute-start.1 = (bf16[384,1152]{1,0:T(8,128)(2,1)}, bf16[384,1152]{1,0:T(8,128)(2,1)S(1)}, u32[]{:S(2)}, u32[]{:S(2)}) collective-permute-start(bf16[384,1152]{1,0:T(8,128)(2,1)} %own_ref.13), channel_id=1, source_target_pairs={{0,8},{8,0},{1,9},{9,1},{2,10},{10,2},{3,11},{11,3},{4,12},{12,4},... | collective-permute-start | bytes 2654216 | tf_op jit(solution)/shard_map/ppermute | solution.py:31
  6.4 18.0 %collective-permute-start = (bf16[384,1152]{1,0:T(8,128)(2,1)}, bf16[384,1152]{1,0:T(8,128)(2,1)S(1)}, u32[]{:S(2)}, u32[]{:S(2)}) collective-permute-start(bf16[384,1152]{1,0:T(8,128)(2,1)} %own_ref.13), channel_id=1, source_target_pairs={{0,16},{8,56},{16,32},{24,8},{32,48},{40,24},{48,0},{56,40},{1,17}... | collective-permute-start | bytes 2654216 | tf_op jit(solution)/shard_map/ppermute | solution.py:56
  24.5 20.7 %collective-permute-start.5 = (bf16[384,1152]{1,0:T(8,128)(2,1)S(1)}, bf16[384,1152]{1,0:T(8,128)(2,1)S(1)}, u32[]{:S(2)}, u32[]{:S(2)}) collective-permute-start(bf16[384,1152]{1,0:T(8,128)(2,1)S(1)} %collective-permute-done.refs_1_.refs_5_.refs_3_), channel_id=1, source_target_pairs={{0,16},{8,56},{16,32},{24,8},{32,48},{40,24},{48,0},{56,40},{1,17}... | collective-permute-start | bytes 2654216 | tf_op jit(solution)/shard_map/ppermute | solution.py:56
  27.5 20.5 %collective-permute-start.6 = (bf16[384,1152]{1,0:T(8,128)(2,1)S(1)}, bf16[384,1152]{1,0:T(8,128)(2,1)S(1)}, u32[]{:S(2)}, u32[]{:S(2)}) collective-permute-start(bf16[384,1152]{1,0:T(8,128)(2,1)S(1)} %collective-permute-done.3.refs_1_.refs_7_.refs_5_), channel_id=1, source_target_pairs={{0,64},{64,0},{1,65},{65,1},{2,66},{66,2},{3,67},{67,3},{4,68},{68... | collective-permute-start | bytes 2654216 | tf_op jit(solution)/shard_map/ppermute | solution.py:23
  29.1 18.9 %collective-permute-start.4 = (bf16[384,1152]{1,0:T(8,128)(2,1)S(1)}, bf16[384,1152]{1,0:T(8,128)(2,1)S(1)}, u32[]{:S(2)}, u32[]{:S(2)}) collective-permute-start(bf16[384,1152]{1,0:T(8,128)(2,1)S(1)} %collective-permute-done.2.refs_2_.refs_0_.refs_6_.refs_4_), channel_id=1, source_target_pairs={{0,16},{8,56},{16,32},{24,8},{32,48},{40,24},{48,0},{56,40},{1,17}... | collective-permute-start | bytes 2654216 | tf_op jit(solution)/shard_map/ppermute | solution.py:56
  29.2 1.2 copy-start
  30.4 5.0 %copy-start.1 = (bf16[384,1152]{1,0:T(8,128)(2,1)S(1)}, bf16[384,1152]{1,0:T(8,128)(2,1)}, u32[]{:S(2)}) copy-start(bf16[384,1152]{1,0:T(8,128)(2,1)} %own_ref.13) | copy-start | bytes 2654212
  32.8 12.4 %collective-permute-start.7 = (bf16[2,2,768,128]{3,2,1,0:T(8,128)(2,1)S(1)}, bf16[2,2,768,128]{3,2,1,0:T(8,128)(2,1)S(1)}, u32[]{:S(2)}, u32[]{:S(2)}) collective-permute-start(bf16[2,2,768,128]{3,2,1,0:T(8,128)(2,1)S(1)} %shard_map.17), channel_id=1, source_target_pairs={{0,1},{1,0},{2,3},{3,2},{8,11},{9,10},{10,9},{11,8},{4,5},{5,4},{6... | collective-permute-start | bytes 2359304 | tf_op jit(solution)/shard_map/ppermute | solution.py:47
  48.0 12.2 %collective-permute-start.9 = (bf16[384,1152]{1,0:T(8,128)(2,1)S(1)}, bf16[384,1152]{1,0:T(8,128)(2,1)S(1)}, u32[]{:S(2)}, u32[]{:S(2)}) collective-permute-start(bf16[384,1152]{1,0:T(8,128)(2,1)S(1)} %collective-permute-done.4.refs_3_.refs_0_.refs_9_.refs_7_), channel_id=1, source_target_pairs={{0,16},{8,56},{16,32},{24,8},{32,48},{40,24},{48,0},{56,40},{1,17}... | collective-permute-start | bytes 2654216 | tf_op jit(solution)/shard_map/ppermute | solution.py:56
  52.5 16.3 %collective-permute-start.8 = (bf16[2,2,768,128]{3,2,1,0:T(8,128)(2,1)S(1)}, bf16[2,2,768,128]{3,2,1,0:T(8,128)(2,1)S(1)}, u32[]{:S(2)}, u32[]{:S(2)}) collective-permute-start(bf16[2,2,768,128]{3,2,1,0:T(8,128)(2,1)S(1)} %shard_map.20), channel_id=1, source_target_pairs={{0,1},{1,0},{2,3},{3,2},{8,11},{9,10},{10,9},{11,8},{4,5},{5,4},{6... | collective-permute-start | bytes 2359304 | tf_op jit(solution)/shard_map/ppermute | solution.py:47
  55.2 11.3 %collective-permute-start.10 = (bf16[2,768,128]{2,1,0:T(8,128)(2,1)S(1)}, bf16[2,768,128]{2,1,0:T(8,128)(2,1)S(1)}, u32[]{:S(2)}, u32[]{:S(2)}) collective-permute-start(bf16[2,768,128]{2,1,0:T(8,128)(2,1)S(1)} %get-tuple-element.67), channel_id=1, source_target_pairs={{0,3},{1,2},{2,1},{3,0},{8,9},{9,8},{10,11},{11,10},{4,7},{5,6},{6... | collective-permute-start | bytes 1179656 | tf_op jit(solution)/shard_map/ppermute | solution.py:47
  68.8 16.3 %collective-permute-start.11 = (bf16[2,2,768,128]{3,2,1,0:T(8,128)(2,1)S(1)}, bf16[2,2,768,128]{3,2,1,0:T(8,128)(2,1)S(1)}, u32[]{:S(2)}, u32[]{:S(2)}) collective-permute-start(bf16[2,2,768,128]{3,2,1,0:T(8,128)(2,1)S(1)} %shard_map.22), channel_id=1, source_target_pairs={{0,1},{1,0},{2,3},{3,2},{8,11},{9,10},{10,9},{11,8},{4,5},{5,4},{6... | collective-permute-start | bytes 2359304 | tf_op jit(solution)/shard_map/ppermute | solution.py:47
  71.5 11.3 %collective-permute-start.12 = (bf16[2,768,128]{2,1,0:T(8,128)(2,1)S(1)}, bf16[2,768,128]{2,1,0:T(8,128)(2,1)S(1)}, u32[]{:S(2)}, u32[]{:S(2)}) collective-permute-start(bf16[2,768,128]{2,1,0:T(8,128)(2,1)S(1)} %get-tuple-element.72), channel_id=1, source_target_pairs={{0,3},{1,2},{2,1},{3,0},{8,9},{9,8},{10,11},{11,10},{4,7},{5,6},{6... | collective-permute-start | bytes 1179656 | tf_op jit(solution)/shard_map/ppermute | solution.py:47
  71.6 8.5 %collective-permute-start.13 = (bf16[768,128]{1,0:T(8,128)(2,1)S(1)}, bf16[768,128]{1,0:T(8,128)(2,1)S(1)}, u32[]{:S(2)}, u32[]{:S(2)}) collective-permute-start(bf16[768,128]{1,0:T(8,128)(2,1)S(1)} %shard_map.25), channel_id=1, source_target_pairs={{0,4},{4,0},{1,5},{5,1},{2,6},{6,2},{3,7},{7,3},{8,12},{12,8},{9,1... | collective-permute-start | bytes 589832 | tf_op jit(solution)/shard_map/ppermute | solution.py:27
  85.2 8.0 %collective-permute-start.14 = (bf16[2,768,128]{2,1,0:T(8,128)(2,1)S(1)}, bf16[2,768,128]{2,1,0:T(8,128)(2,1)S(1)}, u32[]{:S(2)}, u32[]{:S(2)}) collective-permute-start(bf16[2,768,128]{2,1,0:T(8,128)(2,1)S(1)} %get-tuple-element.78), channel_id=1, source_target_pairs={{0,3},{1,2},{2,1},{3,0},{8,9},{9,8},{10,11},{11,10},{4,7},{5,6},{6... | collective-permute-start | bytes 1179656 | tf_op jit(solution)/shard_map/ppermute | solution.py:47
  85.3 7.9 %collective-permute-start.15 = (bf16[768,128]{1,0:T(8,128)(2,1)S(1)}, bf16[768,128]{1,0:T(8,128)(2,1)S(1)}, u32[]{:S(2)}, u32[]{:S(2)}) collective-permute-start(bf16[768,128]{1,0:T(8,128)(2,1)S(1)} %shard_map.27), channel_id=1, source_target_pairs={{0,4},{4,0},{1,5},{5,1},{2,6},{6,2},{3,7},{7,3},{8,12},{12,8},{9,1... | collective-permute-start | bytes 589832 | tf_op jit(solution)/shard_map/ppermute | solution.py:27
  93.3 6.3 %collective-permute-start.16 = (bf16[768,128]{1,0:T(8,128)(2,1)S(1)}, bf16[768,128]{1,0:T(8,128)(2,1)S(1)}, u32[]{:S(2)}, u32[]{:S(2)}) collective-permute-start(bf16[768,128]{1,0:T(8,128)(2,1)S(1)} %shard_map.28), channel_id=1, source_target_pairs={{0,4},{4,0},{1,5},{5,1},{2,6},{6,2},{3,7},{7,3},{8,12},{12,8},{9,1... | collective-permute-start | bytes 589832 | tf_op jit(solution)/shard_map/ppermute | solution.py:27
  99.8 13.6 %collective-permute-start.19 = (bf16[768,384]{1,0:T(8,128)(2,1)S(1)}, bf16[768,384]{1,0:T(8,128)(2,1)S(1)}, u32[]{:S(2)}, u32[]{:S(2)}) collective-permute-start(bf16[768,384]{1,0:T(8,128)(2,1)S(1)} %shard_map.29.refs_0_), channel_id=1, source_target_pairs={{0,4},{4,0},{1,5},{5,1},{2,6},{6,2},{3,7},{7,3},{8,12},{12,8},{9,1... | collective-permute-start | bytes 1769480 | tf_op jit(solution)/shard_map/ppermute | solution.py:27
  102.5 17.2 %collective-permute-start.18 = (bf16[768,384]{1,0:T(8,128)(2,1)S(1)}, bf16[768,384]{1,0:T(8,128)(2,1)S(1)}, u32[]{:S(2)}, u32[]{:S(2)}) collective-permute-start(bf16[768,384]{1,0:T(8,128)(2,1)S(1)} %shard_map.29.refs_0_), channel_id=1, source_target_pairs={{0,3},{1,2},{2,1},{3,0},{4,7},{5,6},{6,5},{7,4},{8,11},{9,10},{10,... | collective-permute-start | bytes 1769480 | tf_op jit(solution)/shard_map/ppermute | solution.py:39
  107.5 13.5 %collective-permute-start.17 = (bf16[768,384]{1,0:T(8,128)(2,1)S(1)}, bf16[768,384]{1,0:T(8,128)(2,1)S(1)}, u32[]{:S(2)}, u32[]{:S(2)}) collective-permute-start(bf16[768,384]{1,0:T(8,128)(2,1)S(1)} %shard_map.29.refs_0_), channel_id=1, source_target_pairs={{0,1},{1,0},{2,3},{3,2},{4,5},{5,4},{6,7},{7,6},{8,9},{9,8},{10,11... | collective-permute-start | bytes 1769480 | tf_op jit(solution)/shard_map/ppermute | solution.py:35
  121.0 13.8 %collective-permute-start.22 = (bf16[768,384]{1,0:T(8,128)(2,1)S(1)}, bf16[768,384]{1,0:T(8,128)(2,1)S(1)}, u32[]{:S(2)}, u32[]{:S(2)}) collective-permute-start(bf16[768,384]{1,0:T(8,128)(2,1)S(1)} %collective-permute-done.19.refs_3_), channel_id=1, source_target_pairs={{0,3},{1,2},{2,1},{3,0},{4,7},{5,6},{6,5},{7,4},{8,11},{9,10},{10,... | collective-permute-start | bytes 1769480 | tf_op jit(solution)/shard_map/ppermute | solution.py:39
  122.5 12.6 %collective-permute-start.21 = (bf16[768,384]{1,0:T(8,128)(2,1)S(1)}, bf16[768,384]{1,0:T(8,128)(2,1)S(1)}, u32[]{:S(2)}, u32[]{:S(2)}) collective-permute-start(bf16[768,384]{1,0:T(8,128)(2,1)S(1)} %collective-permute-done.19.refs_3_), channel_id=1, source_target_pairs={{0,1},{1,0},{2,3},{3,2},{4,5},{5,4},{6,7},{7,6},{8,9},{9,8},{10,11... | collective-permute-start | bytes 1769480 | tf_op jit(solution)/shard_map/ppermute | solution.py:35
  122.5 24.9 %collective-permute-start.20 = (bf16[768,384]{1,0:T(8,128)(2,1)S(1)}, bf16[768,384]{1,0:T(8,128)(2,1)S(1)}, u32[]{:S(2)}, u32[]{:S(2)}) collective-permute-start(bf16[768,384]{1,0:T(8,128)(2,1)S(1)} %collective-permute-done.17.refs_1_), channel_id=1, source_target_pairs={{0,3},{1,2},{2,1},{3,0},{4,7},{5,6},{6,5},{7,4},{8,11},{9,10},{10,... | collective-permute-start | bytes 1769480 | tf_op jit(solution)/shard_map/ppermute | solution.py:39
  135.0 12.4 %collective-permute-start.23 = (bf16[768,384]{1,0:T(8,128)(2,1)S(1)}, bf16[768,384]{1,0:T(8,128)(2,1)S(1)}, u32[]{:S(2)}, u32[]{:S(2)}) collective-permute-start(bf16[768,384]{1,0:T(8,128)(2,1)S(1)} %collective-permute-done.22.refs_1_.refs_5_), channel_id=1, source_target_pairs={{0,1},{1,0},{2,3},{3,2},{4,5},{5,4},{6,7},{7,6},{8,9},{9,8},{10,11... | collective-permute-start | bytes 1769480 | tf_op jit(solution)/shard_map/ppermute | solution.py:35
  149.4 5.8 %collective-permute-start.24 = (bf16[384,1152]{1,0:T(8,128)(2,1)S(1)}, bf16[384,1152]{1,0:T(8,128)(2,1)S(1)}, u32[]{:S(2)}, u32[]{:S(2)}) collective-permute-start(bf16[384,1152]{1,0:T(8,128)(2,1)S(1)} %shard_map.32), channel_id=1, source_target_pairs={{0,8},{8,0},{1,9},{9,1},{2,10},{10,2},{3,11},{11,3},{4,12},{12,4},... | collective-permute-start | bytes 2654216 | tf_op jit(solution)/shard_map/ppermute | solution.py:31
  155.5 21.2 %collective-permute-start.27 = (bf16[384,1152]{1,0:T(8,128)(2,1)S(1)}, bf16[384,1152]{1,0:T(8,128)(2,1)S(1)}, u32[]{:S(2)}, u32[]{:S(2)}) collective-permute-start(bf16[384,1152]{1,0:T(8,128)(2,1)S(1)} %get-tuple-element.94.refs_0_), channel_id=1, source_target_pairs={{0,48},{8,24},{16,0},{24,40},{32,16},{40,56},{48,32},{56,8},{1,49}... | collective-permute-start | bytes 2654216 | tf_op jit(solution)/shard_map/ppermute | solution.py:56
  155.6 21.2 %collective-permute-start.26 = (bf16[384,1152]{1,0:T(8,128)(2,1)S(1)}, bf16[384,1152]{1,0:T(8,128)(2,1)S(1)}, u32[]{:S(2)}, u32[]{:S(2)}) collective-permute-start(bf16[384,1152]{1,0:T(8,128)(2,1)S(1)} %get-tuple-element.94.refs_0_), channel_id=1, source_target_pairs={{0,64},{64,0},{1,65},{65,1},{2,66},{66,2},{3,67},{67,3},{4,68},{68... | collective-permute-start | bytes 2654216 | tf_op jit(solution)/shard_map/ppermute | solution.py:23
  156.3 21.5 %collective-permute-start.25 = (bf16[384,1152]{1,0:T(8,128)(2,1)S(1)}, bf16[384,1152]{1,0:T(8,128)(2,1)S(1)}, u32[]{:S(2)}, u32[]{:S(2)}) collective-permute-start(bf16[384,1152]{1,0:T(8,128)(2,1)S(1)} %get-tuple-element.94.refs_0_), channel_id=1, source_target_pairs={{0,16},{8,56},{16,32},{24,8},{32,48},{40,24},{48,0},{56,40},{1,17}... | collective-permute-start | bytes 2654216 | tf_op jit(solution)/shard_map/ppermute | solution.py:56
  177.8 12.2 %collective-permute-start.28 = (bf16[384,1152]{1,0:T(8,128)(2,1)S(1)}, bf16[384,1152]{1,0:T(8,128)(2,1)S(1)}, u32[]{:S(2)}, u32[]{:S(2)}) collective-permute-start(bf16[384,1152]{1,0:T(8,128)(2,1)S(1)} %collective-permute-done.26.refs_2_), channel_id=1, source_target_pairs={{0,16},{8,56},{16,32},{24,8},{32,48},{40,24},{48,0},{56,40},{1,17}... | collective-permute-start | bytes 2654216 | tf_op jit(solution)/shard_map/ppermute | solution.py:56
  178.5 21.0 %collective-permute-start.29 = (bf16[384,1152]{1,0:T(8,128)(2,1)S(1)}, bf16[384,1152]{1,0:T(8,128)(2,1)S(1)}, u32[]{:S(2)}, u32[]{:S(2)}) collective-permute-start(bf16[384,1152]{1,0:T(8,128)(2,1)S(1)} %collective-permute-done.25.refs_1_), channel_id=1, source_target_pairs={{0,16},{8,56},{16,32},{24,8},{32,48},{40,24},{48,0},{56,40},{1,17}... | collective-permute-start | bytes 2654216 | tf_op jit(solution)/shard_map/ppermute | solution.py:56
  178.5 21.0 %collective-permute-start.30 = (bf16[384,1152]{1,0:T(8,128)(2,1)S(1)}, bf16[384,1152]{1,0:T(8,128)(2,1)S(1)}, u32[]{:S(2)}, u32[]{:S(2)}) collective-permute-start(bf16[384,1152]{1,0:T(8,128)(2,1)S(1)} %collective-permute-done.27.refs_3_), channel_id=1, source_target_pairs={{0,64},{64,0},{1,65},{65,1},{2,66},{66,2},{3,67},{67,3},{4,68},{68... | collective-permute-start | bytes 2654216 | tf_op jit(solution)/shard_map/ppermute | solution.py:23
  199.5 12.8 %collective-permute-start.31 = (bf16[384,1152]{1,0:T(8,128)(2,1)S(1)}, bf16[384,1152]{1,0:T(8,128)(2,1)S(1)}, u32[]{:S(2)}, u32[]{:S(2)}) collective-permute-start(bf16[384,1152]{1,0:T(8,128)(2,1)S(1)} %collective-permute-done.28.refs_2_), channel_id=1, source_target_pairs={{0,16},{8,56},{16,32},{24,8},{32,48},{40,24},{48,0},{56,40},{1,17}... | collective-permute-start | bytes 2654216 | tf_op jit(solution)/shard_map/ppermute | solution.py:56
  213.2 6.6 %collective-permute-start.32 = (bf16[384,1152]{1,0:T(8,128)(2,1)S(1)}, bf16[384,1152]{1,0:T(8,128)(2,1)S(1)}, u32[]{:S(2)}, u32[]{:S(2)}) collective-permute-start(bf16[384,1152]{1,0:T(8,128)(2,1)S(1)} %shard_map.38), channel_id=1, source_target_pairs={{0,8},{8,0},{1,9},{9,1},{2,10},{10,2},{3,11},{11,3},{4,12},{12,4},... | collective-permute-start | bytes 2654216 | tf_op jit(solution)/shard_map/ppermute | solution.py:31

commit v2 on v1

v2 whole, which is shorter than its diff:
```python
import jax
import jax.numpy as jnp
from jax import lax
from jax.experimental import pallas as pl
from jax.experimental.pallas import tpu as pltpu
from jax.sharding import Mesh, PartitionSpec as P

N = 9216

lead_coef = 3.4445
square_coef = -4.775
quart_coef = 2.0315

AXES = ("zl", "y", "c", "zh", "x")
SIZES = (2, 4, 2, 2, 4)
ROW = ("zl", "y", "c")
COL = ("zh", "x")
f32 = jnp.float32
bf16 = jnp.bfloat16
VMEM_LIMIT = 36 * 2**20

def swap_zl(v):
    return lax.ppermute(v, "zl", [(0, 1), (1, 0)])


def swap_zh(v):
    return lax.ppermute(v, "zh", [(0, 1), (1, 0)])


def swap_core(v):
    return lax.ppermute(v, "c", [(0, 1), (1, 0)])


def swap_x1(v):
    return lax.ppermute(v, "x", [(i, i ^ 1) for i in range(4)])


def swap_x3(v):
    return lax.ppermute(v, "x", [(i, i ^ 3) for i in range(4)])


def partner(v, first):
    pairs = []
    for c in range(2):
        by = 1 if (c == 0) == first else 3
        pairs += [(c * 4 + x, c * 4 + (x ^ by)) for x in range(4)]
    return lax.ppermute(v, ("c", "x"), pairs)


def along_y(v, first=True):
    pairs = []
    for y in range(4):
        for c in range(2):
            by = 1 if (c == 0) == first else -1
            pairs.append((y * 2 + c, (y + by) % 4 * 2 + c))
    return lax.ppermute(v, ("y", "c"), pairs)


def together(*values):
    return lax.optimization_barrier(values)


EARLY = ((0, "v"), (0, "r0"), (1, "v"), (0, "r1"))
MIDDLE = ((0, "f"), (1, "r0"), (1, "r1"))
LATE = ((1, "f"),)
ARRIVAL = EARLY + MIDDLE + LATE


VM = pl.BlockSpec(memory_space=pltpu.VMEM)
SM = pl.BlockSpec(memory_space=pltpu.SMEM)
HBM = pl.BlockSpec(memory_space=pltpu.HBM)


def call(kernel, out_shape, in_specs, scratch, *args):
    outs = jax.tree.map(lambda _: VM, out_shape)
    return pl.pallas_call(
        kernel,
        out_shape=out_shape,
        in_specs=in_specs,
        out_specs=outs,
        scratch_shapes=scratch,
        cost_estimate=pl.CostEstimate(flops=0, bytes_accessed=0, transcendentals=0),
        compiler_params=pltpu.CompilerParams(vmem_limit_bytes=VMEM_LIMIT),
    )(*args)


def place_of(where_ref, d, h):
    return jnp.bitwise_xor(where_ref[0], d) * 2 + jnp.bitwise_xor(where_ref[1], h)


def start_copies(copies, refs, panel, sems):
    started = []
    for i, (ref, src, dst, rows) in enumerate(copies):
        copy = pltpu.make_async_copy(refs[ref].at[pl.ds(src, rows)], panel.at[pl.ds(dst, rows)], sems.at[i])
        copy.start()
        started.append(copy)
    return started


def terms_of(where, own, sibling, arrays, send):
    rows, depth = own.shape
    eighth = rows // 8
    count = len(arrays)
    copies = [(i, 0, i * rows, rows) for i in range(count)]

    def kernel(where_ref, own_ref, sib_ref, *refs):
        refs, out, panel, sems = refs[:-3], refs[-3], refs[-2], refs[-1]
        for copy in start_copies(copies, refs, panel, sems):
            copy.wait()
        parts = []
        for d in (where_ref[2], 2) if send else (0, where_ref[3]):
            x = jnp.bitwise_xor(where_ref[0], d)
            for p in range(count):
                first = pl.multiple_of(p * rows + x * 2 * eighth, 2 * eighth)
                parts.append(panel[pl.ds(first, 2 * eighth)])
        left = jnp.concatenate(parts, axis=0)
        for i, right in enumerate((own_ref, sib_ref)):
            value = lax.dot_general(
                left, right[...], (((1,), (1,)), ((), ())), preferred_element_type=f32
            ).astype(out.dtype)
            for slot in range(2):
                for p in range(count):
                    for z in range(2):
                        first = ((slot * count + p) * 2 + z) * eighth
                        h = jnp.bitwise_xor(where_ref[1], z)
                        target = (slot, h, slice(p * eighth, (p + 1) * eighth), slice(i * rows, (i + 1) * rows))
                        out[target] = value[first : first + eighth]

    return call(
        kernel, jax.ShapeDtypeStruct((2, 2, count * eighth, 2 * rows), bf16 if send else f32),
        [SM, VM, VM] + [HBM] * count,
        [pltpu.VMEM((count * rows, depth), bf16), pltpu.SemaphoreType.DMA((count,))],
        where, own, sibling, *arrays,
    )


def sum_pair(*pairs):
    sizes = [keep.shape[2] for keep, _ in pairs]
    flat = [a for pair in pairs for a in pair]

    def kernel(*refs):
        mine, other = refs[-2:]
        first = 0
        for b, size in enumerate(sizes):
            k, g = refs[2 * b : 2 * b + 2]
            other[:, first : first + size] = (k[1] + g[1].astype(f32)).astype(bf16)
            mine[:, first : first + size] = k[0] + g[0].astype(f32)
            first += size

    shape = (2, sum(sizes), pairs[0][0].shape[3])
    out = [jax.ShapeDtypeStruct(shape, f32), jax.ShapeDtypeStruct(shape, bf16)]
    return call(kernel, out, [VM] * len(flat), [], *flat)


def sum_other(*pairs):
    sizes = [mine.shape[1] for mine, _ in pairs]
    flat = [a for pair in pairs for a in pair]

    def kernel(*refs):
        first = 0
        for b, size in enumerate(sizes):
            refs[-1][first : first + size] = (refs[2 * b][1] + refs[2 * b + 1][1].astype(f32)).astype(bf16)
            first += size

    out = jax.ShapeDtypeStruct((sum(sizes), pairs[0][0].shape[2]), bf16)
    return call(kernel, out, [VM] * len(flat), [], *flat)


def finish(pairs, z_parts):
    sizes = [mine.shape[1] for mine, _ in pairs]
    rows = pairs[0][0].shape[2]
    flat = [a for pair in pairs for a in pair] + z_parts

    def kernel(*refs):
        values = []
        for b in range(len(sizes)):
            values.append(refs[2 * b][0] + refs[2 * b + 1][0].astype(f32))
        value = jnp.concatenate(values, axis=0)
        z_part = jnp.concatenate([ref[...] for ref in refs[2 * len(sizes) : -1]], axis=0)
        refs[-1][...] = ((value + z_part.astype(f32)) / N).T.astype(bf16)

    return call(kernel, jax.ShapeDtypeStruct((rows, sum(sizes)), bf16), [VM] * len(flat), [], *flat)


def stack_blocks(arrays):
    shape = (len(arrays),) + arrays[0].shape

    def kernel(*refs):
        refs, out, held, sems, out_sems = refs[:-4], refs[-4], refs[-3], refs[-2], refs[-1]
        started, leaving = [], []
        for i, ref in enumerate(refs):
            started.append(pltpu.make_async_copy(ref, held.at[i], sems.at[i]))
            started[-1].start()
        for i, copy in enumerate(started):
            copy.wait()
            leaving.append(pltpu.make_async_copy(held.at[i], out.at[i], out_sems.at[i]))
            leaving[-1].start()
        for copy in leaving:
            copy.wait()

    return pl.pallas_call(
        kernel,
        out_shape=jax.ShapeDtypeStruct(shape, bf16),
        in_specs=[HBM] * len(arrays),
        out_specs=HBM,
        scratch_shapes=[
            pltpu.VMEM(shape, bf16),
            pltpu.SemaphoreType.DMA((len(arrays),)),
            pltpu.SemaphoreType.DMA((len(arrays),)),
        ],
        cost_estimate=pl.CostEstimate(flops=0, bytes_accessed=0, transcendentals=0),
        compiler_params=pltpu.CompilerParams(vmem_limit_bytes=VMEM_LIMIT),
    )(*arrays)


def times_x(where, full, panel, total, half, dtype):
    spots = list(full)
    both, depth = full[spots[0]].shape
    blocks, block, cols = panel.shape
    eighth = block // 8
    count = len(spots)
    extra = [] if total is None else [total]
    part = slice(0, both) if half is None else slice(half * both // 2, (half + 1) * both // 2)
    rows = part.stop - part.start

    def kernel(where_ref, *refs):
        slices, panel_ref, refs = refs[:count], refs[count], refs[count + 1 :]
        out, held, sems = refs[-3:]
        started = []
        for i, spot in enumerate(spots):
            first = pl.multiple_of(place_of(where_ref, *spot) * eighth, eighth)
            copy = pltpu.make_async_copy(panel_ref.at[:, pl.ds(first, eighth)], held.at[i], sems.at[i])
            copy.start()
            started.append(copy)
        for i in range(0, count, 2):
            group = range(i, min(i + 2, count))
            for k in group:
                started[k].wait()
            left = jnp.concatenate([slices[k][part] for k in group], axis=1)
            right = held[i : i + len(group)].reshape(len(group) * depth, cols)
            value = jnp.dot(left, right, preferred_element_type=f32)
            if i > 0:
                value = out[...] + value
            elif extra:
                value = refs[0][part] + value
            out[...] = value.astype(dtype)

    return call(
        kernel, jax.ShapeDtypeStruct((rows, cols), dtype), [SM] + [VM] * count + [HBM] + [VM] * len(extra),
        [pltpu.VMEM((count, blocks, eighth, cols), bf16), pltpu.SemaphoreType.DMA((count,))],
        where, *[full[spot] for spot in spots], panel, *extra,
    )


def add_rounded(mine, got):
    def kernel(m, g, y, v):
        value = m[...] + g[...].astype(f32)
        y[...] = value
        v[...] = value.astype(bf16)

    out = [jax.ShapeDtypeStruct(mine.shape, f32), jax.ShapeDtypeStruct(mine.shape, bf16)]
    return call(kernel, out, [VM] * 2, [], mine, got)


def arrange(where, full):
    spots = list(full)
    both, depth = full[spots[0]].shape
    eighth = depth // 8

    def kernel(where_ref, *refs):
        out, held = refs[8:]
        for spot, part in zip(spots, refs[:8]):
            held[place_of(where_ref, *spot)] = part[...]
        for p in range(8):
            out[p] = jnp.concatenate([held[e, :, p * eighth : (p + 1) * eighth] for e in range(8)], axis=1)

    out = jax.ShapeDtypeStruct((8, both, depth), bf16)
    return call(
        kernel, out, [SM] + [VM] * 8, [pltpu.VMEM((8, both, depth), bf16)], where, *[full[spot] for spot in spots]
    )


def times_y(gram, arrays, first, total, half, dtype):
    _, both, depth = gram.shape
    cols = arrays[0].shape[1]
    copies = [(i, 0, i * depth, depth) for i in range(len(arrays))]
    extra = [] if total is None else [total]
    halves = (0, 1) if half is None else (half,)
    rows = both // 2

    def kernel(gram_ref, *refs):
        ys = refs[len(extra) : len(extra) + len(arrays)]
        out, panel, sems = refs[-3:]
        for copy in start_copies(copies, ys, panel, sems):
            copy.wait()
        for i, one in enumerate(halves):
            part = slice(one * rows, (one + 1) * rows)
            left = jnp.concatenate([gram_ref[first + p, part] for p in range(len(arrays))], axis=1)
            value = jnp.dot(left, panel[...], preferred_element_type=f32)
            if extra:
                value = refs[0][part] + value
            out[i * rows : (i + 1) * rows] = value.astype(dtype)

    return call(
        kernel, jax.ShapeDtypeStruct((rows * len(halves), cols), dtype), [VM] * (1 + len(extra)) + [HBM] * len(arrays),
        [pltpu.VMEM((len(arrays) * depth, cols), bf16), pltpu.SemaphoreType.DMA((len(arrays),))],
        gram, *extra, *arrays,
    )


def result(own, y, mine, got):
    def kernel(own_ref, y_ref, m, g, out):
        square = m[...] + g[...].astype(f32)
        out[...] = (lead_coef * own_ref[...].astype(f32) + square_coef * y_ref[...] + quart_coef * square).astype(bf16)

    return call(kernel, jax.ShapeDtypeStruct(own.shape, bf16), [VM] * 4, [], own, y, mine, got)


def local(own):
    core = lax.axis_index("c")
    where = jnp.stack([lax.axis_index("x"), lax.axis_index("zh"), 1 + 2 * core, 3 - 2 * core]).astype(jnp.int32)
    x = {}

    def terms(keys, send):
        return terms_of(where, own, w, [x[key] for key in keys], send)

    z = swap_zl(own)
    r0 = along_y(own)
    r1 = along_y(own, False)
    w = swap_core(own)
    r0, w, z, r1 = together(r0, w, z, r1)
    x[0, "v"], x[0, "r0"], x[1, "v"], x[0, "r1"] = own, r0, z, r1
    rz1 = swap_zl(r1)
    rz0 = along_y(z)
    f = along_y(r1, False)
    got1 = partner(terms(EARLY, True), True)
    keep1 = terms(EARLY, False)
    rz0, f, rz1, keep1 = together(rz0, f, rz1, keep1)
    x[0, "f"], x[1, "r0"], x[1, "r1"] = f, rz0, rz1
    fz = along_y(rz0)
    send2 = terms(MIDDLE, True)
    got2 = partner(send2, True)
    keep2 = terms(MIDDLE, False)
    fz, keep2, got1 = together(fz, keep2, got1)
    x[1, "f"] = fz
    got3 = partner(terms(LATE, True), True)
    mine1, other1 = sum_pair((keep1, got1))
    last1 = partner(other1, False)
    keep3 = terms(LATE, False)
    got2, keep3, got3, last1 = together(got2, keep3, got3, last1)
    mine2, other2 = sum_pair((keep2, got2), (keep3, got3))
    z1 = swap_zh(sum_other((mine1, last1)))
    last2 = partner(other2, False)
    last2, z1 = together(last2, z1)
    z2 = swap_zh(sum_other((mine2, last2)))
    mine = finish([(mine1, last1), (mine2, last2)], [z1, z2])
    b0 = swap_zh(mine)
    a1 = swap_x1(mine)
    a3 = swap_x3(mine)
    panel = stack_blocks([x[key] for key in ARRIVAL])
    a1, a3, b0, panel = together(a1, a3, b0, panel)
    b3 = swap_x3(b0)
    b1 = swap_x1(b0)
    a2 = swap_x3(a1)
    near = {(0, 0): mine, (1, 0): a1, (3, 0): a3, (0, 1): b0}
    part = times_x(where, near, panel, None, None, f32)
    b1, b3, part = together(b1, b3, part)
    b2 = swap_x1(b3)
    next_ones = {(1, 1): b1, (3, 1): b3}
    part = times_x(where, next_ones, panel, part, None, f32)
    a2, b2, part = together(a2, b2, part)
    late = {(2, 0): a2, (2, 1): b2}
    give = times_x(where, late, panel, part, 1, bf16)
    got = swap_core(give)
    y = times_x(where, late, panel, part, 0, f32)
    got, y = together(got, y)
    y, v = add_rounded(y, got)

    def add(total, keys, half=None, dtype=f32):
        return times_y(gram, [u[key] for key in keys], ARRIVAL.index(keys[0]), total, half, dtype)

    u = {}
    z = swap_zl(v)
    r0 = along_y(v)
    r1 = along_y(v, False)
    gram = arrange(where, near | next_ones | late)
    r0, z, r1, gram = together(r0, z, r1, gram)
    u[0, "v"], u[0, "r0"], u[1, "v"], u[0, "r1"] = v, r0, z, r1
    rz1 = swap_zl(r1)
    rz0 = along_y(z)
    f = along_y(r1, False)
    total = add(None, EARLY)
    rz0, f, rz1, total = together(rz0, f, rz1, total)
    u[0, "f"], u[1, "r0"], u[1, "r1"] = f, rz0, rz1
    fz = along_y(rz0)
    total = add(total, MIDDLE)
    fz, total = together(fz, total)
    u[1, "f"] = fz
    got = swap_core(add(total, LATE, 1, bf16))
    mine = add(total, LATE, 0)
    got, mine = together(got, mine)
    return result(own, y, mine, got)


def solution(mesh):
    fine = Mesh(mesh.devices.reshape(SIZES), AXES)
    spec = P(ROW, COL)
    return jax.shard_map(local, mesh=fine, in_specs=(spec,), out_specs=spec, check_vma=False)
```

time: 221 us -> 213 us (0.964)
  waiting for transfers between devices: 124 us -> 99.4 us
  starting transfers between devices: 56.7 us -> 64.7 us
  Pallas kernels: 39.5 us -> 47.4 us
    ppermute x6 -> x5, waiting for transfers between devices: 18.6 us -> 7.06 us  [partner(): return lax.ppermute(v, ('c', 'x'), pairs)]
    ppermute x3, waiting for transfers between devices: 21.3 us -> 10.2 us  [swap_x3(): return lax.ppermute(v, 'x', [(i, i ^ 3) for i in range(4)])]
    ppermute x4 -> x3, waiting for transfers between devices: 15.9 us -> 8.28 us  [swap_zh(): return lax.ppermute(v, 'zh', [(0, 1), (1, 0)])]
    ppermute x4, waiting for transfers between devices: 6.49 us -> 13.1 us  [swap_zl(): return lax.ppermute(v, 'zl', [(0, 1), (1, 0)])]
    ppermute x3, starting transfers between devices: 0.16 us -> 6.73 us  [swap_x1(): return lax.ppermute(v, 'x', [(i, i ^ 1) for i in range(4)])]
    ppermute x10, waiting for transfers between devices: 58.6 us -> 52.6 us  [along_y(): return lax.ppermute(v, ('y', 'c'), pairs)]
    ppermute x3, waiting for transfers between devices: 1.49 us -> 6.54 us  [swap_x1(): return lax.ppermute(v, 'x', [(i, i ^ 1) for i in range(4)])]
    pallas_call x24 -> x22, Pallas kernels: 39.5 us -> 44.4 us  [call(): pl.pallas_call(kernel, out_shape=out_shape, in_specs=in_specs, out_specs=...]
  transfers between devices with their start and end apart: 33 -> 31, of which waited for: 26 -> 25; matrix products, arithmetic and copies ran while one was open for 0% -> 0% of each run, Pallas kernels for 16% -> 20%
where the time goes in v2:
time: 213 us
  waiting for transfers between devices  99.4 us (47%)
  starting transfers between devices  64.7 us (30%)
  Pallas kernels  47.4 us (22%)
    ppermute x10, waiting for transfers between devices, along_y(): return lax.ppermute(v, ('y', 'c'), pairs)  52.6 us
    pallas_call x22, Pallas kernels, call(): pl.pallas_call(kernel, out_shape=out_shape, in_specs=in_specs, out_specs=...  44.4 us
    ppermute x10, starting transfers between devices, along_y(): return lax.ppermute(v, ('y', 'c'), pairs)  14.7 us
    ppermute x3, starting transfers between devices, swap_core(): return lax.ppermute(v, 'c', [(0, 1), (1, 0)])  14 us
    ppermute x4, waiting for transfers between devices, swap_zl(): return lax.ppermute(v, 'zl', [(0, 1), (1, 0)])  13.1 us
    ppermute x3, starting transfers between devices, swap_zh(): return lax.ppermute(v, 'zh', [(0, 1), (1, 0)])  10.3 us
    ppermute x3, waiting for transfers between devices, swap_x3(): return lax.ppermute(v, 'x', [(i, i ^ 3) for i in range(4)])  10.2 us
    ppermute x5, starting transfers between devices, partner(): return lax.ppermute(v, ('c', 'x'), pairs)  9.7 us
  transfers between devices with their start and end apart: 31, of which 25 were waited for; matrix products, arithmetic and copies ran while one was open for 0% of the time, Pallas kernels for 20%

profile of v2, /device:TPU:1, one launch (start us, length us, event | category | flops | bytes accessed | tf_op | source)
XLA Modules:
  0.0 212.9 jit_solution(13051186158260864064)
XLA Ops:
  0.0 2.1 collective-permute-start.3
  2.1 1.6 collective-permute-start.2
  3.8 2.7 %collective-permute-start.1 = (bf16[384,1152]{1,0:T(8,128)(2,1)}, bf16[384,1152]{1,0:T(8,128)(2,1)S(1)}, u32[]{:S(2)}, u32[]{:S(2)}) collective-permute-start(bf16[384,1152]{1,0:T(8,128)(2,1)} %own_ref.13), channel_id=1, source_target_pairs={{0,8},{8,0},{1,9},{9,1},{2,10},{10,2},{3,11},{11,3},{4,12},{12,4},... | collective-permute-start | bytes 2654216 | tf_op jit(solution)/shard_map/ppermute | solution.py:31
  6.9 11.0 %collective-permute-done.3.refs_3_ = bf16[384,1152]{1,0:T(8,128)(2,1)S(1)} collective-permute-done((bf16[384,1152]{1,0:T(8,128)(2,1)}, bf16[384,1152]{1,0:T(8,128)(2,1)S(1)}, u32[]{:S(2)}, u32[]{:S(2)}) %collective-permute-start.3) | collective-permute-done | bytes 884768 | tf_op jit(solution)/shard_map/ppermute | solution.py:56
  17.9 3.6 %collective-permute-done.2.refs_2_ = bf16[384,1152]{1,0:T(8,128)(2,1)S(1)} collective-permute-done((bf16[384,1152]{1,0:T(8,128)(2,1)}, bf16[384,1152]{1,0:T(8,128)(2,1)S(1)}, u32[]{:S(2)}, u32[]{:S(2)}) %collective-permute-start.2) | collective-permute-done | bytes 884768 | tf_op jit(solution)/shard_map/ppermute | solution.py:23
  21.5 3.0 %collective-permute-done.refs_1_ = bf16[384,1152]{1,0:T(8,128)(2,1)S(1)} collective-permute-done((bf16[384,1152]{1,0:T(8,128)(2,1)}, bf16[384,1152]{1,0:T(8,128)(2,1)S(1)}, u32[]{:S(2)}, u32[]{:S(2)}) %collective-permute-start) | collective-permute-done | bytes 884768 | tf_op jit(solution)/shard_map/ppermute | solution.py:56
  24.5 3.0 %collective-permute-start.4 = (bf16[384,1152]{1,0:T(8,128)(2,1)S(1)}, bf16[384,1152]{1,0:T(8,128)(2,1)}, u32[]{:S(2)}, u32[]{:S(2)}) collective-permute-start(bf16[384,1152]{1,0:T(8,128)(2,1)S(1)} %collective-permute-done.2.refs_2_), channel_id=1, source_target_pairs={{0,16},{8,56},{16,32},{24,8},{32,48},{40,24},{48,0},{56,40},{1,17}... | collective-permute-start | bytes 2654216 | tf_op jit(solution)/shard_map/ppermute | solution.py:56
  30.4 3.4 %shard_map.19 = bf16[2,2,192,768]{3,2,1,0:T(8,128)(2,1)S(1)} custom-call(s32[4]{0:T(128)S(1)} %pad_add_fusion.where_ref, bf16[384,1152]{1,0:T(8,128)(2,1)S(1)} %copy-done, bf16[384,1152]{1,0:T(8,128)(2,1)S(1)} %collective-permute-done.1.sib_ref, bf16[384,1152]{1,0:T(8,128)(2,1)S(1)} %copy-done, bf16[384,1152]{1,0:T(8,128)(2,1)S(1)} %collective-permute-done.refs_1_, ...), custom_call_target="tpu_custom_call" | custom-call | tf_op jit(solution)/shard_map/pallas_call | solution.py:76
  33.8 2.5 %collective-permute-start.8 = (bf16[2,2,192,768]{3,2,1,0:T(8,128)(2,1)S(1)}, bf16[2,2,192,768]{3,2,1,0:T(8,128)(2,1)S(1)}, u32[]{:S(2)}, u32[]{:S(2)}) collective-permute-start(bf16[2,2,192,768]{3,2,1,0:T(8,128)(2,1)S(1)} %shard_map.19), channel_id=1, source_target_pairs={{0,1},{1,0},{2,3},{3,2},{8,11},{9,10},{10,9},{11,8},{4,5},{5,4},{6... | collective-permute-start | bytes 3538952 | tf_op jit(solution)/shard_map/ppermute | solution.py:47
  36.4 3.4 %shard_map.17.refs_0_ = f32[2,2,192,768]{3,2,1,0:T(8,128)S(1)} custom-call(s32[4]{0:T(128)S(1)} %pad_add_fusion.where_ref, bf16[384,1152]{1,0:T(8,128)(2,1)S(1)} %copy-done.1, bf16[384,1152]{1,0:T(8,128)(2,1)S(1)} %collective-permute-done.1.sib_ref, bf16[384,1152]{1,0:T(8,128)(2,1)S(1)} %copy-done.1, bf16[384,1152]{1,0:T(8,128)(2,1)S(1)} %collective-permute-done.refs_1_, ...), custom_call_target="tpu_custom_call" | custom-call | tf_op jit(solution)/shard_map/pallas_call | solution.py:76
  39.8 4.2 %collective-permute-done.4.refs_1_.refs_5_ = bf16[384,1152]{1,0:T(8,128)(2,1)} collective-permute-done((bf16[384,1152]{1,0:T(8,128)(2,1)S(1)}, bf16[384,1152]{1,0:T(8,128)(2,1)}, u32[]{:S(2)}, u32[]{:S(2)}) %collective-permute-start.4) | collective-permute-done | bytes 884768 | tf_op jit(solution)/shard_map/ppermute | solution.py:56
  44.0 4.4 %collective-permute-done.6.refs_2_.refs_6_ = bf16[384,1152]{1,0:T(8,128)(2,1)} collective-permute-done((bf16[384,1152]{1,0:T(8,128)(2,1)S(1)}, bf16[384,1152]{1,0:T(8,128)(2,1)}, u32[]{:S(2)}, u32[]{:S(2)}) %collective-permute-start.6) | collective-permute-done | bytes 884768 | tf_op jit(solution)/shard_map/ppermute | solution.py:23
  48.8 3.9 %shard_map.21 = bf16[2,2,144,768]{3,2,1,0:T(8,128)(2,1)S(1)} custom-call(s32[4]{0:T(128)S(1)} %pad_add_fusion.where_ref, bf16[384,1152]{1,0:T(8,128)(2,1)S(1)} %copy-done.1, bf16[384,1152]{1,0:T(8,128)(2,1)S(1)} %collective-permute-done.1.sib_ref, bf16[384,1152]{1,0:T(8,128)(2,1)} %collective-permute-done.5.refs_0_.refs_4_, ...), custom_call_target="tpu_custom_call" | custom-call | tf_op jit(solution)/shard_map/pallas_call | solution.py:76
  52.7 2.6 %collective-permute-start.9 = (bf16[2,2,144,768]{3,2,1,0:T(8,128)(2,1)S(1)}, bf16[2,2,144,768]{3,2,1,0:T(8,128)(2,1)S(1)}, u32[]{:S(2)}, u32[]{:S(2)}) collective-permute-start(bf16[2,2,144,768]{3,2,1,0:T(8,128)(2,1)S(1)} %shard_map.21), channel_id=1, source_target_pairs={{0,1},{1,0},{2,3},{3,2},{8,11},{9,10},{10,9},{11,8},{4,5},{5,4},{6... | collective-permute-start | bytes 2654216 | tf_op jit(solution)/shard_map/ppermute | solution.py:47
  55.2 3.9 %shard_map.18.refs_0_ = f32[2,2,144,768]{3,2,1,0:T(8,128)S(1)} custom-call(s32[4]{0:T(128)S(1)} %pad_add_fusion.where_ref, bf16[384,1152]{1,0:T(8,128)(2,1)S(1)} %copy-done.1, bf16[384,1152]{1,0:T(8,128)(2,1)S(1)} %collective-permute-done.1.sib_ref, bf16[384,1152]{1,0:T(8,128)(2,1)} %collective-permute-done.5.refs_0_.refs_4_, ...), custom_call_target="tpu_custom_call" | custom-call | tf_op jit(solution)/shard_map/pallas_call | solution.py:76
  63.7 1.9 collective-permute-start.10
  67.1 6.9 %collective-permute-done.10.refs_3_ = bf16[2,2,48,768]{3,2,1,0:T(8,128)(2,1)S(1)} collective-permute-done((bf16[2,2,48,768]{3,2,1,0:T(8,128)(2,1)S(1)}, bf16[2,2,48,768]{3,2,1,0:T(8,128)(2,1)S(1)}, u32[]{:S(2)}, u32[]{:S(2)}) %collective-permute-start.10) | collective-permute-done | bytes 294944 | tf_op jit(solution)/shard_map/ppermute | solution.py:47
  75.7 3.3 %collective-permute-start.13 = (bf16[192,768]{1,0:T(8,128)(2,1)S(1)}, bf16[192,768]{1,0:T(8,128)(2,1)S(1)}, u32[]{:S(2)}, u32[]{:S(2)}) collective-permute-start(bf16[192,768]{1,0:T(8,128)(2,1)S(1)} %shard_map.25), channel_id=1, source_target_pairs={{0,4},{4,0},{1,5},{5,1},{2,6},{6,2},{3,7},{7,3},{8,12},{12,8},{9,1... | collective-permute-start | bytes 884744 | tf_op jit(solution)/shard_map/ppermute | solution.py:27
  79.0 4.1 %collective-permute-done.13.refs_4_ = bf16[192,768]{1,0:T(8,128)(2,1)S(1)} collective-permute-done((bf16[192,768]{1,0:T(8,128)(2,1)S(1)}, bf16[192,768]{1,0:T(8,128)(2,1)S(1)}, u32[]{:S(2)}, u32[]{:S(2)}) %collective-permute-start.13) | collective-permute-done | bytes 294944 | tf_op jit(solution)/shard_map/ppermute | solution.py:27
  83.4 3.4 %collective-permute-start.14 = (bf16[192,768]{1,0:T(8,128)(2,1)S(1)}, bf16[192,768]{1,0:T(8,128)(2,1)S(1)}, u32[]{:S(2)}, u32[]{:S(2)}) collective-permute-start(bf16[192,768]{1,0:T(8,128)(2,1)S(1)} %shard_map.26), channel_id=1, source_target_pairs={{0,4},{4,0},{1,5},{5,1},{2,6},{6,2},{3,7},{7,3},{8,12},{12,8},{9,1... | collective-permute-start | bytes 884744 | tf_op jit(solution)/shard_map/ppermute | solution.py:27
  86.8 4.2 %collective-permute-done.14.refs_5_ = bf16[192,768]{1,0:T(8,128)(2,1)S(1)} collective-permute-done((bf16[192,768]{1,0:T(8,128)(2,1)S(1)}, bf16[192,768]{1,0:T(8,128)(2,1)S(1)}, u32[]{:S(2)}, u32[]{:S(2)}) %collective-permute-start.14) | collective-permute-done | bytes 294944 | tf_op jit(solution)/shard_map/ppermute | solution.py:27
  91.3 3.5 %collective-permute-start.17 = (bf16[768,384]{1,0:T(8,128)(2,1)S(1)}, bf16[768,384]{1,0:T(8,128)(2,1)S(1)}, u32[]{:S(2)}, u32[]{:S(2)}) collective-permute-start(bf16[768,384]{1,0:T(8,128)(2,1)S(1)} %shard_map.27.refs_0_), channel_id=1, source_target_pairs={{0,4},{4,0},{1,5},{5,1},{2,6},{6,2},{3,7},{7,3},{8,12},{12,8},{9,1... | collective-permute-start | bytes 1769480 | tf_op jit(solution)/shard_map/ppermute | solution.py:27
  94.8 2.9 %collective-permute-start.16 = (bf16[768,384]{1,0:T(8,128)(2,1)S(1)}, bf16[768,384]{1,0:T(8,128)(2,1)S(1)}, u32[]{:S(2)}, u32[]{:S(2)}) collective-permute-start(bf16[768,384]{1,0:T(8,128)(2,1)S(1)} %shard_map.27.refs_0_), channel_id=1, source_target_pairs={{0,3},{1,2},{2,1},{3,0},{4,7},{5,6},{6,5},{7,4},{8,11},{9,10},{10,... | collective-permute-start | bytes 1769480 | tf_op jit(solution)/shard_map/ppermute | solution.py:39
  97.7 2.6 %collective-permute-start.15 = (bf16[768,384]{1,0:T(8,128)(2,1)S(1)}, bf16[768,384]{1,0:T(8,128)(2,1)S(1)}, u32[]{:S(2)}, u32[]{:S(2)}) collective-permute-start(bf16[768,384]{1,0:T(8,128)(2,1)S(1)} %shard_map.27.refs_0_), channel_id=1, source_target_pairs={{0,1},{1,0},{2,3},{3,2},{4,5},{5,4},{6,7},{7,6},{8,9},{9,8},{10,11... | collective-permute-start | bytes 1769480 | tf_op jit(solution)/shard_map/ppermute | solution.py:35
  100.4 2.9 %shard_map.28.refs_4_.refs_2_ = bf16[8,384,1152]{2,1,0:T(8,128)(2,1)S(1)} custom-call(bf16[384,1152]{1,0:T(8,128)(2,1)S(1)} %copy-done.1, bf16[384,1152]{1,0:T(8,128)(2,1)S(1)} %collective-permute-done.refs_1_, bf16[384,1152]{1,0:T(8,128)(2,1)S(1)} %collective-permute-done.2.refs_2_, bf16[384,1152]{1,0:T(8,128)(2,1)S(1)} %collective-permute-done.3.refs_3_, ...), custom_call_target="tpu_custom_call" | custom-call | tf_op jit(solution)/shard_map/pallas_call | solution.py:201
  103.3 2.0 collective-permute-done.16.refs_2_
  105.3 4.5 %collective-permute-done.15.refs_1_ = bf16[768,384]{1,0:T(8,128)(2,1)S(1)} collective-permute-done((bf16[768,384]{1,0:T(8,128)(2,1)S(1)}, bf16[768,384]{1,0:T(8,128)(2,1)S(1)}, u32[]{:S(2)}, u32[]{:S(2)}) %collective-permute-start.15) | collective-permute-done | bytes 589856 | tf_op jit(solution)/shard_map/ppermute | solution.py:35
  109.8 2.6 %collective-permute-start.19 = (bf16[768,384]{1,0:T(8,128)(2,1)S(1)}, bf16[768,384]{1,0:T(8,128)(2,1)S(1)}, u32[]{:S(2)}, u32[]{:S(2)}) collective-permute-start(bf16[768,384]{1,0:T(8,128)(2,1)S(1)} %collective-permute-done.17.refs_3_), channel_id=1, source_target_pairs={{0,1},{1,0},{2,3},{3,2},{4,5},{5,4},{6,7},{7,6},{8,9},{9,8},{10,11... | collective-permute-start | bytes 1769480 | tf_op jit(solution)/shard_map/ppermute | solution.py:35
  112.4 1.7 collective-permute-start.18
  114.1 4.9 %shard_map.29.refs_3_ = f32[768,1152]{1,0:T(8,128)S(1)} custom-call(s32[4]{0:T(128)S(1)} %pad_add_fusion.where_ref, bf16[768,384]{1,0:T(8,128)(2,1)S(1)} %shard_map.27.refs_0_, bf16[768,384]{1,0:T(8,128)(2,1)S(1)} %collective-permute-done.15.refs_1_, bf16[768,384]{1,0:T(8,128)(2,1)S(1)} %collective-permute-done.16.refs_2_, ...), custom_call_target="tpu_custom_call" | custom-call | tf_op jit(solution)/shard_map/pallas_call | solution.py:76
  120.5 1.9 collective-permute-done.19.refs_0_.refs_4_
  123.9 2.4 %shard_map.30.refs_3_ = f32[768,1152]{1,0:T(8,128)S(1)} custom-call(s32[4]{0:T(128)S(1)} %pad_add_fusion.where_ref, bf16[768,384]{1,0:T(8,128)(2,1)S(1)} %collective-permute-done.19.refs_0_.refs_4_, bf16[768,384]{1,0:T(8,128)(2,1)S(1)} %collective-permute-done.20.refs_1_.refs_5_, bf16[8,384,1152]{2,1,0:T(8,128)(2,1)S(1)} %shard_map.28.refs_4_.refs_2_, ...), custom_call_target="tpu_custom_call" | custom-call | tf_op jit(solution)/shard_map/pallas_call | solution.py:76
  126.4 6.8 %collective-permute-done.18.refs_0_.refs_6_ = bf16[768,384]{1,0:T(8,128)(2,1)S(1)} collective-permute-done((bf16[768,384]{1,0:T(8,128)(2,1)S(1)}, bf16[768,384]{1,0:T(8,128)(2,1)S(1)}, u32[]{:S(2)}, u32[]{:S(2)}) %collective-permute-start.18) | collective-permute-done | bytes 589856 | tf_op jit(solution)/shard_map/ppermute | solution.py:39
  133.2 1.7 shard_map.31
  134.9 9.4 %collective-permute-start.22 = (bf16[384,1152]{1,0:T(8,128)(2,1)S(1)}, bf16[384,1152]{1,0:T(8,128)(2,1)S(1)}, u32[]{:S(2)}, u32[]{:S(2)}) collective-permute-start(bf16[384,1152]{1,0:T(8,128)(2,1)S(1)} %shard_map.31), channel_id=1, source_target_pairs={{0,8},{8,0},{1,9},{9,1},{2,10},{10,2},{3,11},{11,3},{4,12},{12,4},... | collective-permute-start | bytes 2654216 | tf_op jit(solution)/shard_map/ppermute | solution.py:31
  144.4 1.7 shard_map.32.m
  146.7 2.4 %collective-permute-start.25 = (bf16[384,1152]{1,0:T(8,128)(2,1)S(1)}, bf16[384,1152]{1,0:T(8,128)(2,1)S(1)}, u32[]{:S(2)}, u32[]{:S(2)}) collective-permute-start(bf16[384,1152]{1,0:T(8,128)(2,1)S(1)} %get-tuple-element.86.refs_0_), channel_id=1, source_target_pairs={{0,48},{8,24},{16,0},{24,40},{32,16},{40,56},{48,32},{56,8},{1,49}... | collective-permute-start | bytes 2654216 | tf_op jit(solution)/shard_map/ppermute | solution.py:56
  151.1 4.6 %shard_map.34.gram_ref = bf16[8,768,384]{2,1,0:T(8,128)(2,1)S(1)} custom-call(s32[4]{0:T(128)S(1)} %pad_add_fusion.where_ref, bf16[768,384]{1,0:T(8,128)(2,1)S(1)} %shard_map.27.refs_0_, bf16[768,384]{1,0:T(8,128)(2,1)S(1)} %collective-permute-done.15.refs_1_, bf16[768,384]{1,0:T(8,128)(2,1)S(1)} %collective-permute-done.16.refs_2_, ...), custom_call_target="tpu_custom_call" | custom-call | tf_op jit(solution)/shard_map/pallas_call | solution.py:76
  155.7 10.1 %collective-permute-done.25.refs_3_ = bf16[384,1152]{1,0:T(8,128)(2,1)S(1)} collective-permute-done((bf16[384,1152]{1,0:T(8,128)(2,1)S(1)}, bf16[384,1152]{1,0:T(8,128)(2,1)S(1)}, u32[]{:S(2)}, u32[]{:S(2)}) %collective-permute-start.25) | collective-permute-done | bytes 884768 | tf_op jit(solution)/shard_map/ppermute | solution.py:56
  165.8 2.6 %collective-permute-done.24.refs_2_ = bf16[384,1152]{1,0:T(8,128)(2,1)S(1)} collective-permute-done((bf16[384,1152]{1,0:T(8,128)(2,1)S(1)}, bf16[384,1152]{1,0:T(8,128)(2,1)S(1)}, u32[]{:S(2)}, u32[]{:S(2)}) %collective-permute-start.24) | collective-permute-done | bytes 884768 | tf_op jit(solution)/shard_map/ppermute | solution.py:23
  168.4 2.0 collective-permute-done.23.refs_1_
  170.4 3.4 %collective-permute-start.26 = (bf16[384,1152]{1,0:T(8,128)(2,1)S(1)}, bf16[384,1152]{1,0:T(8,128)(2,1)S(1)}, u32[]{:S(2)}, u32[]{:S(2)}) collective-permute-start(bf16[384,1152]{1,0:T(8,128)(2,1)S(1)} %collective-permute-done.24.refs_2_), channel_id=1, source_target_pairs={{0,16},{8,56},{16,32},{24,8},{32,48},{40,24},{48,0},{56,40},{1,17}... | collective-permute-start | bytes 2654216 | tf_op jit(solution)/shard_map/ppermute | solution.py:56
  174.6 4.0 %shard_map.35.refs_0_ = f32[768,1152]{1,0:T(8,128)S(1)} custom-call(bf16[8,768,384]{2,1,0:T(8,128)(2,1)S(1)} %shard_map.34.gram_ref, bf16[384,1152]{1,0:T(8,128)(2,1)S(1)} %get-tuple-element.86.refs_0_, bf16[384,1152]{1,0:T(8,128)(2,1)S(1)} %collective-permute-done.23.refs_1_, bf16[384,1152]{1,0:T(8,128)(2,1)S(1)} %collective-permute-done.24.refs_2_, ...), custom_call_target="tpu_custom_call" | custom-call | tf_op jit(solution)/shard_map/pallas_call | solution.py:76
  178.6 12.7 %collective-permute-done.26.refs_2_ = bf16[384,1152]{1,0:T(8,128)(2,1)S(1)} collective-permute-done((bf16[384,1152]{1,0:T(8,128)(2,1)S(1)}, bf16[384,1152]{1,0:T(8,128)(2,1)S(1)}, u32[]{:S(2)}, u32[]{:S(2)}) %collective-permute-start.26) | collective-permute-done | bytes 884768 | tf_op jit(solution)/shard_map/ppermute | solution.py:56
  191.3 2.5 %collective-permute-done.28.refs_3_ = bf16[384,1152]{1,0:T(8,128)(2,1)S(1)} collective-permute-done((bf16[384,1152]{1,0:T(8,128)(2,1)S(1)}, bf16[384,1152]{1,0:T(8,128)(2,1)S(1)}, u32[]{:S(2)}, u32[]{:S(2)}) %collective-permute-start.28) | collective-permute-done | bytes 884768 | tf_op jit(solution)/shard_map/ppermute | solution.py:23
  196.1 3.2 %shard_map.36.refs_0_ = f32[768,1152]{1,0:T(8,128)S(1)} custom-call(bf16[8,768,384]{2,1,0:T(8,128)(2,1)S(1)} %shard_map.34.gram_ref, f32[768,1152]{1,0:T(8,128)S(1)} %shard_map.35.refs_0_, bf16[384,1152]{1,0:T(8,128)(2,1)S(1)} %collective-permute-done.27.refs_1_, bf16[384,1152]{1,0:T(8,128)(2,1)S(1)} %collective-permute-done.26.refs_2_, ...), custom_call_target="tpu_custom_call" | custom-call | tf_op jit(solution)/shard_map/pallas_call | solution.py:76
  199.3 7.3 %collective-permute-done.29.refs_1_ = bf16[384,1152]{1,0:T(8,128)(2,1)S(1)} collective-permute-done((bf16[384,1152]{1,0:T(8,128)(2,1)S(1)}, bf16[384,1152]{1,0:T(8,128)(2,1)S(1)}, u32[]{:S(2)}, u32[]{:S(2)}) %collective-permute-start.29) | collective-permute-done | bytes 884768 | tf_op jit(solution)/shard_map/ppermute | solution.py:56
  207.5 1.9 collective-permute-start.30
  (42 shorter events, 25.2 us)
Async XLA Ops:
  0.0 17.9 %collective-permute-start.3 = (bf16[384,1152]{1,0:T(8,128)(2,1)}, bf16[384,1152]{1,0:T(8,128)(2,1)S(1)}, u32[]{:S(2)}, u32[]{:S(2)}) collective-permute-start(bf16[384,1152]{1,0:T(8,128)(2,1)} %own_ref.13), channel_id=1, source_target_pairs={{0,48},{8,24},{16,0},{24,40},{32,16},{40,56},{48,32},{56,8},{1,49}... | collective-permute-start | bytes 2654216 | tf_op jit(solution)/shard_map/ppermute | solution.py:56
  2.1 19.4 %collective-permute-start.2 = (bf16[384,1152]{1,0:T(8,128)(2,1)}, bf16[384,1152]{1,0:T(8,128)(2,1)S(1)}, u32[]{:S(2)}, u32[]{:S(2)}) collective-permute-start(bf16[384,1152]{1,0:T(8,128)(2,1)} %own_ref.13), channel_id=1, source_target_pairs={{0,64},{64,0},{1,65},{65,1},{2,66},{66,2},{3,67},{67,3},{4,68},{68... | collective-permute-start | bytes 2654216 | tf_op jit(solution)/shard_map/ppermute | solution.py:23
  3.8 17.7 %collective-permute-start.1 = (bf16[384,1152]{1,0:T(8,128)(2,1)}, bf16[384,1152]{1,0:T(8,128)(2,1)S(1)}, u32[]{:S(2)}, u32[]{:S(2)}) collective-permute-start(bf16[384,1152]{1,0:T(8,128)(2,1)} %own_ref.13), channel_id=1, source_target_pairs={{0,8},{8,0},{1,9},{9,1},{2,10},{10,2},{3,11},{11,3},{4,12},{12,4},... | collective-permute-start | bytes 2654216 | tf_op jit(solution)/shard_map/ppermute | solution.py:31
  6.4 18.0 %collective-permute-start = (bf16[384,1152]{1,0:T(8,128)(2,1)}, bf16[384,1152]{1,0:T(8,128)(2,1)S(1)}, u32[]{:S(2)}, u32[]{:S(2)}) collective-permute-start(bf16[384,1152]{1,0:T(8,128)(2,1)} %own_ref.13), channel_id=1, source_target_pairs={{0,16},{8,56},{16,32},{24,8},{32,48},{40,24},{48,0},{56,40},{1,17}... | collective-permute-start | bytes 2654216 | tf_op jit(solution)/shard_map/ppermute | solution.py:56
  24.5 19.5 %collective-permute-start.4 = (bf16[384,1152]{1,0:T(8,128)(2,1)S(1)}, bf16[384,1152]{1,0:T(8,128)(2,1)}, u32[]{:S(2)}, u32[]{:S(2)}) collective-permute-start(bf16[384,1152]{1,0:T(8,128)(2,1)S(1)} %collective-permute-done.2.refs_2_), channel_id=1, source_target_pairs={{0,16},{8,56},{16,32},{24,8},{32,48},{40,24},{48,0},{56,40},{1,17}... | collective-permute-start | bytes 2654216 | tf_op jit(solution)/shard_map/ppermute | solution.py:56
  27.5 20.8 %collective-permute-start.6 = (bf16[384,1152]{1,0:T(8,128)(2,1)S(1)}, bf16[384,1152]{1,0:T(8,128)(2,1)}, u32[]{:S(2)}, u32[]{:S(2)}) collective-permute-start(bf16[384,1152]{1,0:T(8,128)(2,1)S(1)} %collective-permute-done.3.refs_3_), channel_id=1, source_target_pairs={{0,64},{64,0},{1,65},{65,1},{2,66},{66,2},{3,67},{67,3},{4,68},{68... | collective-permute-start | bytes 2654216 | tf_op jit(solution)/shard_map/ppermute | solution.py:23
  29.1 19.2 %collective-permute-start.5 = (bf16[384,1152]{1,0:T(8,128)(2,1)S(1)}, bf16[384,1152]{1,0:T(8,128)(2,1)}, u32[]{:S(2)}, u32[]{:S(2)}) collective-permute-start(bf16[384,1152]{1,0:T(8,128)(2,1)S(1)} %collective-permute-done.3.refs_3_), channel_id=1, source_target_pairs={{0,48},{8,24},{16,0},{24,40},{32,16},{40,56},{48,32},{56,8},{1,49}... | collective-permute-start | bytes 2654216 | tf_op jit(solution)/shard_map/ppermute | solution.py:56
  29.2 1.2 copy-start
  30.4 6.0 %copy-start.1 = (bf16[384,1152]{1,0:T(8,128)(2,1)S(1)}, bf16[384,1152]{1,0:T(8,128)(2,1)}, u32[]{:S(2)}) copy-start(bf16[384,1152]{1,0:T(8,128)(2,1)} %own_ref.13) | copy-start | bytes 2654212
  33.8 25.3 %collective-permute-start.8 = (bf16[2,2,192,768]{3,2,1,0:T(8,128)(2,1)S(1)}, bf16[2,2,192,768]{3,2,1,0:T(8,128)(2,1)S(1)}, u32[]{:S(2)}, u32[]{:S(2)}) collective-permute-start(bf16[2,2,192,768]{3,2,1,0:T(8,128)(2,1)S(1)} %shard_map.19), channel_id=1, source_target_pairs={{0,1},{1,0},{2,3},{3,2},{8,11},{9,10},{10,9},{11,8},{4,5},{5,4},{6... | collective-permute-start | bytes 3538952 | tf_op jit(solution)/shard_map/ppermute | solution.py:47
  48.3 12.4 %collective-permute-start.7 = (bf16[384,1152]{1,0:T(8,128)(2,1)}, bf16[384,1152]{1,0:T(8,128)(2,1)S(1)}, u32[]{:S(2)}, u32[]{:S(2)}) collective-permute-start(bf16[384,1152]{1,0:T(8,128)(2,1)} %collective-permute-done.4.refs_1_.refs_5_), channel_id=1, source_target_pairs={{0,16},{8,56},{16,32},{24,8},{32,48},{40,24},{48,0},{56,40},{1,17}... | collective-permute-start | bytes 2654216 | tf_op jit(solution)/shard_map/ppermute | solution.py:56
  52.7 14.4 %collective-permute-start.9 = (bf16[2,2,144,768]{3,2,1,0:T(8,128)(2,1)S(1)}, bf16[2,2,144,768]{3,2,1,0:T(8,128)(2,1)S(1)}, u32[]{:S(2)}, u32[]{:S(2)}) collective-permute-start(bf16[2,2,144,768]{3,2,1,0:T(8,128)(2,1)S(1)} %shard_map.21), channel_id=1, source_target_pairs={{0,1},{1,0},{2,3},{3,2},{8,11},{9,10},{10,9},{11,8},{4,5},{5,4},{6... | collective-permute-start | bytes 2654216 | tf_op jit(solution)/shard_map/ppermute | solution.py:47
  60.9 13.1 %collective-permute-start.11 = (bf16[2,192,768]{2,1,0:T(8,128)(2,1)S(1)}, bf16[2,192,768]{2,1,0:T(8,128)(2,1)S(1)}, u32[]{:S(2)}, u32[]{:S(2)}) collective-permute-start(bf16[2,192,768]{2,1,0:T(8,128)(2,1)S(1)} %get-tuple-element.63), channel_id=1, source_target_pairs={{0,3},{1,2},{2,1},{3,0},{8,9},{9,8},{10,11},{11,10},{4,7},{5,6},{6... | collective-permute-start | bytes 1769480 | tf_op jit(solution)/shard_map/ppermute | solution.py:47
  63.7 10.3 %collective-permute-start.10 = (bf16[2,2,48,768]{3,2,1,0:T(8,128)(2,1)S(1)}, bf16[2,2,48,768]{3,2,1,0:T(8,128)(2,1)S(1)}, u32[]{:S(2)}, u32[]{:S(2)}) collective-permute-start(bf16[2,2,48,768]{3,2,1,0:T(8,128)(2,1)S(1)} %shard_map.23), channel_id=1, source_target_pairs={{0,1},{1,0},{2,3},{3,2},{8,11},{9,10},{10,9},{11,8},{4,5},{5,4},{6... | collective-permute-start | bytes 884744 | tf_op jit(solution)/shard_map/ppermute | solution.py:47
  74.2 9.1 %collective-permute-start.12 = (bf16[2,192,768]{2,1,0:T(8,128)(2,1)S(1)}, bf16[2,192,768]{2,1,0:T(8,128)(2,1)S(1)}, u32[]{:S(2)}, u32[]{:S(2)}) collective-permute-start(bf16[2,192,768]{2,1,0:T(8,128)(2,1)S(1)} %get-tuple-element.70), channel_id=1, source_target_pairs={{0,3},{1,2},{2,1},{3,0},{8,9},{9,8},{10,11},{11,10},{4,7},{5,6},{6... | collective-permute-start | bytes 1769480 | tf_op jit(solution)/shard_map/ppermute | solution.py:47
  75.7 7.4 %collective-permute-start.13 = (bf16[192,768]{1,0:T(8,128)(2,1)S(1)}, bf16[192,768]{1,0:T(8,128)(2,1)S(1)}, u32[]{:S(2)}, u32[]{:S(2)}) collective-permute-start(bf16[192,768]{1,0:T(8,128)(2,1)S(1)} %shard_map.25), channel_id=1, source_target_pairs={{0,4},{4,0},{1,5},{5,1},{2,6},{6,2},{3,7},{7,3},{8,12},{12,8},{9,1... | collective-permute-start | bytes 884744 | tf_op jit(solution)/shard_map/ppermute | solution.py:27
  83.4 7.6 %collective-permute-start.14 = (bf16[192,768]{1,0:T(8,128)(2,1)S(1)}, bf16[192,768]{1,0:T(8,128)(2,1)S(1)}, u32[]{:S(2)}, u32[]{:S(2)}) collective-permute-start(bf16[192,768]{1,0:T(8,128)(2,1)S(1)} %shard_map.26), channel_id=1, source_target_pairs={{0,4},{4,0},{1,5},{5,1},{2,6},{6,2},{3,7},{7,3},{8,12},{12,8},{9,1... | collective-permute-start | bytes 884744 | tf_op jit(solution)/shard_map/ppermute | solution.py:27
  91.3 12.0 %collective-permute-start.17 = (bf16[768,384]{1,0:T(8,128)(2,1)S(1)}, bf16[768,384]{1,0:T(8,128)(2,1)S(1)}, u32[]{:S(2)}, u32[]{:S(2)}) collective-permute-start(bf16[768,384]{1,0:T(8,128)(2,1)S(1)} %shard_map.27.refs_0_), channel_id=1, source_target_pairs={{0,4},{4,0},{1,5},{5,1},{2,6},{6,2},{3,7},{7,3},{8,12},{12,8},{9,1... | collective-permute-start | bytes 1769480 | tf_op jit(solution)/shard_map/ppermute | solution.py:27
  94.8 10.5 %collective-permute-start.16 = (bf16[768,384]{1,0:T(8,128)(2,1)S(1)}, bf16[768,384]{1,0:T(8,128)(2,1)S(1)}, u32[]{:S(2)}, u32[]{:S(2)}) collective-permute-start(bf16[768,384]{1,0:T(8,128)(2,1)S(1)} %shard_map.27.refs_0_), channel_id=1, source_target_pairs={{0,3},{1,2},{2,1},{3,0},{4,7},{5,6},{6,5},{7,4},{8,11},{9,10},{10,... | collective-permute-start | bytes 1769480 | tf_op jit(solution)/shard_map/ppermute | solution.py:39
  97.7 12.1 %collective-permute-start.15 = (bf16[768,384]{1,0:T(8,128)(2,1)S(1)}, bf16[768,384]{1,0:T(8,128)(2,1)S(1)}, u32[]{:S(2)}, u32[]{:S(2)}) collective-permute-start(bf16[768,384]{1,0:T(8,128)(2,1)S(1)} %shard_map.27.refs_0_), channel_id=1, source_target_pairs={{0,1},{1,0},{2,3},{3,2},{4,5},{5,4},{6,7},{7,6},{8,9},{9,8},{10,11... | collective-permute-start | bytes 1769480 | tf_op jit(solution)/shard_map/ppermute | solution.py:35
  109.8 10.7 %collective-permute-start.20 = (bf16[768,384]{1,0:T(8,128)(2,1)S(1)}, bf16[768,384]{1,0:T(8,128)(2,1)S(1)}, u32[]{:S(2)}, u32[]{:S(2)}) collective-permute-start(bf16[768,384]{1,0:T(8,128)(2,1)S(1)} %collective-permute-done.17.refs_3_), channel_id=1, source_target_pairs={{0,3},{1,2},{2,1},{3,0},{4,7},{5,6},{6,5},{7,4},{8,11},{9,10},{10,... | collective-permute-start | bytes 1769480 | tf_op jit(solution)/shard_map/ppermute | solution.py:39
  109.8 12.6 %collective-permute-start.19 = (bf16[768,384]{1,0:T(8,128)(2,1)S(1)}, bf16[768,384]{1,0:T(8,128)(2,1)S(1)}, u32[]{:S(2)}, u32[]{:S(2)}) collective-permute-start(bf16[768,384]{1,0:T(8,128)(2,1)S(1)} %collective-permute-done.17.refs_3_), channel_id=1, source_target_pairs={{0,1},{1,0},{2,3},{3,2},{4,5},{5,4},{6,7},{7,6},{8,9},{9,8},{10,11... | collective-permute-start | bytes 1769480 | tf_op jit(solution)/shard_map/ppermute | solution.py:35
  112.4 20.7 %collective-permute-start.18 = (bf16[768,384]{1,0:T(8,128)(2,1)S(1)}, bf16[768,384]{1,0:T(8,128)(2,1)S(1)}, u32[]{:S(2)}, u32[]{:S(2)}) collective-permute-start(bf16[768,384]{1,0:T(8,128)(2,1)S(1)} %collective-permute-done.15.refs_1_), channel_id=1, source_target_pairs={{0,3},{1,2},{2,1},{3,0},{4,7},{5,6},{6,5},{7,4},{8,11},{9,10},{10,... | collective-permute-start | bytes 1769480 | tf_op jit(solution)/shard_map/ppermute | solution.py:39
  122.4 10.8 %collective-permute-start.21 = (bf16[768,384]{1,0:T(8,128)(2,1)S(1)}, bf16[768,384]{1,0:T(8,128)(2,1)S(1)}, u32[]{:S(2)}, u32[]{:S(2)}) collective-permute-start(bf16[768,384]{1,0:T(8,128)(2,1)S(1)} %collective-permute-done.20.refs_1_.refs_5_), channel_id=1, source_target_pairs={{0,1},{1,0},{2,3},{3,2},{4,5},{5,4},{6,7},{7,6},{8,9},{9,8},{10,11... | collective-permute-start | bytes 1769480 | tf_op jit(solution)/shard_map/ppermute | solution.py:35
  134.9 11.5 %collective-permute-start.22 = (bf16[384,1152]{1,0:T(8,128)(2,1)S(1)}, bf16[384,1152]{1,0:T(8,128)(2,1)S(1)}, u32[]{:S(2)}, u32[]{:S(2)}) collective-permute-start(bf16[384,1152]{1,0:T(8,128)(2,1)S(1)} %shard_map.31), channel_id=1, source_target_pairs={{0,8},{8,0},{1,9},{9,1},{2,10},{10,2},{3,11},{11,3},{4,12},{12,4},... | collective-permute-start | bytes 2654216 | tf_op jit(solution)/shard_map/ppermute | solution.py:31
  146.7 19.1 %collective-permute-start.25 = (bf16[384,1152]{1,0:T(8,128)(2,1)S(1)}, bf16[384,1152]{1,0:T(8,128)(2,1)S(1)}, u32[]{:S(2)}, u32[]{:S(2)}) collective-permute-start(bf16[384,1152]{1,0:T(8,128)(2,1)S(1)} %get-tuple-element.86.refs_0_), channel_id=1, source_target_pairs={{0,48},{8,24},{16,0},{24,40},{32,16},{40,56},{48,32},{56,8},{1,49}... | collective-permute-start | bytes 2654216 | tf_op jit(solution)/shard_map/ppermute | solution.py:56
  149.1 19.3 %collective-permute-start.24 = (bf16[384,1152]{1,0:T(8,128)(2,1)S(1)}, bf16[384,1152]{1,0:T(8,128)(2,1)S(1)}, u32[]{:S(2)}, u32[]{:S(2)}) collective-permute-start(bf16[384,1152]{1,0:T(8,128)(2,1)S(1)} %get-tuple-element.86.refs_0_), channel_id=1, source_target_pairs={{0,64},{64,0},{1,65},{65,1},{2,66},{66,2},{3,67},{67,3},{4,68},{68... | collective-permute-start | bytes 2654216 | tf_op jit(solution)/shard_map/ppermute | solution.py:23
  149.8 20.6 %collective-permute-start.23 = (bf16[384,1152]{1,0:T(8,128)(2,1)S(1)}, bf16[384,1152]{1,0:T(8,128)(2,1)S(1)}, u32[]{:S(2)}, u32[]{:S(2)}) collective-permute-start(bf16[384,1152]{1,0:T(8,128)(2,1)S(1)} %get-tuple-element.86.refs_0_), channel_id=1, source_target_pairs={{0,16},{8,56},{16,32},{24,8},{32,48},{40,24},{48,0},{56,40},{1,17}... | collective-permute-start | bytes 2654216 | tf_op jit(solution)/shard_map/ppermute | solution.py:56
  170.4 20.8 %collective-permute-start.26 = (bf16[384,1152]{1,0:T(8,128)(2,1)S(1)}, bf16[384,1152]{1,0:T(8,128)(2,1)S(1)}, u32[]{:S(2)}, u32[]{:S(2)}) collective-permute-start(bf16[384,1152]{1,0:T(8,128)(2,1)S(1)} %collective-permute-done.24.refs_2_), channel_id=1, source_target_pairs={{0,16},{8,56},{16,32},{24,8},{32,48},{40,24},{48,0},{56,40},{1,17}... | collective-permute-start | bytes 2654216 | tf_op jit(solution)/shard_map/ppermute | solution.py:56
  173.8 19.9 %collective-permute-start.28 = (bf16[384,1152]{1,0:T(8,128)(2,1)S(1)}, bf16[384,1152]{1,0:T(8,128)(2,1)S(1)}, u32[]{:S(2)}, u32[]{:S(2)}) collective-permute-start(bf16[384,1152]{1,0:T(8,128)(2,1)S(1)} %collective-permute-done.25.refs_3_), channel_id=1, source_target_pairs={{0,64},{64,0},{1,65},{65,1},{2,66},{66,2},{3,67},{67,3},{4,68},{68... | collective-permute-start | bytes 2654216 | tf_op jit(solution)/shard_map/ppermute | solution.py:23
  174.6 19.8 %collective-permute-start.27 = (bf16[384,1152]{1,0:T(8,128)(2,1)S(1)}, bf16[384,1152]{1,0:T(8,128)(2,1)S(1)}, u32[]{:S(2)}, u32[]{:S(2)}) collective-permute-start(bf16[384,1152]{1,0:T(8,128)(2,1)S(1)} %collective-permute-done.25.refs_3_), channel_id=1, source_target_pairs={{0,48},{8,24},{16,0},{24,40},{32,16},{40,56},{48,32},{56,8},{1,49}... | collective-permute-start | bytes 2654216 | tf_op jit(solution)/shard_map/ppermute | solution.py:56
  194.4 12.2 %collective-permute-start.29 = (bf16[384,1152]{1,0:T(8,128)(2,1)S(1)}, bf16[384,1152]{1,0:T(8,128)(2,1)S(1)}, u32[]{:S(2)}, u32[]{:S(2)}) collective-permute-start(bf16[384,1152]{1,0:T(8,128)(2,1)S(1)} %collective-permute-done.26.refs_2_), channel_id=1, source_target_pairs={{0,16},{8,56},{16,32},{24,8},{32,48},{40,24},{48,0},{56,40},{1,17}... | collective-permute-start | bytes 2654216 | tf_op jit(solution)/shard_map/ppermute | solution.py:56
  207.5 3.9 %collective-permute-start.30 = (bf16[384,1152]{1,0:T(8,128)(2,1)S(1)}, bf16[384,1152]{1,0:T(8,128)(2,1)S(1)}, u32[]{:S(2)}, u32[]{:S(2)}) collective-permute-start(bf16[384,1152]{1,0:T(8,128)(2,1)S(1)} %shard_map.37), channel_id=1, source_target_pairs={{0,8},{8,0},{1,9},{9,1},{2,10},{10,2},{3,11},{11,3},{4,12},{12,4},... | collective-permute-start | bytes 2654216 | tf_op jit(solution)/shard_map/ppermute | solution.py:31

commit v3 on v2

--- a/solution.py
+++ b/solution.py
@@ -60,10 +60,11 @@
     return lax.optimization_barrier(values)
 
 
-EARLY = ((0, "v"), (0, "r0"), (1, "v"), (0, "r1"))
+OWN = ((0, "v"),)
+EARLY = ((0, "r0"), (1, "v"), (0, "r1"))
 MIDDLE = ((0, "f"), (1, "r0"), (1, "r1"))
 LATE = ((1, "f"),)
-ARRIVAL = EARLY + MIDDLE + LATE
+ARRIVAL = OWN + EARLY + MIDDLE + LATE
 
 
 VM = pl.BlockSpec(memory_space=pltpu.VMEM)
@@ -328,8 +329,11 @@
     r0 = along_y(own)
     r1 = along_y(own, False)
     w = swap_core(own)
-    r0, w, z, r1 = together(r0, w, z, r1)
-    x[0, "v"], x[0, "r0"], x[1, "v"], x[0, "r1"] = own, r0, z, r1
+    x[0, "v"] = own
+    got0 = partner(terms(OWN, True), True)
+    keep0 = terms(OWN, False)
+    r0, w, z, r1, got0, keep0 = together(r0, w, z, r1, got0, keep0)
+    x[0, "r0"], x[1, "v"], x[0, "r1"] = r0, z, r1
     rz1 = swap_zl(r1)
     rz0 = along_y(z)
     f = along_y(r1, False)
@@ -338,18 +342,17 @@
     rz0, f, rz1, keep1 = together(rz0, f, rz1, keep1)
     x[0, "f"], x[1, "r0"], x[1, "r1"] = f, rz0, rz1
     fz = along_y(rz0)
-    send2 = terms(MIDDLE, True)
-    got2 = partner(send2, True)
+    mine1, other1 = sum_pair((keep0, got0), (keep1, got1))
+    last1 = partner(other1, False)
+    got2 = partner(terms(MIDDLE, True), True)
     keep2 = terms(MIDDLE, False)
-    fz, keep2, got1 = together(fz, keep2, got1)
+    fz, keep2, last1 = together(fz, keep2, last1)
     x[1, "f"] = fz
     got3 = partner(terms(LATE, True), True)
-    mine1, other1 = sum_pair((keep1, got1))
-    last1 = partner(other1, False)
+    z1 = swap_zh(sum_other((mine1, last1)))
     keep3 = terms(LATE, False)
-    got2, keep3, got3, last1 = together(got2, keep3, got3, last1)
+    got2, keep3, got3 = together(got2, keep3, got3)
     mine2, other2 = sum_pair((keep2, got2), (keep3, got3))
-    z1 = swap_zh(sum_other((mine1, last1)))
     last2 = partner(other2, False)
     last2, z1 = together(last2, z1)
     z2 = swap_zh(sum_other((mine2, last2)))
@@ -389,7 +392,7 @@
     rz1 = swap_zl(r1)
     rz0 = along_y(z)
     f = along_y(r1, False)
-    total = add(None, EARLY)
+    total = add(None, OWN + EARLY)
     rz0, f, rz1, total = together(rz0, f, rz1, total)
     u[0, "f"], u[1, "r0"], u[1, "r1"] = f, rz0, rz1
     fz = along_y(rz0)

time: 213 us -> 211 us (level)
  starting transfers between devices: 64.7 us -> 56.4 us
  waiting for transfers between devices: 99.4 us -> 107 us
    ppermute x3, waiting for transfers between devices: 10.2 us -> 19.2 us  [swap_x3(): return lax.ppermute(v, 'x', [(i, i ^ 3) for i in range(4)])]
    ppermute x3, starting transfers between devices: 14 us -> 7.89 us  [swap_core(): return lax.ppermute(v, 'c', [(0, 1), (1, 0)])]
    ppermute x3, starting transfers between devices: 6.73 us -> 3.47 us  [swap_x1(): return lax.ppermute(v, 'x', [(i, i ^ 1) for i in range(4)])]
    ppermute x5 -> x6, starting transfers between devices: 9.7 us -> 12.6 us  [partner(): return lax.ppermute(v, ('c', 'x'), pairs)]
    ppermute x3, waiting for transfers between devices: 6.54 us -> 3.69 us  [swap_x1(): return lax.ppermute(v, 'x', [(i, i ^ 1) for i in range(4)])]
    ppermute x10, starting transfers between devices: 14.7 us -> 12.5 us  [along_y(): return lax.ppermute(v, ('y', 'c'), pairs)]
    ppermute x5 -> x6, waiting for transfers between devices: 7.06 us -> 6.38 us  [partner(): return lax.ppermute(v, ('c', 'x'), pairs)]
    pallas_call x22 -> x24, Pallas kernels: 44.4 us -> 43.9 us  [call(): pl.pallas_call(kernel, out_shape=out_shape, in_specs=in_specs, out_specs=...]
  transfers between devices with their start and end apart: 31 -> 32, of which waited for: 25 -> 27; matrix products, arithmetic and copies ran while one was open for 0% -> 0% of each run, Pallas kernels for 20% -> 20%
where the time goes in v3:
time: 211 us
  waiting for transfers between devices  107 us (51%)
  starting transfers between devices  56.4 us (27%)
  Pallas kernels  46.9 us (22%)
    ppermute x10, waiting for transfers between devices, along_y(): return lax.ppermute(v, ('y', 'c'), pairs)  51.8 us
    pallas_call x24, Pallas kernels, call(): pl.pallas_call(kernel, out_shape=out_shape, in_specs=in_specs, out_specs=...  43.9 us
    ppermute x3, waiting for transfers between devices, swap_x3(): return lax.ppermute(v, 'x', [(i, i ^ 3) for i in range(4)])  19.2 us
    ppermute x4, waiting for transfers between devices, swap_zl(): return lax.ppermute(v, 'zl', [(0, 1), (1, 0)])  14 us
    ppermute x6, starting transfers between devices, partner(): return lax.ppermute(v, ('c', 'x'), pairs)  12.6 us
    ppermute x10, starting transfers between devices, along_y(): return lax.ppermute(v, ('y', 'c'), pairs)  12.5 us
    ppermute x3, starting transfers between devices, swap_zh(): return lax.ppermute(v, 'zh', [(0, 1), (1, 0)])  10.6 us
    ppermute x3, waiting for transfers between devices, swap_zh(): return lax.ppermute(v, 'zh', [(0, 1), (1, 0)])  9.95 us
  transfers between devices with their start and end apart: 32, of which 27 were waited for; matrix products, arithmetic and copies ran while one was open for 0% of the time, Pallas kernels for 20%

profile of v3, /device:TPU:1, one launch (start us, length us, event | category | flops | bytes accessed | tf_op | source)
XLA Modules:
  0.0 211.3 jit_solution(2391334419503459071)
XLA Ops:
  2.8 1.6 collective-permute-start.2
  8.6 2.6 %collective-permute-start.4 = (bf16[2,2,48,768]{3,2,1,0:T(8,128)(2,1)S(1)}, bf16[2,2,48,768]{3,2,1,0:T(8,128)(2,1)S(1)}, u32[]{:S(2)}, u32[]{:S(2)}) collective-permute-start(bf16[2,2,48,768]{3,2,1,0:T(8,128)(2,1)S(1)} %shard_map.17), channel_id=1, source_target_pairs={{0,1},{1,0},{2,3},{3,2},{8,11},{9,10},{10,9},{11,8},{4,5},{5,4},{6... | collective-permute-start | bytes 884744 | tf_op jit(solution)/shard_map/ppermute | solution.py:47
  12.7 6.6 %collective-permute-done.3.refs_2_.refs_3_ = bf16[384,1152]{1,0:T(8,128)(2,1)S(1)} collective-permute-done((bf16[384,1152]{1,0:T(8,128)(2,1)}, bf16[384,1152]{1,0:T(8,128)(2,1)S(1)}, u32[]{:S(2)}, u32[]{:S(2)}) %collective-permute-start.3) | collective-permute-done | bytes 884768 | tf_op jit(solution)/shard_map/ppermute | solution.py:56
  19.3 3.6 %collective-permute-done.2.refs_1_.refs_2_ = bf16[384,1152]{1,0:T(8,128)(2,1)S(1)} collective-permute-done((bf16[384,1152]{1,0:T(8,128)(2,1)}, bf16[384,1152]{1,0:T(8,128)(2,1)S(1)}, u32[]{:S(2)}, u32[]{:S(2)}) %collective-permute-start.2) | collective-permute-done | bytes 884768 | tf_op jit(solution)/shard_map/ppermute | solution.py:23
  22.8 1.6 collective-permute-done.refs_0_.refs_1_
  24.5 3.0 %collective-permute-start.5 = (bf16[384,1152]{1,0:T(8,128)(2,1)S(1)}, bf16[384,1152]{1,0:T(8,128)(2,1)S(1)}, u32[]{:S(2)}, u32[]{:S(2)}) collective-permute-start(bf16[384,1152]{1,0:T(8,128)(2,1)S(1)} %collective-permute-done.2.refs_1_.refs_2_), channel_id=1, source_target_pairs={{0,16},{8,56},{16,32},{24,8},{32,48},{40,24},{48,0},{56,40},{1,17}... | collective-permute-start | bytes 2654216 | tf_op jit(solution)/shard_map/ppermute | solution.py:56
  28.6 2.7 %shard_map.20 = bf16[2,2,144,768]{3,2,1,0:T(8,128)(2,1)S(1)} custom-call(s32[4]{0:T(128)S(1)} %pad_add_fusion.where_ref, bf16[384,1152]{1,0:T(8,128)(2,1)S(1)} %copy-done.1, bf16[384,1152]{1,0:T(8,128)(2,1)S(1)} %collective-permute-done.1.sib_ref, bf16[384,1152]{1,0:T(8,128)(2,1)S(1)} %collective-permute-done.refs_0_.refs_1_, ...), custom_call_target="tpu_custom_call" | custom-call | tf_op jit(solution)/shard_map/pallas_call | solution.py:77
  31.4 2.6 %collective-permute-start.8 = (bf16[2,2,144,768]{3,2,1,0:T(8,128)(2,1)S(1)}, bf16[2,2,144,768]{3,2,1,0:T(8,128)(2,1)S(1)}, u32[]{:S(2)}, u32[]{:S(2)}) collective-permute-start(bf16[2,2,144,768]{3,2,1,0:T(8,128)(2,1)S(1)} %shard_map.20), channel_id=1, source_target_pairs={{0,1},{1,0},{2,3},{3,2},{8,11},{9,10},{10,9},{11,8},{4,5},{5,4},{6... | collective-permute-start | bytes 2654216 | tf_op jit(solution)/shard_map/ppermute | solution.py:47
  33.9 2.7 %shard_map.19.refs_2_ = f32[2,2,144,768]{3,2,1,0:T(8,128)S(1)} custom-call(s32[4]{0:T(128)S(1)} %pad_add_fusion.where_ref, bf16[384,1152]{1,0:T(8,128)(2,1)S(1)} %copy-done.1, bf16[384,1152]{1,0:T(8,128)(2,1)S(1)} %collective-permute-done.1.sib_ref, bf16[384,1152]{1,0:T(8,128)(2,1)S(1)} %collective-permute-done.refs_0_.refs_1_, ...), custom_call_target="tpu_custom_call" | custom-call | tf_op jit(solution)/shard_map/pallas_call | solution.py:77
  36.6 7.3 %collective-permute-done.5.refs_1_.refs_5_ = bf16[384,1152]{1,0:T(8,128)(2,1)S(1)} collective-permute-done((bf16[384,1152]{1,0:T(8,128)(2,1)S(1)}, bf16[384,1152]{1,0:T(8,128)(2,1)S(1)}, u32[]{:S(2)}, u32[]{:S(2)}) %collective-permute-start.5) | collective-permute-done | bytes 884768 | tf_op jit(solution)/shard_map/ppermute | solution.py:56
  44.0 3.7 %collective-permute-done.7.refs_2_.refs_6_ = bf16[384,1152]{1,0:T(8,128)(2,1)S(1)} collective-permute-done((bf16[384,1152]{1,0:T(8,128)(2,1)S(1)}, bf16[384,1152]{1,0:T(8,128)(2,1)S(1)}, u32[]{:S(2)}, u32[]{:S(2)}) %collective-permute-start.7) | collective-permute-done | bytes 884768 | tf_op jit(solution)/shard_map/ppermute | solution.py:23
  50.7 2.7 %shard_map.23 = bf16[2,2,144,768]{3,2,1,0:T(8,128)(2,1)S(1)} custom-call(s32[4]{0:T(128)S(1)} %pad_add_fusion.where_ref, bf16[384,1152]{1,0:T(8,128)(2,1)S(1)} %copy-done.1, bf16[384,1152]{1,0:T(8,128)(2,1)S(1)} %collective-permute-done.1.sib_ref, bf16[384,1152]{1,0:T(8,128)(2,1)S(1)} %collective-permute-done.6.refs_0_.refs_4_, ...), custom_call_target="tpu_custom_call" | custom-call | tf_op jit(solution)/shard_map/pallas_call | solution.py:77
  53.4 1.9 collective-permute-start.11
  55.3 2.7 %shard_map.22.refs_0_ = f32[2,2,144,768]{3,2,1,0:T(8,128)S(1)} custom-call(s32[4]{0:T(128)S(1)} %pad_add_fusion.where_ref, bf16[384,1152]{1,0:T(8,128)(2,1)S(1)} %copy-done.1, bf16[384,1152]{1,0:T(8,128)(2,1)S(1)} %collective-permute-done.1.sib_ref, bf16[384,1152]{1,0:T(8,128)(2,1)S(1)} %collective-permute-done.6.refs_0_.refs_4_, ...), custom_call_target="tpu_custom_call" | custom-call | tf_op jit(solution)/shard_map/pallas_call | solution.py:77
  58.1 1.8 collective-permute-done.10.refs_1_
  60.5 1.5 shard_map.25
  62.0 3.9 %collective-permute-start.12 = (bf16[2,2,48,768]{3,2,1,0:T(8,128)(2,1)S(1)}, bf16[2,2,48,768]{3,2,1,0:T(8,128)(2,1)S(1)}, u32[]{:S(2)}, u32[]{:S(2)}) collective-permute-start(bf16[2,2,48,768]{3,2,1,0:T(8,128)(2,1)S(1)} %shard_map.25), channel_id=1, source_target_pairs={{0,1},{1,0},{2,3},{3,2},{8,11},{9,10},{10,9},{11,8},{4,5},{5,4},{6... | collective-permute-start | bytes 884744 | tf_op jit(solution)/shard_map/ppermute | solution.py:47
  68.5 3.2 %collective-permute-done.12.refs_3_ = bf16[2,2,48,768]{3,2,1,0:T(8,128)(2,1)S(1)} collective-permute-done((bf16[2,2,48,768]{3,2,1,0:T(8,128)(2,1)S(1)}, bf16[2,2,48,768]{3,2,1,0:T(8,128)(2,1)S(1)}, u32[]{:S(2)}, u32[]{:S(2)}) %collective-permute-start.12) | collective-permute-done | bytes 294944 | tf_op jit(solution)/shard_map/ppermute | solution.py:47
  72.3 3.7 %collective-permute-start.14 = (bf16[192,768]{1,0:T(8,128)(2,1)S(1)}, bf16[192,768]{1,0:T(8,128)(2,1)S(1)}, u32[]{:S(2)}, u32[]{:S(2)}) collective-permute-start(bf16[192,768]{1,0:T(8,128)(2,1)S(1)} %shard_map.27), channel_id=1, source_target_pairs={{0,4},{4,0},{1,5},{5,1},{2,6},{6,2},{3,7},{7,3},{8,12},{12,8},{9,1... | collective-permute-start | bytes 884744 | tf_op jit(solution)/shard_map/ppermute | solution.py:27
  76.0 4.6 %collective-permute-done.14.refs_4_ = bf16[192,768]{1,0:T(8,128)(2,1)S(1)} collective-permute-done((bf16[192,768]{1,0:T(8,128)(2,1)S(1)}, bf16[192,768]{1,0:T(8,128)(2,1)S(1)}, u32[]{:S(2)}, u32[]{:S(2)}) %collective-permute-start.14) | collective-permute-done | bytes 294944 | tf_op jit(solution)/shard_map/ppermute | solution.py:27
  81.0 3.9 %collective-permute-start.15 = (bf16[192,768]{1,0:T(8,128)(2,1)S(1)}, bf16[192,768]{1,0:T(8,128)(2,1)S(1)}, u32[]{:S(2)}, u32[]{:S(2)}) collective-permute-start(bf16[192,768]{1,0:T(8,128)(2,1)S(1)} %shard_map.28), channel_id=1, source_target_pairs={{0,4},{4,0},{1,5},{5,1},{2,6},{6,2},{3,7},{7,3},{8,12},{12,8},{9,1... | collective-permute-start | bytes 884744 | tf_op jit(solution)/shard_map/ppermute | solution.py:27
  84.9 4.7 %collective-permute-done.15.refs_5_ = bf16[192,768]{1,0:T(8,128)(2,1)S(1)} collective-permute-done((bf16[192,768]{1,0:T(8,128)(2,1)S(1)}, bf16[192,768]{1,0:T(8,128)(2,1)S(1)}, u32[]{:S(2)}, u32[]{:S(2)}) %collective-permute-start.15) | collective-permute-done | bytes 294944 | tf_op jit(solution)/shard_map/ppermute | solution.py:27
  89.9 3.0 %collective-permute-start.18 = (bf16[768,384]{1,0:T(8,128)(2,1)S(1)}, bf16[768,384]{1,0:T(8,128)(2,1)S(1)}, u32[]{:S(2)}, u32[]{:S(2)}) collective-permute-start(bf16[768,384]{1,0:T(8,128)(2,1)S(1)} %shard_map.29.refs_0_), channel_id=1, source_target_pairs={{0,4},{4,0},{1,5},{5,1},{2,6},{6,2},{3,7},{7,3},{8,12},{12,8},{9,1... | collective-permute-start | bytes 1769480 | tf_op jit(solution)/shard_map/ppermute | solution.py:27
  92.9 3.5 %collective-permute-start.17 = (bf16[768,384]{1,0:T(8,128)(2,1)S(1)}, bf16[768,384]{1,0:T(8,128)(2,1)S(1)}, u32[]{:S(2)}, u32[]{:S(2)}) collective-permute-start(bf16[768,384]{1,0:T(8,128)(2,1)S(1)} %shard_map.29.refs_0_), channel_id=1, source_target_pairs={{0,3},{1,2},{2,1},{3,0},{4,7},{5,6},{6,5},{7,4},{8,11},{9,10},{10,... | collective-permute-start | bytes 1769480 | tf_op jit(solution)/shard_map/ppermute | solution.py:39
  96.5 2.9 %collective-permute-start.16 = (bf16[768,384]{1,0:T(8,128)(2,1)S(1)}, bf16[768,384]{1,0:T(8,128)(2,1)S(1)}, u32[]{:S(2)}, u32[]{:S(2)}) collective-permute-start(bf16[768,384]{1,0:T(8,128)(2,1)S(1)} %shard_map.29.refs_0_), channel_id=1, source_target_pairs={{0,1},{1,0},{2,3},{3,2},{4,5},{5,4},{6,7},{7,6},{8,9},{9,8},{10,11... | collective-permute-start | bytes 1769480 | tf_op jit(solution)/shard_map/ppermute | solution.py:35
  99.3 3.0 %shard_map.30.refs_4_.refs_2_ = bf16[8,384,1152]{2,1,0:T(8,128)(2,1)S(1)} custom-call(bf16[384,1152]{1,0:T(8,128)(2,1)S(1)} %copy-done.1, bf16[384,1152]{1,0:T(8,128)(2,1)S(1)} %collective-permute-done.refs_0_.refs_1_, bf16[384,1152]{1,0:T(8,128)(2,1)S(1)} %collective-permute-done.2.refs_1_.refs_2_, ...), custom_call_target="tpu_custom_call" | custom-call | tf_op jit(solution)/shard_map/pallas_call | solution.py:202
  103.0 4.1 %collective-permute-done.17.refs_2_ = bf16[768,384]{1,0:T(8,128)(2,1)S(1)} collective-permute-done((bf16[768,384]{1,0:T(8,128)(2,1)S(1)}, bf16[768,384]{1,0:T(8,128)(2,1)S(1)}, u32[]{:S(2)}, u32[]{:S(2)}) %collective-permute-start.17) | collective-permute-done | bytes 589856 | tf_op jit(solution)/shard_map/ppermute | solution.py:39
  107.1 3.7 %collective-permute-done.16.refs_1_ = bf16[768,384]{1,0:T(8,128)(2,1)S(1)} collective-permute-done((bf16[768,384]{1,0:T(8,128)(2,1)S(1)}, bf16[768,384]{1,0:T(8,128)(2,1)S(1)}, u32[]{:S(2)}, u32[]{:S(2)}) %collective-permute-start.16) | collective-permute-done | bytes 589856 | tf_op jit(solution)/shard_map/ppermute | solution.py:35
  112.3 1.8 collective-permute-start.19
  114.1 4.9 %shard_map.31.refs_3_ = f32[768,1152]{1,0:T(8,128)S(1)} custom-call(s32[4]{0:T(128)S(1)} %pad_add_fusion.where_ref, bf16[768,384]{1,0:T(8,128)(2,1)S(1)} %shard_map.29.refs_0_, bf16[768,384]{1,0:T(8,128)(2,1)S(1)} %collective-permute-done.16.refs_1_, bf16[768,384]{1,0:T(8,128)(2,1)S(1)} %collective-permute-done.17.refs_2_, ...), custom_call_target="tpu_custom_call" | custom-call | tf_op jit(solution)/shard_map/pallas_call | solution.py:77
  119.0 5.0 %collective-permute-done.21.refs_1_.refs_5_ = bf16[768,384]{1,0:T(8,128)(2,1)S(1)} collective-permute-done((bf16[768,384]{1,0:T(8,128)(2,1)S(1)}, bf16[768,384]{1,0:T(8,128)(2,1)S(1)}, u32[]{:S(2)}, u32[]{:S(2)}) %collective-permute-start.21) | collective-permute-done | bytes 589856 | tf_op jit(solution)/shard_map/ppermute | solution.py:39
  124.0 2.4 %shard_map.32.refs_3_ = f32[768,1152]{1,0:T(8,128)S(1)} custom-call(s32[4]{0:T(128)S(1)} %pad_add_fusion.where_ref, bf16[768,384]{1,0:T(8,128)(2,1)S(1)} %collective-permute-done.20.refs_0_.refs_4_, bf16[768,384]{1,0:T(8,128)(2,1)S(1)} %collective-permute-done.21.refs_1_.refs_5_, bf16[8,384,1152]{2,1,0:T(8,128)(2,1)S(1)} %shard_map.30.refs_4_.refs_2_, ...), custom_call_target="tpu_custom_call" | custom-call | tf_op jit(solution)/shard_map/pallas_call | solution.py:77
  126.5 10.2 %collective-permute-done.19.refs_0_.refs_6_ = bf16[768,384]{1,0:T(8,128)(2,1)S(1)} collective-permute-done((bf16[768,384]{1,0:T(8,128)(2,1)S(1)}, bf16[768,384]{1,0:T(8,128)(2,1)S(1)}, u32[]{:S(2)}, u32[]{:S(2)}) %collective-permute-start.19) | collective-permute-done | bytes 589856 | tf_op jit(solution)/shard_map/ppermute | solution.py:39
  136.6 1.7 shard_map.33
  138.3 4.4 %collective-permute-start.23 = (bf16[384,1152]{1,0:T(8,128)(2,1)S(1)}, bf16[384,1152]{1,0:T(8,128)(2,1)S(1)}, u32[]{:S(2)}, u32[]{:S(2)}) collective-permute-start(bf16[384,1152]{1,0:T(8,128)(2,1)S(1)} %shard_map.33), channel_id=1, source_target_pairs={{0,8},{8,0},{1,9},{9,1},{2,10},{10,2},{3,11},{11,3},{4,12},{12,4},... | collective-permute-start | bytes 2654216 | tf_op jit(solution)/shard_map/ppermute | solution.py:31
  142.8 1.7 shard_map.34.m
  145.1 2.4 %collective-permute-start.26 = (bf16[384,1152]{1,0:T(8,128)(2,1)S(1)}, bf16[384,1152]{1,0:T(8,128)(2,1)S(1)}, u32[]{:S(2)}, u32[]{:S(2)}) collective-permute-start(bf16[384,1152]{1,0:T(8,128)(2,1)S(1)} %get-tuple-element.88.refs_0_), channel_id=1, source_target_pairs={{0,48},{8,24},{16,0},{24,40},{32,16},{40,56},{48,32},{56,8},{1,49}... | collective-permute-start | bytes 2654216 | tf_op jit(solution)/shard_map/ppermute | solution.py:56
  148.4 4.6 %shard_map.36.gram_ref = bf16[8,768,384]{2,1,0:T(8,128)(2,1)S(1)} custom-call(s32[4]{0:T(128)S(1)} %pad_add_fusion.where_ref, bf16[768,384]{1,0:T(8,128)(2,1)S(1)} %shard_map.29.refs_0_, bf16[768,384]{1,0:T(8,128)(2,1)S(1)} %collective-permute-done.16.refs_1_, bf16[768,384]{1,0:T(8,128)(2,1)S(1)} %collective-permute-done.17.refs_2_, ...), custom_call_target="tpu_custom_call" | custom-call | tf_op jit(solution)/shard_map/pallas_call | solution.py:77
  153.0 12.4 %collective-permute-done.26.refs_3_ = bf16[384,1152]{1,0:T(8,128)(2,1)S(1)} collective-permute-done((bf16[384,1152]{1,0:T(8,128)(2,1)S(1)}, bf16[384,1152]{1,0:T(8,128)(2,1)S(1)}, u32[]{:S(2)}, u32[]{:S(2)}) %collective-permute-start.26) | collective-permute-done | bytes 884768 | tf_op jit(solution)/shard_map/ppermute | solution.py:56
  165.4 2.6 %collective-permute-done.25.refs_2_ = bf16[384,1152]{1,0:T(8,128)(2,1)S(1)} collective-permute-done((bf16[384,1152]{1,0:T(8,128)(2,1)S(1)}, bf16[384,1152]{1,0:T(8,128)(2,1)S(1)}, u32[]{:S(2)}, u32[]{:S(2)}) %collective-permute-start.25) | collective-permute-done | bytes 884768 | tf_op jit(solution)/shard_map/ppermute | solution.py:23
  168.3 2.9 %collective-permute-start.27 = (bf16[384,1152]{1,0:T(8,128)(2,1)S(1)}, bf16[384,1152]{1,0:T(8,128)(2,1)S(1)}, u32[]{:S(2)}, u32[]{:S(2)}) collective-permute-start(bf16[384,1152]{1,0:T(8,128)(2,1)S(1)} %collective-permute-done.25.refs_2_), channel_id=1, source_target_pairs={{0,16},{8,56},{16,32},{24,8},{32,48},{40,24},{48,0},{56,40},{1,17}... | collective-permute-start | bytes 2654216 | tf_op jit(solution)/shard_map/ppermute | solution.py:56
  171.2 4.0 %shard_map.37.refs_0_ = f32[768,1152]{1,0:T(8,128)S(1)} custom-call(bf16[8,768,384]{2,1,0:T(8,128)(2,1)S(1)} %shard_map.36.gram_ref, bf16[384,1152]{1,0:T(8,128)(2,1)S(1)} %get-tuple-element.88.refs_0_, bf16[384,1152]{1,0:T(8,128)(2,1)S(1)} %collective-permute-done.24.refs_1_, bf16[384,1152]{1,0:T(8,128)(2,1)S(1)} %collective-permute-done.25.refs_2_, ...), custom_call_target="tpu_custom_call" | custom-call | tf_op jit(solution)/shard_map/pallas_call | solution.py:77
  175.2 12.9 %collective-permute-done.27.refs_2_ = bf16[384,1152]{1,0:T(8,128)(2,1)S(1)} collective-permute-done((bf16[384,1152]{1,0:T(8,128)(2,1)S(1)}, bf16[384,1152]{1,0:T(8,128)(2,1)S(1)}, u32[]{:S(2)}, u32[]{:S(2)}) %collective-permute-start.27) | collective-permute-done | bytes 884768 | tf_op jit(solution)/shard_map/ppermute | solution.py:56
  188.1 4.1 %collective-permute-done.29.refs_3_ = bf16[384,1152]{1,0:T(8,128)(2,1)S(1)} collective-permute-done((bf16[384,1152]{1,0:T(8,128)(2,1)S(1)}, bf16[384,1152]{1,0:T(8,128)(2,1)S(1)}, u32[]{:S(2)}, u32[]{:S(2)}) %collective-permute-start.29) | collective-permute-done | bytes 884768 | tf_op jit(solution)/shard_map/ppermute | solution.py:23
  192.7 3.3 %shard_map.38.refs_0_ = f32[768,1152]{1,0:T(8,128)S(1)} custom-call(bf16[8,768,384]{2,1,0:T(8,128)(2,1)S(1)} %shard_map.36.gram_ref, f32[768,1152]{1,0:T(8,128)S(1)} %shard_map.37.refs_0_, bf16[384,1152]{1,0:T(8,128)(2,1)S(1)} %collective-permute-done.28.refs_1_, bf16[384,1152]{1,0:T(8,128)(2,1)S(1)} %collective-permute-done.27.refs_2_, ...), custom_call_target="tpu_custom_call" | custom-call | tf_op jit(solution)/shard_map/pallas_call | solution.py:77
  196.0 8.9 %collective-permute-done.30.refs_1_ = bf16[384,1152]{1,0:T(8,128)(2,1)S(1)} collective-permute-done((bf16[384,1152]{1,0:T(8,128)(2,1)S(1)}, bf16[384,1152]{1,0:T(8,128)(2,1)S(1)}, u32[]{:S(2)}, u32[]{:S(2)}) %collective-permute-start.30) | collective-permute-done | bytes 884768 | tf_op jit(solution)/shard_map/ppermute | solution.py:56
  205.7 2.1 collective-permute-start.31
  209.8 1.5 shard_map.41
  (46 shorter events, 24.6 us)
Async XLA Ops:
  0.0 6.0 %collective-permute-start.1 = (bf16[384,1152]{1,0:T(8,128)(2,1)}, bf16[384,1152]{1,0:T(8,128)(2,1)S(1)}, u32[]{:S(2)}, u32[]{:S(2)}) collective-permute-start(bf16[384,1152]{1,0:T(8,128)(2,1)} %own_ref.17), channel_id=1, source_target_pairs={{0,8},{8,0},{1,9},{9,1},{2,10},{10,2},{3,11},{11,3},{4,12},{12,4},... | collective-permute-start | bytes 2654216 | tf_op jit(solution)/shard_map/ppermute | solution.py:31
  1.4 17.8 %collective-permute-start.3 = (bf16[384,1152]{1,0:T(8,128)(2,1)}, bf16[384,1152]{1,0:T(8,128)(2,1)S(1)}, u32[]{:S(2)}, u32[]{:S(2)}) collective-permute-start(bf16[384,1152]{1,0:T(8,128)(2,1)} %own_ref.17), channel_id=1, source_target_pairs={{0,48},{8,24},{16,0},{24,40},{32,16},{40,56},{48,32},{56,8},{1,49}... | collective-permute-start | bytes 2654216 | tf_op jit(solution)/shard_map/ppermute | solution.py:56
  2.8 20.0 %collective-permute-start.2 = (bf16[384,1152]{1,0:T(8,128)(2,1)}, bf16[384,1152]{1,0:T(8,128)(2,1)S(1)}, u32[]{:S(2)}, u32[]{:S(2)}) collective-permute-start(bf16[384,1152]{1,0:T(8,128)(2,1)} %own_ref.17), channel_id=1, source_target_pairs={{0,64},{64,0},{1,65},{65,1},{2,66},{66,2},{3,67},{67,3},{4,68},{68... | collective-permute-start | bytes 2654216 | tf_op jit(solution)/shard_map/ppermute | solution.py:23
  4.4 20.0 %collective-permute-start = (bf16[384,1152]{1,0:T(8,128)(2,1)}, bf16[384,1152]{1,0:T(8,128)(2,1)S(1)}, u32[]{:S(2)}, u32[]{:S(2)}) collective-permute-start(bf16[384,1152]{1,0:T(8,128)(2,1)} %own_ref.17), channel_id=1, source_target_pairs={{0,16},{8,56},{16,32},{24,8},{32,48},{40,24},{48,0},{56,40},{1,17}... | collective-permute-start | bytes 2654216 | tf_op jit(solution)/shard_map/ppermute | solution.py:56
  6.0 1.2 copy-start
  8.6 20.0 %copy-start.1 = (bf16[384,1152]{1,0:T(8,128)(2,1)S(1)}, bf16[384,1152]{1,0:T(8,128)(2,1)}, u32[]{:S(2)}) copy-start(bf16[384,1152]{1,0:T(8,128)(2,1)} %own_ref.17) | copy-start | bytes 2654212
  8.6 15.9 %collective-permute-start.4 = (bf16[2,2,48,768]{3,2,1,0:T(8,128)(2,1)S(1)}, bf16[2,2,48,768]{3,2,1,0:T(8,128)(2,1)S(1)}, u32[]{:S(2)}, u32[]{:S(2)}) collective-permute-start(bf16[2,2,48,768]{3,2,1,0:T(8,128)(2,1)S(1)} %shard_map.17), channel_id=1, source_target_pairs={{0,1},{1,0},{2,3},{3,2},{8,11},{9,10},{10,9},{11,8},{4,5},{5,4},{6... | collective-permute-start | bytes 884744 | tf_op jit(solution)/shard_map/ppermute | solution.py:47
  24.5 19.5 %collective-permute-start.5 = (bf16[384,1152]{1,0:T(8,128)(2,1)S(1)}, bf16[384,1152]{1,0:T(8,128)(2,1)S(1)}, u32[]{:S(2)}, u32[]{:S(2)}) collective-permute-start(bf16[384,1152]{1,0:T(8,128)(2,1)S(1)} %collective-permute-done.2.refs_1_.refs_2_), channel_id=1, source_target_pairs={{0,16},{8,56},{16,32},{24,8},{32,48},{40,24},{48,0},{56,40},{1,17}... | collective-permute-start | bytes 2654216 | tf_op jit(solution)/shard_map/ppermute | solution.py:56
  27.5 20.2 %collective-permute-start.7 = (bf16[384,1152]{1,0:T(8,128)(2,1)S(1)}, bf16[384,1152]{1,0:T(8,128)(2,1)S(1)}, u32[]{:S(2)}, u32[]{:S(2)}) collective-permute-start(bf16[384,1152]{1,0:T(8,128)(2,1)S(1)} %collective-permute-done.3.refs_2_.refs_3_), channel_id=1, source_target_pairs={{0,64},{64,0},{1,65},{65,1},{2,66},{66,2},{3,67},{67,3},{4,68},{68... | collective-permute-start | bytes 2654216 | tf_op jit(solution)/shard_map/ppermute | solution.py:23
  28.6 19.7 %collective-permute-start.6 = (bf16[384,1152]{1,0:T(8,128)(2,1)S(1)}, bf16[384,1152]{1,0:T(8,128)(2,1)S(1)}, u32[]{:S(2)}, u32[]{:S(2)}) collective-permute-start(bf16[384,1152]{1,0:T(8,128)(2,1)S(1)} %collective-permute-done.3.refs_2_.refs_3_), channel_id=1, source_target_pairs={{0,48},{8,24},{16,0},{24,40},{32,16},{40,56},{48,32},{56,8},{1,49}... | collective-permute-start | bytes 2654216 | tf_op jit(solution)/shard_map/ppermute | solution.py:56
  31.4 17.8 %collective-permute-start.8 = (bf16[2,2,144,768]{3,2,1,0:T(8,128)(2,1)S(1)}, bf16[2,2,144,768]{3,2,1,0:T(8,128)(2,1)S(1)}, u32[]{:S(2)}, u32[]{:S(2)}) collective-permute-start(bf16[2,2,144,768]{3,2,1,0:T(8,128)(2,1)S(1)} %shard_map.20), channel_id=1, source_target_pairs={{0,1},{1,0},{2,3},{3,2},{8,11},{9,10},{10,9},{11,8},{4,5},{5,4},{6... | collective-permute-start | bytes 2654216 | tf_op jit(solution)/shard_map/ppermute | solution.py:47
  48.3 12.2 %collective-permute-start.9 = (bf16[384,1152]{1,0:T(8,128)(2,1)S(1)}, bf16[384,1152]{1,0:T(8,128)(2,1)S(1)}, u32[]{:S(2)}, u32[]{:S(2)}) collective-permute-start(bf16[384,1152]{1,0:T(8,128)(2,1)S(1)} %collective-permute-done.5.refs_1_.refs_5_), channel_id=1, source_target_pairs={{0,16},{8,56},{16,32},{24,8},{32,48},{40,24},{48,0},{56,40},{1,17}... | collective-permute-start | bytes 2654216 | tf_op jit(solution)/shard_map/ppermute | solution.py:56
  49.4 10.5 %collective-permute-start.10 = (bf16[2,192,768]{2,1,0:T(8,128)(2,1)S(1)}, bf16[2,192,768]{2,1,0:T(8,128)(2,1)S(1)}, u32[]{:S(2)}, u32[]{:S(2)}) collective-permute-start(bf16[2,192,768]{2,1,0:T(8,128)(2,1)S(1)} %get-tuple-element.64), channel_id=1, source_target_pairs={{0,3},{1,2},{2,1},{3,0},{8,9},{9,8},{10,11},{11,10},{4,7},{5,6},{6... | collective-permute-start | bytes 1769480 | tf_op jit(solution)/shard_map/ppermute | solution.py:47
  53.4 15.0 %collective-permute-start.11 = (bf16[2,2,144,768]{3,2,1,0:T(8,128)(2,1)S(1)}, bf16[2,2,144,768]{3,2,1,0:T(8,128)(2,1)S(1)}, u32[]{:S(2)}, u32[]{:S(2)}) collective-permute-start(bf16[2,2,144,768]{3,2,1,0:T(8,128)(2,1)S(1)} %shard_map.23), channel_id=1, source_target_pairs={{0,1},{1,0},{2,3},{3,2},{8,11},{9,10},{10,9},{11,8},{4,5},{5,4},{6... | collective-permute-start | bytes 2654216 | tf_op jit(solution)/shard_map/ppermute | solution.py:47
  62.0 9.6 %collective-permute-start.12 = (bf16[2,2,48,768]{3,2,1,0:T(8,128)(2,1)S(1)}, bf16[2,2,48,768]{3,2,1,0:T(8,128)(2,1)S(1)}, u32[]{:S(2)}, u32[]{:S(2)}) collective-permute-start(bf16[2,2,48,768]{3,2,1,0:T(8,128)(2,1)S(1)} %shard_map.25), channel_id=1, source_target_pairs={{0,1},{1,0},{2,3},{3,2},{8,11},{9,10},{10,9},{11,8},{4,5},{5,4},{6... | collective-permute-start | bytes 884744 | tf_op jit(solution)/shard_map/ppermute | solution.py:47
  71.8 9.1 %collective-permute-start.13 = (bf16[2,192,768]{2,1,0:T(8,128)(2,1)S(1)}, bf16[2,192,768]{2,1,0:T(8,128)(2,1)S(1)}, u32[]{:S(2)}, u32[]{:S(2)}) collective-permute-start(bf16[2,192,768]{2,1,0:T(8,128)(2,1)S(1)} %get-tuple-element.72), channel_id=1, source_target_pairs={{0,3},{1,2},{2,1},{3,0},{8,9},{9,8},{10,11},{11,10},{4,7},{5,6},{6... | collective-permute-start | bytes 1769480 | tf_op jit(solution)/shard_map/ppermute | solution.py:47
  72.3 8.3 %collective-permute-start.14 = (bf16[192,768]{1,0:T(8,128)(2,1)S(1)}, bf16[192,768]{1,0:T(8,128)(2,1)S(1)}, u32[]{:S(2)}, u32[]{:S(2)}) collective-permute-start(bf16[192,768]{1,0:T(8,128)(2,1)S(1)} %shard_map.27), channel_id=1, source_target_pairs={{0,4},{4,0},{1,5},{5,1},{2,6},{6,2},{3,7},{7,3},{8,12},{12,8},{9,1... | collective-permute-start | bytes 884744 | tf_op jit(solution)/shard_map/ppermute | solution.py:27
  81.0 8.5 %collective-permute-start.15 = (bf16[192,768]{1,0:T(8,128)(2,1)S(1)}, bf16[192,768]{1,0:T(8,128)(2,1)S(1)}, u32[]{:S(2)}, u32[]{:S(2)}) collective-permute-start(bf16[192,768]{1,0:T(8,128)(2,1)S(1)} %shard_map.28), channel_id=1, source_target_pairs={{0,4},{4,0},{1,5},{5,1},{2,6},{6,2},{3,7},{7,3},{8,12},{12,8},{9,1... | collective-permute-start | bytes 884744 | tf_op jit(solution)/shard_map/ppermute | solution.py:27
  89.9 13.1 %collective-permute-start.18 = (bf16[768,384]{1,0:T(8,128)(2,1)S(1)}, bf16[768,384]{1,0:T(8,128)(2,1)S(1)}, u32[]{:S(2)}, u32[]{:S(2)}) collective-permute-start(bf16[768,384]{1,0:T(8,128)(2,1)S(1)} %shard_map.29.refs_0_), channel_id=1, source_target_pairs={{0,4},{4,0},{1,5},{5,1},{2,6},{6,2},{3,7},{7,3},{8,12},{12,8},{9,1... | collective-permute-start | bytes 1769480 | tf_op jit(solution)/shard_map/ppermute | solution.py:27
  92.9 14.2 %collective-permute-start.17 = (bf16[768,384]{1,0:T(8,128)(2,1)S(1)}, bf16[768,384]{1,0:T(8,128)(2,1)S(1)}, u32[]{:S(2)}, u32[]{:S(2)}) collective-permute-start(bf16[768,384]{1,0:T(8,128)(2,1)S(1)} %shard_map.29.refs_0_), channel_id=1, source_target_pairs={{0,3},{1,2},{2,1},{3,0},{4,7},{5,6},{6,5},{7,4},{8,11},{9,10},{10,... | collective-permute-start | bytes 1769480 | tf_op jit(solution)/shard_map/ppermute | solution.py:39
  96.5 14.3 %collective-permute-start.16 = (bf16[768,384]{1,0:T(8,128)(2,1)S(1)}, bf16[768,384]{1,0:T(8,128)(2,1)S(1)}, u32[]{:S(2)}, u32[]{:S(2)}) collective-permute-start(bf16[768,384]{1,0:T(8,128)(2,1)S(1)} %shard_map.29.refs_0_), channel_id=1, source_target_pairs={{0,1},{1,0},{2,3},{3,2},{4,5},{5,4},{6,7},{7,6},{8,9},{9,8},{10,11... | collective-permute-start | bytes 1769480 | tf_op jit(solution)/shard_map/ppermute | solution.py:35
  110.8 13.2 %collective-permute-start.21 = (bf16[768,384]{1,0:T(8,128)(2,1)S(1)}, bf16[768,384]{1,0:T(8,128)(2,1)S(1)}, u32[]{:S(2)}, u32[]{:S(2)}) collective-permute-start(bf16[768,384]{1,0:T(8,128)(2,1)S(1)} %collective-permute-done.18.refs_3_), channel_id=1, source_target_pairs={{0,3},{1,2},{2,1},{3,0},{4,7},{5,6},{6,5},{7,4},{8,11},{9,10},{10,... | collective-permute-start | bytes 1769480 | tf_op jit(solution)/shard_map/ppermute | solution.py:39
  111.7 12.3 %collective-permute-start.20 = (bf16[768,384]{1,0:T(8,128)(2,1)S(1)}, bf16[768,384]{1,0:T(8,128)(2,1)S(1)}, u32[]{:S(2)}, u32[]{:S(2)}) collective-permute-start(bf16[768,384]{1,0:T(8,128)(2,1)S(1)} %collective-permute-done.18.refs_3_), channel_id=1, source_target_pairs={{0,1},{1,0},{2,3},{3,2},{4,5},{5,4},{6,7},{7,6},{8,9},{9,8},{10,11... | collective-permute-start | bytes 1769480 | tf_op jit(solution)/shard_map/ppermute | solution.py:35
  112.3 24.3 %collective-permute-start.19 = (bf16[768,384]{1,0:T(8,128)(2,1)S(1)}, bf16[768,384]{1,0:T(8,128)(2,1)S(1)}, u32[]{:S(2)}, u32[]{:S(2)}) collective-permute-start(bf16[768,384]{1,0:T(8,128)(2,1)S(1)} %collective-permute-done.16.refs_1_), channel_id=1, source_target_pairs={{0,3},{1,2},{2,1},{3,0},{4,7},{5,6},{6,5},{7,4},{8,11},{9,10},{10,... | collective-permute-start | bytes 1769480 | tf_op jit(solution)/shard_map/ppermute | solution.py:39
  124.0 12.6 %collective-permute-start.22 = (bf16[768,384]{1,0:T(8,128)(2,1)S(1)}, bf16[768,384]{1,0:T(8,128)(2,1)S(1)}, u32[]{:S(2)}, u32[]{:S(2)}) collective-permute-start(bf16[768,384]{1,0:T(8,128)(2,1)S(1)} %collective-permute-done.21.refs_1_.refs_5_), channel_id=1, source_target_pairs={{0,1},{1,0},{2,3},{3,2},{4,5},{5,4},{6,7},{7,6},{8,9},{9,8},{10,11... | collective-permute-start | bytes 1769480 | tf_op jit(solution)/shard_map/ppermute | solution.py:35
  138.3 6.5 %collective-permute-start.23 = (bf16[384,1152]{1,0:T(8,128)(2,1)S(1)}, bf16[384,1152]{1,0:T(8,128)(2,1)S(1)}, u32[]{:S(2)}, u32[]{:S(2)}) collective-permute-start(bf16[384,1152]{1,0:T(8,128)(2,1)S(1)} %shard_map.33), channel_id=1, source_target_pairs={{0,8},{8,0},{1,9},{9,1},{2,10},{10,2},{3,11},{11,3},{4,12},{12,4},... | collective-permute-start | bytes 2654216 | tf_op jit(solution)/shard_map/ppermute | solution.py:31
  145.1 20.3 %collective-permute-start.26 = (bf16[384,1152]{1,0:T(8,128)(2,1)S(1)}, bf16[384,1152]{1,0:T(8,128)(2,1)S(1)}, u32[]{:S(2)}, u32[]{:S(2)}) collective-permute-start(bf16[384,1152]{1,0:T(8,128)(2,1)S(1)} %get-tuple-element.88.refs_0_), channel_id=1, source_target_pairs={{0,48},{8,24},{16,0},{24,40},{32,16},{40,56},{48,32},{56,8},{1,49}... | collective-permute-start | bytes 2654216 | tf_op jit(solution)/shard_map/ppermute | solution.py:56
  147.6 20.4 %collective-permute-start.25 = (bf16[384,1152]{1,0:T(8,128)(2,1)S(1)}, bf16[384,1152]{1,0:T(8,128)(2,1)S(1)}, u32[]{:S(2)}, u32[]{:S(2)}) collective-permute-start(bf16[384,1152]{1,0:T(8,128)(2,1)S(1)} %get-tuple-element.88.refs_0_), channel_id=1, source_target_pairs={{0,64},{64,0},{1,65},{65,1},{2,66},{66,2},{3,67},{67,3},{4,68},{68... | collective-permute-start | bytes 2654216 | tf_op jit(solution)/shard_map/ppermute | solution.py:23
  147.9 20.4 %collective-permute-start.24 = (bf16[384,1152]{1,0:T(8,128)(2,1)S(1)}, bf16[384,1152]{1,0:T(8,128)(2,1)S(1)}, u32[]{:S(2)}, u32[]{:S(2)}) collective-permute-start(bf16[384,1152]{1,0:T(8,128)(2,1)S(1)} %get-tuple-element.88.refs_0_), channel_id=1, source_target_pairs={{0,16},{8,56},{16,32},{24,8},{32,48},{40,24},{48,0},{56,40},{1,17}... | collective-permute-start | bytes 2654216 | tf_op jit(solution)/shard_map/ppermute | solution.py:56
  168.3 19.8 %collective-permute-start.27 = (bf16[384,1152]{1,0:T(8,128)(2,1)S(1)}, bf16[384,1152]{1,0:T(8,128)(2,1)S(1)}, u32[]{:S(2)}, u32[]{:S(2)}) collective-permute-start(bf16[384,1152]{1,0:T(8,128)(2,1)S(1)} %collective-permute-done.25.refs_2_), channel_id=1, source_target_pairs={{0,16},{8,56},{16,32},{24,8},{32,48},{40,24},{48,0},{56,40},{1,17}... | collective-permute-start | bytes 2654216 | tf_op jit(solution)/shard_map/ppermute | solution.py:56
  171.2 21.0 %collective-permute-start.29 = (bf16[384,1152]{1,0:T(8,128)(2,1)S(1)}, bf16[384,1152]{1,0:T(8,128)(2,1)S(1)}, u32[]{:S(2)}, u32[]{:S(2)}) collective-permute-start(bf16[384,1152]{1,0:T(8,128)(2,1)S(1)} %collective-permute-done.26.refs_3_), channel_id=1, source_target_pairs={{0,64},{64,0},{1,65},{65,1},{2,66},{66,2},{3,67},{67,3},{4,68},{68... | collective-permute-start | bytes 2654216 | tf_op jit(solution)/shard_map/ppermute | solution.py:23
  171.2 21.4 %collective-permute-start.28 = (bf16[384,1152]{1,0:T(8,128)(2,1)S(1)}, bf16[384,1152]{1,0:T(8,128)(2,1)S(1)}, u32[]{:S(2)}, u32[]{:S(2)}) collective-permute-start(bf16[384,1152]{1,0:T(8,128)(2,1)S(1)} %collective-permute-done.26.refs_3_), channel_id=1, source_target_pairs={{0,48},{8,24},{16,0},{24,40},{32,16},{40,56},{48,32},{56,8},{1,49}... | collective-permute-start | bytes 2654216 | tf_op jit(solution)/shard_map/ppermute | solution.py:56
  192.7 12.2 %collective-permute-start.30 = (bf16[384,1152]{1,0:T(8,128)(2,1)S(1)}, bf16[384,1152]{1,0:T(8,128)(2,1)S(1)}, u32[]{:S(2)}, u32[]{:S(2)}) collective-permute-start(bf16[384,1152]{1,0:T(8,128)(2,1)S(1)} %collective-permute-done.27.refs_2_), channel_id=1, source_target_pairs={{0,16},{8,56},{16,32},{24,8},{32,48},{40,24},{48,0},{56,40},{1,17}... | collective-permute-start | bytes 2654216 | tf_op jit(solution)/shard_map/ppermute | solution.py:56
  205.7 4.1 %collective-permute-start.31 = (bf16[384,1152]{1,0:T(8,128)(2,1)S(1)}, bf16[384,1152]{1,0:T(8,128)(2,1)S(1)}, u32[]{:S(2)}, u32[]{:S(2)}) collective-permute-start(bf16[384,1152]{1,0:T(8,128)(2,1)S(1)} %shard_map.39), channel_id=1, source_target_pairs={{0,8},{8,0},{1,9},{9,1},{2,10},{10,2},{3,11},{11,3},{4,12},{12,4},... | collective-permute-start | bytes 2654216 | tf_op jit(solution)/shard_map/ppermute | solution.py:31

commit v4 on v3

--- a/solution.py
+++ b/solution.py
@@ -98,13 +98,13 @@
     return started
 
 
-def terms_of(where, own, sibling, arrays, send):
-    rows, depth = own.shape
+def terms_of(where, right, arrays, send):
+    rows, depth = arrays[0].shape
     eighth = rows // 8
     count = len(arrays)
     copies = [(i, 0, i * rows, rows) for i in range(count)]
 
-    def kernel(where_ref, own_ref, sib_ref, *refs):
+    def kernel(where_ref, right_ref, *refs):
         refs, out, panel, sems = refs[:-3], refs[-3], refs[-2], refs[-1]
         for copy in start_copies(copies, refs, panel, sems):
             copy.wait()
@@ -115,23 +115,19 @@
                 first = pl.multiple_of(p * rows + x * 2 * eighth, 2 * eighth)
                 parts.append(panel[pl.ds(first, 2 * eighth)])
         left = jnp.concatenate(parts, axis=0)
-        for i, right in enumerate((own_ref, sib_ref)):
-            value = lax.dot_general(
-                left, right[...], (((1,), (1,)), ((), ())), preferred_element_type=f32
-            ).astype(out.dtype)
-            for slot in range(2):
-                for p in range(count):
-                    for z in range(2):
-                        first = ((slot * count + p) * 2 + z) * eighth
-                        h = jnp.bitwise_xor(where_ref[1], z)
-                        target = (slot, h, slice(p * eighth, (p + 1) * eighth), slice(i * rows, (i + 1) * rows))
-                        out[target] = value[first : first + eighth]
+        value = jnp.dot(left, right_ref[...], preferred_element_type=f32).astype(out.dtype)
+        for slot in range(2):
+            for p in range(count):
+                for z in range(2):
+                    first = ((slot * count + p) * 2 + z) * eighth
+                    h = jnp.bitwise_xor(where_ref[1], z)
+                    out[slot, h, p * eighth : (p + 1) * eighth] = value[first : first + eighth]
 
     return call(
         kernel, jax.ShapeDtypeStruct((2, 2, count * eighth, 2 * rows), bf16 if send else f32),
-        [SM, VM, VM] + [HBM] * count,
+        [SM, VM] + [HBM] * count,
         [pltpu.VMEM((count * rows, depth), bf16), pltpu.SemaphoreType.DMA((count,))],
-        where, own, sibling, *arrays,
+        where, right, *arrays,
     )
 
 
@@ -323,12 +319,14 @@
     x = {}
 
     def terms(keys, send):
-        return terms_of(where, own, w, [x[key] for key in keys], send)
+        return terms_of(where, right, [x[key] for key in keys], send)
 
     z = swap_zl(own)
     r0 = along_y(own)
     r1 = along_y(own, False)
     w = swap_core(own)
+    both = jnp.concatenate(together(own, w), axis=0)
+    right = both.T
     x[0, "v"] = own
     got0 = partner(terms(OWN, True), True)
     keep0 = terms(OWN, False)

time: 211 us -> 214 us (1.014)
  starting transfers between devices: 56.4 us -> 59.6 us
  waiting for transfers between devices: 107 us -> 104 us
  local copies, waits for them, and re-layouts: 1.18 us -> 3.59 us
  Pallas kernels: 46.9 us -> 44.7 us
    ppermute x10, waiting for transfers between devices: 51.8 us -> 48.3 us  [along_y(): return lax.ppermute(v, ('y', 'c'), pairs)]
    pallas_call x24, Pallas kernels: 43.9 us -> 41.7 us  [call(): pl.pallas_call(kernel, out_shape=out_shape, in_specs=in_specs, out_specs=...]
  transfers between devices with their start and end apart: 32 -> 32, of which waited for: 27 -> 26; matrix products, arithmetic and copies ran while one was open for 0% -> 1% of each run, Pallas kernels for 20% -> 19%
where the time goes in v4:
time: 214 us
  waiting for transfers between devices  104 us (49%)
  starting transfers between devices  59.6 us (28%)
  Pallas kernels  44.7 us (21%)
  local copies, waits for them, and re-layouts  3.59 us (2%)
    ppermute x10, waiting for transfers between devices, along_y(): return lax.ppermute(v, ('y', 'c'), pairs)  48.3 us
    pallas_call x24, Pallas kernels, call(): pl.pallas_call(kernel, out_shape=out_shape, in_specs=in_specs, out_specs=...  41.7 us
    ppermute x3, waiting for transfers between devices, swap_x3(): return lax.ppermute(v, 'x', [(i, i ^ 3) for i in range(4)])  18.4 us
    ppermute x10, starting transfers between devices, along_y(): return lax.ppermute(v, ('y', 'c'), pairs)  14.3 us
    ppermute x4, waiting for transfers between devices, swap_zl(): return lax.ppermute(v, 'zl', [(0, 1), (1, 0)])  14.1 us
    ppermute x6, starting transfers between devices, partner(): return lax.ppermute(v, ('c', 'x'), pairs)  13.1 us
    ppermute x3, starting transfers between devices, swap_zh(): return lax.ppermute(v, 'zh', [(0, 1), (1, 0)])  10.5 us
    ppermute x3, waiting for transfers between devices, swap_zh(): return lax.ppermute(v, 'zh', [(0, 1), (1, 0)])  10 us
  transfers between devices with their start and end apart: 32, of which 26 were waited for; matrix products, arithmetic and copies ran while one was open for 1% of the time, Pallas kernels for 19%

profile of v4, /device:TPU:1, one launch (start us, length us, event | category | flops | bytes accessed | tf_op | source)
XLA Modules:
  0.0 213.9 jit_solution(12667790390060426096)
XLA Ops:
  0.0 2.3 %copy.2 = bf16[384,1152]{0,1:T(8,128)(2,1)} copy(bf16[384,1152]{1,0:T(8,128)(2,1)} %own_ref.1) | data formatting | bytes 1769472 | tf_op args[0]
  5.1 1.6 collective-permute-start.2
  9.6 1.6 maximum_bitcast_fusion.right_ref
  12.4 2.6 %collective-permute-start.4 = (bf16[2,2,48,768]{3,2,1,0:T(8,128)(2,1)S(1)}, bf16[2,2,48,768]{3,2,1,0:T(8,128)(2,1)S(1)}, u32[]{:S(2)}, u32[]{:S(2)}) collective-permute-start(bf16[2,2,48,768]{3,2,1,0:T(8,128)(2,1)S(1)} %shard_map.17), channel_id=1, source_target_pairs={{0,1},{1,0},{2,3},{3,2},{8,11},{9,10},{10,9},{11,8},{4,5},{5,4},{6... | collective-permute-start | bytes 884744 | tf_op jit(solution)/shard_map/ppermute | solution.py:47
  16.3 5.0 %collective-permute-done.3.refs_2_.refs_3_ = bf16[384,1152]{1,0:T(8,128)(2,1)S(1)} collective-permute-done((bf16[384,1152]{1,0:T(8,128)(2,1)S(1)}, bf16[384,1152]{1,0:T(8,128)(2,1)S(1)}, u32[]{:S(2)}, u32[]{:S(2)}) %collective-permute-start.3) | collective-permute-done | bytes 884768 | tf_op jit(solution)/shard_map/ppermute | solution.py:56
  21.3 3.5 %collective-permute-done.2.refs_1_.refs_2_ = bf16[384,1152]{1,0:T(8,128)(2,1)S(1)} collective-permute-done((bf16[384,1152]{1,0:T(8,128)(2,1)S(1)}, bf16[384,1152]{1,0:T(8,128)(2,1)S(1)}, u32[]{:S(2)}, u32[]{:S(2)}) %collective-permute-start.2) | collective-permute-done | bytes 884768 | tf_op jit(solution)/shard_map/ppermute | solution.py:23
  24.8 1.6 collective-permute-done.refs_0_.refs_1_
  26.5 3.1 %collective-permute-start.5 = (bf16[384,1152]{1,0:T(8,128)(2,1)S(1)}, bf16[384,1152]{1,0:T(8,128)(2,1)S(1)}, u32[]{:S(2)}, u32[]{:S(2)}) collective-permute-start(bf16[384,1152]{1,0:T(8,128)(2,1)S(1)} %collective-permute-done.2.refs_1_.refs_2_), channel_id=1, source_target_pairs={{0,16},{8,56},{16,32},{24,8},{32,48},{40,24},{48,0},{56,40},{1,17}... | collective-permute-start | bytes 2654216 | tf_op jit(solution)/shard_map/ppermute | solution.py:56
  30.8 2.4 %shard_map.20 = bf16[2,2,144,768]{3,2,1,0:T(8,128)(2,1)S(1)} custom-call(s32[4]{0:T(128)S(1)} %pad_add_fusion.where_ref, bf16[1152,768]{1,0:T(8,128)(2,1)S(1)} %maximum_bitcast_fusion.right_ref, bf16[384,1152]{1,0:T(8,128)(2,1)S(1)} %collective-permute-done.refs_0_.refs_1_, bf16[384,1152]{1,0:T(8,128)(2,1)S(1)} %collective-permute-done.2.refs_1_.refs_2_, ...), custom_call_target="tpu_custom_call" | custom-call | tf_op jit(solution)/shard_map/pallas_call | solution.py:77
  33.3 2.5 %collective-permute-start.8 = (bf16[2,2,144,768]{3,2,1,0:T(8,128)(2,1)S(1)}, bf16[2,2,144,768]{3,2,1,0:T(8,128)(2,1)S(1)}, u32[]{:S(2)}, u32[]{:S(2)}) collective-permute-start(bf16[2,2,144,768]{3,2,1,0:T(8,128)(2,1)S(1)} %shard_map.20), channel_id=1, source_target_pairs={{0,1},{1,0},{2,3},{3,2},{8,11},{9,10},{10,9},{11,8},{4,5},{5,4},{6... | collective-permute-start | bytes 2654216 | tf_op jit(solution)/shard_map/ppermute | solution.py:47
  35.8 2.4 %shard_map.19.refs_2_ = f32[2,2,144,768]{3,2,1,0:T(8,128)S(1)} custom-call(s32[4]{0:T(128)S(1)} %pad_add_fusion.where_ref, bf16[1152,768]{1,0:T(8,128)(2,1)S(1)} %maximum_bitcast_fusion.right_ref, bf16[384,1152]{1,0:T(8,128)(2,1)S(1)} %collective-permute-done.refs_0_.refs_1_, bf16[384,1152]{1,0:T(8,128)(2,1)S(1)} %collective-permute-done.2.refs_1_.refs_2_, ...), custom_call_target="tpu_custom_call" | custom-call | tf_op jit(solution)/shard_map/pallas_call | solution.py:77
  38.2 7.9 %collective-permute-done.5.refs_1_.refs_5_ = bf16[384,1152]{1,0:T(8,128)(2,1)S(1)} collective-permute-done((bf16[384,1152]{1,0:T(8,128)(2,1)S(1)}, bf16[384,1152]{1,0:T(8,128)(2,1)S(1)}, u32[]{:S(2)}, u32[]{:S(2)}) %collective-permute-start.5) | collective-permute-done | bytes 884768 | tf_op jit(solution)/shard_map/ppermute | solution.py:56
  46.1 3.7 %collective-permute-done.7.refs_2_.refs_6_ = bf16[384,1152]{1,0:T(8,128)(2,1)S(1)} collective-permute-done((bf16[384,1152]{1,0:T(8,128)(2,1)S(1)}, bf16[384,1152]{1,0:T(8,128)(2,1)S(1)}, u32[]{:S(2)}, u32[]{:S(2)}) %collective-permute-start.7) | collective-permute-done | bytes 884768 | tf_op jit(solution)/shard_map/ppermute | solution.py:23
  52.8 2.4 %shard_map.23 = bf16[2,2,144,768]{3,2,1,0:T(8,128)(2,1)S(1)} custom-call(s32[4]{0:T(128)S(1)} %pad_add_fusion.where_ref, bf16[1152,768]{1,0:T(8,128)(2,1)S(1)} %maximum_bitcast_fusion.right_ref, bf16[384,1152]{1,0:T(8,128)(2,1)S(1)} %collective-permute-done.6.refs_0_.refs_4_, bf16[384,1152]{1,0:T(8,128)(2,1)S(1)} %collective-permute-done.5.refs_1_.refs_5_, ...), custom_call_target="tpu_custom_call" | custom-call | tf_op jit(solution)/shard_map/pallas_call | solution.py:77
  55.2 1.9 collective-permute-start.11
  57.1 2.4 %shard_map.22.refs_0_ = f32[2,2,144,768]{3,2,1,0:T(8,128)S(1)} custom-call(s32[4]{0:T(128)S(1)} %pad_add_fusion.where_ref, bf16[1152,768]{1,0:T(8,128)(2,1)S(1)} %maximum_bitcast_fusion.right_ref, bf16[384,1152]{1,0:T(8,128)(2,1)S(1)} %collective-permute-done.6.refs_0_.refs_4_, bf16[384,1152]{1,0:T(8,128)(2,1)S(1)} %collective-permute-done.5.refs_1_.refs_5_, ...), custom_call_target="tpu_custom_call" | custom-call | tf_op jit(solution)/shard_map/pallas_call | solution.py:77
  59.6 2.9 %collective-permute-done.10.refs_1_ = bf16[2,192,768]{2,1,0:T(8,128)(2,1)S(1)} collective-permute-done((bf16[2,192,768]{2,1,0:T(8,128)(2,1)S(1)}, bf16[2,192,768]{2,1,0:T(8,128)(2,1)S(1)}, u32[]{:S(2)}, u32[]{:S(2)}) %collective-permute-start.10) | collective-permute-done | bytes 589856 | tf_op jit(solution)/shard_map/ppermute | solution.py:47
  63.9 4.4 %collective-permute-start.12 = (bf16[2,2,48,768]{3,2,1,0:T(8,128)(2,1)S(1)}, bf16[2,2,48,768]{3,2,1,0:T(8,128)(2,1)S(1)}, u32[]{:S(2)}, u32[]{:S(2)}) collective-permute-start(bf16[2,2,48,768]{3,2,1,0:T(8,128)(2,1)S(1)} %shard_map.25), channel_id=1, source_target_pairs={{0,1},{1,0},{2,3},{3,2},{8,11},{9,10},{10,9},{11,8},{4,5},{5,4},{6... | collective-permute-start | bytes 884744 | tf_op jit(solution)/shard_map/ppermute | solution.py:47
  70.5 3.2 %collective-permute-done.12.refs_3_ = bf16[2,2,48,768]{3,2,1,0:T(8,128)(2,1)S(1)} collective-permute-done((bf16[2,2,48,768]{3,2,1,0:T(8,128)(2,1)S(1)}, bf16[2,2,48,768]{3,2,1,0:T(8,128)(2,1)S(1)}, u32[]{:S(2)}, u32[]{:S(2)}) %collective-permute-start.12) | collective-permute-done | bytes 294944 | tf_op jit(solution)/shard_map/ppermute | solution.py:47
  74.2 3.7 %collective-permute-start.14 = (bf16[192,768]{1,0:T(8,128)(2,1)S(1)}, bf16[192,768]{1,0:T(8,128)(2,1)S(1)}, u32[]{:S(2)}, u32[]{:S(2)}) collective-permute-start(bf16[192,768]{1,0:T(8,128)(2,1)S(1)} %shard_map.27), channel_id=1, source_target_pairs={{0,4},{4,0},{1,5},{5,1},{2,6},{6,2},{3,7},{7,3},{8,12},{12,8},{9,1... | collective-permute-start | bytes 884744 | tf_op jit(solution)/shard_map/ppermute | solution.py:27
  77.9 4.5 %collective-permute-done.14.refs_4_ = bf16[192,768]{1,0:T(8,128)(2,1)S(1)} collective-permute-done((bf16[192,768]{1,0:T(8,128)(2,1)S(1)}, bf16[192,768]{1,0:T(8,128)(2,1)S(1)}, u32[]{:S(2)}, u32[]{:S(2)}) %collective-permute-start.14) | collective-permute-done | bytes 294944 | tf_op jit(solution)/shard_map/ppermute | solution.py:27
  83.0 3.9 %collective-permute-start.15 = (bf16[192,768]{1,0:T(8,128)(2,1)S(1)}, bf16[192,768]{1,0:T(8,128)(2,1)S(1)}, u32[]{:S(2)}, u32[]{:S(2)}) collective-permute-start(bf16[192,768]{1,0:T(8,128)(2,1)S(1)} %shard_map.28), channel_id=1, source_target_pairs={{0,4},{4,0},{1,5},{5,1},{2,6},{6,2},{3,7},{7,3},{8,12},{12,8},{9,1... | collective-permute-start | bytes 884744 | tf_op jit(solution)/shard_map/ppermute | solution.py:27
  86.8 4.7 %collective-permute-done.15.refs_5_ = bf16[192,768]{1,0:T(8,128)(2,1)S(1)} collective-permute-done((bf16[192,768]{1,0:T(8,128)(2,1)S(1)}, bf16[192,768]{1,0:T(8,128)(2,1)S(1)}, u32[]{:S(2)}, u32[]{:S(2)}) %collective-permute-start.15) | collective-permute-done | bytes 294944 | tf_op jit(solution)/shard_map/ppermute | solution.py:27
  91.9 2.9 %collective-permute-start.18 = (bf16[768,384]{1,0:T(8,128)(2,1)S(1)}, bf16[768,384]{1,0:T(8,128)(2,1)S(1)}, u32[]{:S(2)}, u32[]{:S(2)}) collective-permute-start(bf16[768,384]{1,0:T(8,128)(2,1)S(1)} %shard_map.29.refs_0_), channel_id=1, source_target_pairs={{0,4},{4,0},{1,5},{5,1},{2,6},{6,2},{3,7},{7,3},{8,12},{12,8},{9,1... | collective-permute-start | bytes 1769480 | tf_op jit(solution)/shard_map/ppermute | solution.py:27
  94.8 3.2 %collective-permute-start.17 = (bf16[768,384]{1,0:T(8,128)(2,1)S(1)}, bf16[768,384]{1,0:T(8,128)(2,1)S(1)}, u32[]{:S(2)}, u32[]{:S(2)}) collective-permute-start(bf16[768,384]{1,0:T(8,128)(2,1)S(1)} %shard_map.29.refs_0_), channel_id=1, source_target_pairs={{0,3},{1,2},{2,1},{3,0},{4,7},{5,6},{6,5},{7,4},{8,11},{9,10},{10,... | collective-permute-start | bytes 1769480 | tf_op jit(solution)/shard_map/ppermute | solution.py:39
  98.0 3.2 %collective-permute-start.16 = (bf16[768,384]{1,0:T(8,128)(2,1)S(1)}, bf16[768,384]{1,0:T(8,128)(2,1)S(1)}, u32[]{:S(2)}, u32[]{:S(2)}) collective-permute-start(bf16[768,384]{1,0:T(8,128)(2,1)S(1)} %shard_map.29.refs_0_), channel_id=1, source_target_pairs={{0,1},{1,0},{2,3},{3,2},{4,5},{5,4},{6,7},{7,6},{8,9},{9,8},{10,11... | collective-permute-start | bytes 1769480 | tf_op jit(solution)/shard_map/ppermute | solution.py:35
  101.1 3.0 %shard_map.30.refs_4_.refs_2_ = bf16[8,384,1152]{2,1,0:T(8,128)(2,1)S(1)} custom-call(bf16[384,1152]{1,0:T(8,128)(2,1)S(1)} %copy-done, bf16[384,1152]{1,0:T(8,128)(2,1)S(1)} %collective-permute-done.refs_0_.refs_1_, bf16[384,1152]{1,0:T(8,128)(2,1)S(1)} %collective-permute-done.2.refs_1_.refs_2_, ...), custom_call_target="tpu_custom_call" | custom-call | tf_op jit(solution)/shard_map/pallas_call | solution.py:198
  105.0 3.2 %collective-permute-done.17.refs_2_ = bf16[768,384]{1,0:T(8,128)(2,1)S(1)} collective-permute-done((bf16[768,384]{1,0:T(8,128)(2,1)S(1)}, bf16[768,384]{1,0:T(8,128)(2,1)S(1)}, u32[]{:S(2)}, u32[]{:S(2)}) %collective-permute-start.17) | collective-permute-done | bytes 589856 | tf_op jit(solution)/shard_map/ppermute | solution.py:39
  108.2 4.4 %collective-permute-done.16.refs_1_ = bf16[768,384]{1,0:T(8,128)(2,1)S(1)} collective-permute-done((bf16[768,384]{1,0:T(8,128)(2,1)S(1)}, bf16[768,384]{1,0:T(8,128)(2,1)S(1)}, u32[]{:S(2)}, u32[]{:S(2)}) %collective-permute-start.16) | collective-permute-done | bytes 589856 | tf_op jit(solution)/shard_map/ppermute | solution.py:35
  114.0 1.8 collective-permute-start.19
  115.8 4.9 %shard_map.31.refs_3_ = f32[768,1152]{1,0:T(8,128)S(1)} custom-call(s32[4]{0:T(128)S(1)} %pad_add_fusion.where_ref, bf16[768,384]{1,0:T(8,128)(2,1)S(1)} %shard_map.29.refs_0_, bf16[768,384]{1,0:T(8,128)(2,1)S(1)} %collective-permute-done.16.refs_1_, bf16[768,384]{1,0:T(8,128)(2,1)S(1)} %collective-permute-done.17.refs_2_, ...), custom_call_target="tpu_custom_call" | custom-call | tf_op jit(solution)/shard_map/pallas_call | solution.py:77
  120.7 5.0 %collective-permute-done.21.refs_1_.refs_5_ = bf16[768,384]{1,0:T(8,128)(2,1)S(1)} collective-permute-done((bf16[768,384]{1,0:T(8,128)(2,1)S(1)}, bf16[768,384]{1,0:T(8,128)(2,1)S(1)}, u32[]{:S(2)}, u32[]{:S(2)}) %collective-permute-start.21) | collective-permute-done | bytes 589856 | tf_op jit(solution)/shard_map/ppermute | solution.py:39
  125.8 2.4 %shard_map.32.refs_3_ = f32[768,1152]{1,0:T(8,128)S(1)} custom-call(s32[4]{0:T(128)S(1)} %pad_add_fusion.where_ref, bf16[768,384]{1,0:T(8,128)(2,1)S(1)} %collective-permute-done.20.refs_0_.refs_4_, bf16[768,384]{1,0:T(8,128)(2,1)S(1)} %collective-permute-done.21.refs_1_.refs_5_, bf16[8,384,1152]{2,1,0:T(8,128)(2,1)S(1)} %shard_map.30.refs_4_.refs_2_, ...), custom_call_target="tpu_custom_call" | custom-call | tf_op jit(solution)/shard_map/pallas_call | solution.py:77
  128.2 10.2 %collective-permute-done.19.refs_0_.refs_6_ = bf16[768,384]{1,0:T(8,128)(2,1)S(1)} collective-permute-done((bf16[768,384]{1,0:T(8,128)(2,1)S(1)}, bf16[768,384]{1,0:T(8,128)(2,1)S(1)}, u32[]{:S(2)}, u32[]{:S(2)}) %collective-permute-start.19) | collective-permute-done | bytes 589856 | tf_op jit(solution)/shard_map/ppermute | solution.py:39
  138.4 1.7 shard_map.33
  140.1 4.4 %collective-permute-start.23 = (bf16[384,1152]{1,0:T(8,128)(2,1)S(1)}, bf16[384,1152]{1,0:T(8,128)(2,1)S(1)}, u32[]{:S(2)}, u32[]{:S(2)}) collective-permute-start(bf16[384,1152]{1,0:T(8,128)(2,1)S(1)} %shard_map.33), channel_id=1, source_target_pairs={{0,8},{8,0},{1,9},{9,1},{2,10},{10,2},{3,11},{11,3},{4,12},{12,4},... | collective-permute-start | bytes 2654216 | tf_op jit(solution)/shard_map/ppermute | solution.py:31
  144.6 1.7 shard_map.34.m
  146.8 2.3 %collective-permute-start.26 = (bf16[384,1152]{1,0:T(8,128)(2,1)S(1)}, bf16[384,1152]{1,0:T(8,128)(2,1)S(1)}, u32[]{:S(2)}, u32[]{:S(2)}) collective-permute-start(bf16[384,1152]{1,0:T(8,128)(2,1)S(1)} %get-tuple-element.90.refs_0_), channel_id=1, source_target_pairs={{0,48},{8,24},{16,0},{24,40},{32,16},{40,56},{48,32},{56,8},{1,49}... | collective-permute-start | bytes 2654216 | tf_op jit(solution)/shard_map/ppermute | solution.py:56
  150.4 4.6 %shard_map.36.gram_ref = bf16[8,768,384]{2,1,0:T(8,128)(2,1)S(1)} custom-call(s32[4]{0:T(128)S(1)} %pad_add_fusion.where_ref, bf16[768,384]{1,0:T(8,128)(2,1)S(1)} %shard_map.29.refs_0_, bf16[768,384]{1,0:T(8,128)(2,1)S(1)} %collective-permute-done.16.refs_1_, bf16[768,384]{1,0:T(8,128)(2,1)S(1)} %collective-permute-done.17.refs_2_, ...), custom_call_target="tpu_custom_call" | custom-call | tf_op jit(solution)/shard_map/pallas_call | solution.py:77
  155.0 11.6 %collective-permute-done.26.refs_3_ = bf16[384,1152]{1,0:T(8,128)(2,1)S(1)} collective-permute-done((bf16[384,1152]{1,0:T(8,128)(2,1)S(1)}, bf16[384,1152]{1,0:T(8,128)(2,1)S(1)}, u32[]{:S(2)}, u32[]{:S(2)}) %collective-permute-start.26) | collective-permute-done | bytes 884768 | tf_op jit(solution)/shard_map/ppermute | solution.py:56
  166.6 2.6 %collective-permute-done.25.refs_2_ = bf16[384,1152]{1,0:T(8,128)(2,1)S(1)} collective-permute-done((bf16[384,1152]{1,0:T(8,128)(2,1)S(1)}, bf16[384,1152]{1,0:T(8,128)(2,1)S(1)}, u32[]{:S(2)}, u32[]{:S(2)}) %collective-permute-start.25) | collective-permute-done | bytes 884768 | tf_op jit(solution)/shard_map/ppermute | solution.py:23
  169.9 3.2 %collective-permute-start.27 = (bf16[384,1152]{1,0:T(8,128)(2,1)S(1)}, bf16[384,1152]{1,0:T(8,128)(2,1)S(1)}, u32[]{:S(2)}, u32[]{:S(2)}) collective-permute-start(bf16[384,1152]{1,0:T(8,128)(2,1)S(1)} %collective-permute-done.25.refs_2_), channel_id=1, source_target_pairs={{0,16},{8,56},{16,32},{24,8},{32,48},{40,24},{48,0},{56,40},{1,17}... | collective-permute-start | bytes 2654216 | tf_op jit(solution)/shard_map/ppermute | solution.py:56
  173.2 4.0 %shard_map.37.refs_0_ = f32[768,1152]{1,0:T(8,128)S(1)} custom-call(bf16[8,768,384]{2,1,0:T(8,128)(2,1)S(1)} %shard_map.36.gram_ref, bf16[384,1152]{1,0:T(8,128)(2,1)S(1)} %get-tuple-element.90.refs_0_, bf16[384,1152]{1,0:T(8,128)(2,1)S(1)} %collective-permute-done.24.refs_1_, bf16[384,1152]{1,0:T(8,128)(2,1)S(1)} %collective-permute-done.25.refs_2_, ...), custom_call_target="tpu_custom_call" | custom-call | tf_op jit(solution)/shard_map/pallas_call | solution.py:77
  177.2 13.2 %collective-permute-done.27.refs_2_ = bf16[384,1152]{1,0:T(8,128)(2,1)S(1)} collective-permute-done((bf16[384,1152]{1,0:T(8,128)(2,1)S(1)}, bf16[384,1152]{1,0:T(8,128)(2,1)S(1)}, u32[]{:S(2)}, u32[]{:S(2)}) %collective-permute-start.27) | collective-permute-done | bytes 884768 | tf_op jit(solution)/shard_map/ppermute | solution.py:56
  190.4 4.3 %collective-permute-done.29.refs_3_ = bf16[384,1152]{1,0:T(8,128)(2,1)S(1)} collective-permute-done((bf16[384,1152]{1,0:T(8,128)(2,1)S(1)}, bf16[384,1152]{1,0:T(8,128)(2,1)S(1)}, u32[]{:S(2)}, u32[]{:S(2)}) %collective-permute-start.29) | collective-permute-done | bytes 884768 | tf_op jit(solution)/shard_map/ppermute | solution.py:23
  196.2 3.3 %shard_map.38.refs_0_ = f32[768,1152]{1,0:T(8,128)S(1)} custom-call(bf16[8,768,384]{2,1,0:T(8,128)(2,1)S(1)} %shard_map.36.gram_ref, f32[768,1152]{1,0:T(8,128)S(1)} %shard_map.37.refs_0_, bf16[384,1152]{1,0:T(8,128)(2,1)S(1)} %collective-permute-done.28.refs_1_, bf16[384,1152]{1,0:T(8,128)(2,1)S(1)} %collective-permute-done.27.refs_2_, ...), custom_call_target="tpu_custom_call" | custom-call | tf_op jit(solution)/shard_map/pallas_call | solution.py:77
  199.5 7.4 %collective-permute-done.30.refs_1_ = bf16[384,1152]{1,0:T(8,128)(2,1)S(1)} collective-permute-done((bf16[384,1152]{1,0:T(8,128)(2,1)S(1)}, bf16[384,1152]{1,0:T(8,128)(2,1)S(1)}, u32[]{:S(2)}, u32[]{:S(2)}) %collective-permute-start.30) | collective-permute-done | bytes 884768 | tf_op jit(solution)/shard_map/ppermute | solution.py:56
  207.7 2.7 %collective-permute-start.31 = (bf16[384,1152]{1,0:T(8,128)(2,1)S(1)}, bf16[384,1152]{1,0:T(8,128)(2,1)S(1)}, u32[]{:S(2)}, u32[]{:S(2)}) collective-permute-start(bf16[384,1152]{1,0:T(8,128)(2,1)S(1)} %shard_map.39), channel_id=1, source_target_pairs={{0,8},{8,0},{1,9},{9,1},{2,10},{10,2},{3,11},{11,3},{4,12},{12,4},... | collective-permute-start | bytes 2654216 | tf_op jit(solution)/shard_map/ppermute | solution.py:31
  (47 shorter events, 28.2 us)
Async XLA Ops:
  0.0 3.7 %copy-start = (bf16[384,1152]{1,0:T(8,128)(2,1)S(1)}, bf16[384,1152]{1,0:T(8,128)(2,1)}, u32[]{:S(2)}) copy-start(bf16[384,1152]{1,0:T(8,128)(2,1)} %own_ref.1) | copy-start | bytes 2654212
  2.3 6.0 %collective-permute-start.1 = (bf16[384,1152]{0,1:T(8,128)(2,1)}, bf16[384,1152]{0,1:T(8,128)(2,1)}, u32[]{:S(2)}, u32[]{:S(2)}) collective-permute-start(bf16[384,1152]{0,1:T(8,128)(2,1)} %copy.2), channel_id=1, source_target_pairs={{0,8},{8,0},{1,9},{9,1},{2,10},{10,2},{3,11},{11,3},{4,12},{12,4},... | collective-permute-start | bytes 2654216 | tf_op jit(solution)/shard_map/ppermute | solution.py:31
  3.7 17.6 %collective-permute-start.3 = (bf16[384,1152]{1,0:T(8,128)(2,1)S(1)}, bf16[384,1152]{1,0:T(8,128)(2,1)S(1)}, u32[]{:S(2)}, u32[]{:S(2)}) collective-permute-start(bf16[384,1152]{1,0:T(8,128)(2,1)S(1)} %copy-done), channel_id=1, source_target_pairs={{0,48},{8,24},{16,0},{24,40},{32,16},{40,56},{48,32},{56,8},{1,49}... | collective-permute-start | bytes 2654216 | tf_op jit(solution)/shard_map/ppermute | solution.py:56
  5.1 19.8 %collective-permute-start.2 = (bf16[384,1152]{1,0:T(8,128)(2,1)S(1)}, bf16[384,1152]{1,0:T(8,128)(2,1)S(1)}, u32[]{:S(2)}, u32[]{:S(2)}) collective-permute-start(bf16[384,1152]{1,0:T(8,128)(2,1)S(1)} %copy-done), channel_id=1, source_target_pairs={{0,64},{64,0},{1,65},{65,1},{2,66},{66,2},{3,67},{67,3},{4,68},{68... | collective-permute-start | bytes 2654216 | tf_op jit(solution)/shard_map/ppermute | solution.py:23
  6.7 19.7 %collective-permute-start = (bf16[384,1152]{1,0:T(8,128)(2,1)S(1)}, bf16[384,1152]{1,0:T(8,128)(2,1)S(1)}, u32[]{:S(2)}, u32[]{:S(2)}) collective-permute-start(bf16[384,1152]{1,0:T(8,128)(2,1)S(1)} %copy-done), channel_id=1, source_target_pairs={{0,16},{8,56},{16,32},{24,8},{32,48},{40,24},{48,0},{56,40},{1,17}... | collective-permute-start | bytes 2654216 | tf_op jit(solution)/shard_map/ppermute | solution.py:56
  12.4 14.0 %collective-permute-start.4 = (bf16[2,2,48,768]{3,2,1,0:T(8,128)(2,1)S(1)}, bf16[2,2,48,768]{3,2,1,0:T(8,128)(2,1)S(1)}, u32[]{:S(2)}, u32[]{:S(2)}) collective-permute-start(bf16[2,2,48,768]{3,2,1,0:T(8,128)(2,1)S(1)} %shard_map.17), channel_id=1, source_target_pairs={{0,1},{1,0},{2,3},{3,2},{8,11},{9,10},{10,9},{11,8},{4,5},{5,4},{6... | collective-permute-start | bytes 884744 | tf_op jit(solution)/shard_map/ppermute | solution.py:47
  26.5 19.6 %collective-permute-start.5 = (bf16[384,1152]{1,0:T(8,128)(2,1)S(1)}, bf16[384,1152]{1,0:T(8,128)(2,1)S(1)}, u32[]{:S(2)}, u32[]{:S(2)}) collective-permute-start(bf16[384,1152]{1,0:T(8,128)(2,1)S(1)} %collective-permute-done.2.refs_1_.refs_2_), channel_id=1, source_target_pairs={{0,16},{8,56},{16,32},{24,8},{32,48},{40,24},{48,0},{56,40},{1,17}... | collective-permute-start | bytes 2654216 | tf_op jit(solution)/shard_map/ppermute | solution.py:56
  29.6 20.2 %collective-permute-start.7 = (bf16[384,1152]{1,0:T(8,128)(2,1)S(1)}, bf16[384,1152]{1,0:T(8,128)(2,1)S(1)}, u32[]{:S(2)}, u32[]{:S(2)}) collective-permute-start(bf16[384,1152]{1,0:T(8,128)(2,1)S(1)} %collective-permute-done.3.refs_2_.refs_3_), channel_id=1, source_target_pairs={{0,64},{64,0},{1,65},{65,1},{2,66},{66,2},{3,67},{67,3},{4,68},{68... | collective-permute-start | bytes 2654216 | tf_op jit(solution)/shard_map/ppermute | solution.py:23
  30.8 19.6 %collective-permute-start.6 = (bf16[384,1152]{1,0:T(8,128)(2,1)S(1)}, bf16[384,1152]{1,0:T(8,128)(2,1)S(1)}, u32[]{:S(2)}, u32[]{:S(2)}) collective-permute-start(bf16[384,1152]{1,0:T(8,128)(2,1)S(1)} %collective-permute-done.3.refs_2_.refs_3_), channel_id=1, source_target_pairs={{0,48},{8,24},{16,0},{24,40},{32,16},{40,56},{48,32},{56,8},{1,49}... | collective-permute-start | bytes 2654216 | tf_op jit(solution)/shard_map/ppermute | solution.py:56
  33.3 18.1 %collective-permute-start.8 = (bf16[2,2,144,768]{3,2,1,0:T(8,128)(2,1)S(1)}, bf16[2,2,144,768]{3,2,1,0:T(8,128)(2,1)S(1)}, u32[]{:S(2)}, u32[]{:S(2)}) collective-permute-start(bf16[2,2,144,768]{3,2,1,0:T(8,128)(2,1)S(1)} %shard_map.20), channel_id=1, source_target_pairs={{0,1},{1,0},{2,3},{3,2},{8,11},{9,10},{10,9},{11,8},{4,5},{5,4},{6... | collective-permute-start | bytes 2654216 | tf_op jit(solution)/shard_map/ppermute | solution.py:47
  50.4 12.2 %collective-permute-start.9 = (bf16[384,1152]{1,0:T(8,128)(2,1)S(1)}, bf16[384,1152]{1,0:T(8,128)(2,1)S(1)}, u32[]{:S(2)}, u32[]{:S(2)}) collective-permute-start(bf16[384,1152]{1,0:T(8,128)(2,1)S(1)} %collective-permute-done.5.refs_1_.refs_5_), channel_id=1, source_target_pairs={{0,16},{8,56},{16,32},{24,8},{32,48},{40,24},{48,0},{56,40},{1,17}... | collective-permute-start | bytes 2654216 | tf_op jit(solution)/shard_map/ppermute | solution.py:56
  51.5 10.9 %collective-permute-start.10 = (bf16[2,192,768]{2,1,0:T(8,128)(2,1)S(1)}, bf16[2,192,768]{2,1,0:T(8,128)(2,1)S(1)}, u32[]{:S(2)}, u32[]{:S(2)}) collective-permute-start(bf16[2,192,768]{2,1,0:T(8,128)(2,1)S(1)} %get-tuple-element.66), channel_id=1, source_target_pairs={{0,3},{1,2},{2,1},{3,0},{8,9},{9,8},{10,11},{11,10},{4,7},{5,6},{6... | collective-permute-start | bytes 1769480 | tf_op jit(solution)/shard_map/ppermute | solution.py:47
  55.2 15.2 %collective-permute-start.11 = (bf16[2,2,144,768]{3,2,1,0:T(8,128)(2,1)S(1)}, bf16[2,2,144,768]{3,2,1,0:T(8,128)(2,1)S(1)}, u32[]{:S(2)}, u32[]{:S(2)}) collective-permute-start(bf16[2,2,144,768]{3,2,1,0:T(8,128)(2,1)S(1)} %shard_map.23), channel_id=1, source_target_pairs={{0,1},{1,0},{2,3},{3,2},{8,11},{9,10},{10,9},{11,8},{4,5},{5,4},{6... | collective-permute-start | bytes 2654216 | tf_op jit(solution)/shard_map/ppermute | solution.py:47
  63.9 9.7 %collective-permute-start.12 = (bf16[2,2,48,768]{3,2,1,0:T(8,128)(2,1)S(1)}, bf16[2,2,48,768]{3,2,1,0:T(8,128)(2,1)S(1)}, u32[]{:S(2)}, u32[]{:S(2)}) collective-permute-start(bf16[2,2,48,768]{3,2,1,0:T(8,128)(2,1)S(1)} %shard_map.25), channel_id=1, source_target_pairs={{0,1},{1,0},{2,3},{3,2},{8,11},{9,10},{10,9},{11,8},{4,5},{5,4},{6... | collective-permute-start | bytes 884744 | tf_op jit(solution)/shard_map/ppermute | solution.py:47
  73.8 9.1 %collective-permute-start.13 = (bf16[2,192,768]{2,1,0:T(8,128)(2,1)S(1)}, bf16[2,192,768]{2,1,0:T(8,128)(2,1)S(1)}, u32[]{:S(2)}, u32[]{:S(2)}) collective-permute-start(bf16[2,192,768]{2,1,0:T(8,128)(2,1)S(1)} %get-tuple-element.74), channel_id=1, source_target_pairs={{0,3},{1,2},{2,1},{3,0},{8,9},{9,8},{10,11},{11,10},{4,7},{5,6},{6... | collective-permute-start | bytes 1769480 | tf_op jit(solution)/shard_map/ppermute | solution.py:47
  74.2 8.2 %collective-permute-start.14 = (bf16[192,768]{1,0:T(8,128)(2,1)S(1)}, bf16[192,768]{1,0:T(8,128)(2,1)S(1)}, u32[]{:S(2)}, u32[]{:S(2)}) collective-permute-start(bf16[192,768]{1,0:T(8,128)(2,1)S(1)} %shard_map.27), channel_id=1, source_target_pairs={{0,4},{4,0},{1,5},{5,1},{2,6},{6,2},{3,7},{7,3},{8,12},{12,8},{9,1... | collective-permute-start | bytes 884744 | tf_op jit(solution)/shard_map/ppermute | solution.py:27
  83.0 8.6 %collective-permute-start.15 = (bf16[192,768]{1,0:T(8,128)(2,1)S(1)}, bf16[192,768]{1,0:T(8,128)(2,1)S(1)}, u32[]{:S(2)}, u32[]{:S(2)}) collective-permute-start(bf16[192,768]{1,0:T(8,128)(2,1)S(1)} %shard_map.28), channel_id=1, source_target_pairs={{0,4},{4,0},{1,5},{5,1},{2,6},{6,2},{3,7},{7,3},{8,12},{12,8},{9,1... | collective-permute-start | bytes 884744 | tf_op jit(solution)/shard_map/ppermute | solution.py:27
  91.9 13.1 %collective-permute-start.18 = (bf16[768,384]{1,0:T(8,128)(2,1)S(1)}, bf16[768,384]{1,0:T(8,128)(2,1)S(1)}, u32[]{:S(2)}, u32[]{:S(2)}) collective-permute-start(bf16[768,384]{1,0:T(8,128)(2,1)S(1)} %shard_map.29.refs_0_), channel_id=1, source_target_pairs={{0,4},{4,0},{1,5},{5,1},{2,6},{6,2},{3,7},{7,3},{8,12},{12,8},{9,1... | collective-permute-start | bytes 1769480 | tf_op jit(solution)/shard_map/ppermute | solution.py:27
  94.8 13.4 %collective-permute-start.17 = (bf16[768,384]{1,0:T(8,128)(2,1)S(1)}, bf16[768,384]{1,0:T(8,128)(2,1)S(1)}, u32[]{:S(2)}, u32[]{:S(2)}) collective-permute-start(bf16[768,384]{1,0:T(8,128)(2,1)S(1)} %shard_map.29.refs_0_), channel_id=1, source_target_pairs={{0,3},{1,2},{2,1},{3,0},{4,7},{5,6},{6,5},{7,4},{8,11},{9,10},{10,... | collective-permute-start | bytes 1769480 | tf_op jit(solution)/shard_map/ppermute | solution.py:39
  98.0 14.6 %collective-permute-start.16 = (bf16[768,384]{1,0:T(8,128)(2,1)S(1)}, bf16[768,384]{1,0:T(8,128)(2,1)S(1)}, u32[]{:S(2)}, u32[]{:S(2)}) collective-permute-start(bf16[768,384]{1,0:T(8,128)(2,1)S(1)} %shard_map.29.refs_0_), channel_id=1, source_target_pairs={{0,1},{1,0},{2,3},{3,2},{4,5},{5,4},{6,7},{7,6},{8,9},{9,8},{10,11... | collective-permute-start | bytes 1769480 | tf_op jit(solution)/shard_map/ppermute | solution.py:35
  112.6 13.2 %collective-permute-start.21 = (bf16[768,384]{1,0:T(8,128)(2,1)S(1)}, bf16[768,384]{1,0:T(8,128)(2,1)S(1)}, u32[]{:S(2)}, u32[]{:S(2)}) collective-permute-start(bf16[768,384]{1,0:T(8,128)(2,1)S(1)} %collective-permute-done.18.refs_3_), channel_id=1, source_target_pairs={{0,3},{1,2},{2,1},{3,0},{4,7},{5,6},{6,5},{7,4},{8,11},{9,10},{10,... | collective-permute-start | bytes 1769480 | tf_op jit(solution)/shard_map/ppermute | solution.py:39
  113.5 12.3 %collective-permute-start.20 = (bf16[768,384]{1,0:T(8,128)(2,1)S(1)}, bf16[768,384]{1,0:T(8,128)(2,1)S(1)}, u32[]{:S(2)}, u32[]{:S(2)}) collective-permute-start(bf16[768,384]{1,0:T(8,128)(2,1)S(1)} %collective-permute-done.18.refs_3_), channel_id=1, source_target_pairs={{0,1},{1,0},{2,3},{3,2},{4,5},{5,4},{6,7},{7,6},{8,9},{9,8},{10,11... | collective-permute-start | bytes 1769480 | tf_op jit(solution)/shard_map/ppermute | solution.py:35
  114.0 24.4 %collective-permute-start.19 = (bf16[768,384]{1,0:T(8,128)(2,1)S(1)}, bf16[768,384]{1,0:T(8,128)(2,1)S(1)}, u32[]{:S(2)}, u32[]{:S(2)}) collective-permute-start(bf16[768,384]{1,0:T(8,128)(2,1)S(1)} %collective-permute-done.16.refs_1_), channel_id=1, source_target_pairs={{0,3},{1,2},{2,1},{3,0},{4,7},{5,6},{6,5},{7,4},{8,11},{9,10},{10,... | collective-permute-start | bytes 1769480 | tf_op jit(solution)/shard_map/ppermute | solution.py:39
  125.8 12.6 %collective-permute-start.22 = (bf16[768,384]{1,0:T(8,128)(2,1)S(1)}, bf16[768,384]{1,0:T(8,128)(2,1)S(1)}, u32[]{:S(2)}, u32[]{:S(2)}) collective-permute-start(bf16[768,384]{1,0:T(8,128)(2,1)S(1)} %collective-permute-done.21.refs_1_.refs_5_), channel_id=1, source_target_pairs={{0,1},{1,0},{2,3},{3,2},{4,5},{5,4},{6,7},{7,6},{8,9},{9,8},{10,11... | collective-permute-start | bytes 1769480 | tf_op jit(solution)/shard_map/ppermute | solution.py:35
  140.1 6.5 %collective-permute-start.23 = (bf16[384,1152]{1,0:T(8,128)(2,1)S(1)}, bf16[384,1152]{1,0:T(8,128)(2,1)S(1)}, u32[]{:S(2)}, u32[]{:S(2)}) collective-permute-start(bf16[384,1152]{1,0:T(8,128)(2,1)S(1)} %shard_map.33), channel_id=1, source_target_pairs={{0,8},{8,0},{1,9},{9,1},{2,10},{10,2},{3,11},{11,3},{4,12},{12,4},... | collective-permute-start | bytes 2654216 | tf_op jit(solution)/shard_map/ppermute | solution.py:31
  146.8 19.7 %collective-permute-start.26 = (bf16[384,1152]{1,0:T(8,128)(2,1)S(1)}, bf16[384,1152]{1,0:T(8,128)(2,1)S(1)}, u32[]{:S(2)}, u32[]{:S(2)}) collective-permute-start(bf16[384,1152]{1,0:T(8,128)(2,1)S(1)} %get-tuple-element.90.refs_0_), channel_id=1, source_target_pairs={{0,48},{8,24},{16,0},{24,40},{32,16},{40,56},{48,32},{56,8},{1,49}... | collective-permute-start | bytes 2654216 | tf_op jit(solution)/shard_map/ppermute | solution.py:56
  149.2 20.0 %collective-permute-start.25 = (bf16[384,1152]{1,0:T(8,128)(2,1)S(1)}, bf16[384,1152]{1,0:T(8,128)(2,1)S(1)}, u32[]{:S(2)}, u32[]{:S(2)}) collective-permute-start(bf16[384,1152]{1,0:T(8,128)(2,1)S(1)} %get-tuple-element.90.refs_0_), channel_id=1, source_target_pairs={{0,64},{64,0},{1,65},{65,1},{2,66},{66,2},{3,67},{67,3},{4,68},{68... | collective-permute-start | bytes 2654216 | tf_op jit(solution)/shard_map/ppermute | solution.py:23
  150.0 20.0 %collective-permute-start.24 = (bf16[384,1152]{1,0:T(8,128)(2,1)S(1)}, bf16[384,1152]{1,0:T(8,128)(2,1)S(1)}, u32[]{:S(2)}, u32[]{:S(2)}) collective-permute-start(bf16[384,1152]{1,0:T(8,128)(2,1)S(1)} %get-tuple-element.90.refs_0_), channel_id=1, source_target_pairs={{0,16},{8,56},{16,32},{24,8},{32,48},{40,24},{48,0},{56,40},{1,17}... | collective-permute-start | bytes 2654216 | tf_op jit(solution)/shard_map/ppermute | solution.py:56
  169.9 20.5 %collective-permute-start.27 = (bf16[384,1152]{1,0:T(8,128)(2,1)S(1)}, bf16[384,1152]{1,0:T(8,128)(2,1)S(1)}, u32[]{:S(2)}, u32[]{:S(2)}) collective-permute-start(bf16[384,1152]{1,0:T(8,128)(2,1)S(1)} %collective-permute-done.25.refs_2_), channel_id=1, source_target_pairs={{0,16},{8,56},{16,32},{24,8},{32,48},{40,24},{48,0},{56,40},{1,17}... | collective-permute-start | bytes 2654216 | tf_op jit(solution)/shard_map/ppermute | solution.py:56
  173.2 21.5 %collective-permute-start.29 = (bf16[384,1152]{1,0:T(8,128)(2,1)S(1)}, bf16[384,1152]{1,0:T(8,128)(2,1)S(1)}, u32[]{:S(2)}, u32[]{:S(2)}) collective-permute-start(bf16[384,1152]{1,0:T(8,128)(2,1)S(1)} %collective-permute-done.26.refs_3_), channel_id=1, source_target_pairs={{0,64},{64,0},{1,65},{65,1},{2,66},{66,2},{3,67},{67,3},{4,68},{68... | collective-permute-start | bytes 2654216 | tf_op jit(solution)/shard_map/ppermute | solution.py:23
  173.2 21.5 %collective-permute-start.28 = (bf16[384,1152]{1,0:T(8,128)(2,1)S(1)}, bf16[384,1152]{1,0:T(8,128)(2,1)S(1)}, u32[]{:S(2)}, u32[]{:S(2)}) collective-permute-start(bf16[384,1152]{1,0:T(8,128)(2,1)S(1)} %collective-permute-done.26.refs_3_), channel_id=1, source_target_pairs={{0,48},{8,24},{16,0},{24,40},{32,16},{40,56},{48,32},{56,8},{1,49}... | collective-permute-start | bytes 2654216 | tf_op jit(solution)/shard_map/ppermute | solution.py:56
  194.7 12.2 %collective-permute-start.30 = (bf16[384,1152]{1,0:T(8,128)(2,1)S(1)}, bf16[384,1152]{1,0:T(8,128)(2,1)S(1)}, u32[]{:S(2)}, u32[]{:S(2)}) collective-permute-start(bf16[384,1152]{1,0:T(8,128)(2,1)S(1)} %collective-permute-done.27.refs_2_), channel_id=1, source_target_pairs={{0,16},{8,56},{16,32},{24,8},{32,48},{40,24},{48,0},{56,40},{1,17}... | collective-permute-start | bytes 2654216 | tf_op jit(solution)/shard_map/ppermute | solution.py:56
  207.7 4.7 %collective-permute-start.31 = (bf16[384,1152]{1,0:T(8,128)(2,1)S(1)}, bf16[384,1152]{1,0:T(8,128)(2,1)S(1)}, u32[]{:S(2)}, u32[]{:S(2)}) collective-permute-start(bf16[384,1152]{1,0:T(8,128)(2,1)S(1)} %shard_map.39), channel_id=1, source_target_pairs={{0,8},{8,0},{1,9},{9,1},{2,10},{10,2},{3,11},{11,3},{4,12},{12,4},... | collective-permute-start | bytes 2654216 | tf_op jit(solution)/shard_map/ppermute | solution.py:31
